TPU v7x, 32 devices: a whole 2x2x4 slice. The times are simulated.
32 devices in a mesh: dp: 8 (over y, x, core), tensor: 4 (over z).
Axes of the slice: x: 2, y: 2, z: 4, core: 2. Of those that a mesh axis runs over, the one named last changes fastest.
Arguments:
- latents: bfloat16 [16, 256, 768], P('dp'), may hold values from -6 to 6
- condition: bfloat16 [16, 768], P('dp', 'tensor'), may hold values from -6 to 6
- modulator: bfloat16 [768, 4608], P('tensor'), may hold values from -0.21875 to 0.21875
- modulator_bias: bfloat16 [4608], replicated, may hold values from -1.5 to 1.5
- attn_input: bfloat16 [3, 768, 768], P(None, None, 'tensor'), may hold values from -0.21875 to 0.21875
- attn_input_bias: bfloat16 [2, 768], P(None, 'tensor'), may hold values from -2.5 to 2.5
- attn_output: bfloat16 [768, 768], P('tensor'), may hold values from -1.75 to 1.75
- attn_output_bias: bfloat16 [768], replicated, may hold values from -2.5 to 2.5
- ffn_input: bfloat16 [768, 3072], P(None, 'tensor'), may hold values from -0.21875 to 0.21875
- ffn_input_bias: bfloat16 [3072], P('tensor'), may hold values from -2.5 to 2.5
- ffn_output: bfloat16 [3072, 768], P('tensor'), may hold values from -0.109375 to 0.109375
- ffn_output_bias: bfloat16 [768], replicated, may hold values from -2.5 to 2.5
- cotangent: bfloat16 [16, 256, 768], P('dp'), may hold values from -6 to 6
Outputs:
- layer_out: bfloat16 [16, 256, 768], P('dp')
- latents_grad: float32 [16, 256, 768], P('dp')
- condition_grad: float32 [16, 768], P('dp', 'tensor')
- modulator_grad: float32 [768, 4608], P('tensor')
- modulator_bias_grad: float32 [4608], replicated
- attn_input_grad: float32 [3, 768, 768], P(None, None, 'tensor')
- attn_input_bias_grad: float32 [2, 768], P(None, 'tensor')
- attn_output_grad: float32 [768, 768], P('tensor')
- attn_output_bias_grad: float32 [768], replicated
- ffn_input_grad: float32 [768, 3072], P(None, 'tensor')
- ffn_input_bias_grad: float32 [3072], P('tensor')
- ffn_output_grad: float32 [3072, 768], P('tensor')
- ffn_output_bias_grad: float32 [768], replicated
All inputs are finite; a program needn't handle non-finite values.
Results may differ from a plain program's by a relative error of at most 0.014.
The roundings to bfloat16 on the way count: a program that leaves them out, or rounds other values in their place, can miss the bound.
Values sent between devices are 32-bit elements; how exact they have to be, the bound alone decides.
No kernel may reach another device: no remote copies, remote signals or barrier semaphores. Data moves between devices by JAX's collectives and lax.ppermute only.
A program may use at most 128 MiB of HBM per device.

v0:
```python
import jax
import jax.numpy as jnp
from jax import lax
from jax.sharding import PartitionSpec as P

HEAD = 64


epsilon = 1e-06


def norm_parts(values):
    centre = values - jnp.mean(values, axis=-1, keepdims=True)
    inverse = lax.rsqrt(jnp.mean(centre * centre, axis=-1, keepdims=True) + epsilon)
    return (centre * inverse, inverse)


def norm_back(grad, normed, inverse):
    return (
        grad
        - jnp.mean(grad, axis=-1, keepdims=True)
        - normed * jnp.mean(grad * normed, axis=-1, keepdims=True)
    ) * inverse


def per_device(
    latents,
    condition,
    modulator,
    modulator_bias,
    attn_input,
    attn_input_bias,
    attn_output,
    attn_output_bias,
    ffn_input,
    ffn_input_bias,
    ffn_output,
    ffn_output_bias,
    cotangent,
):
    image_count, positions, features = latents.shape
    head_count = attn_input.shape[2] // HEAD
    score_scale = HEAD ** (-0.5)
    cond_float = condition.astype(jnp.float32)
    context_low = jax.nn.silu(cond_float).astype(jnp.bfloat16)
    modulation = lax.psum(
        jnp.dot(context_low, modulator, preferred_element_type=jnp.float32), "tensor"
    )
    modulation = modulation + modulator_bias.astype(jnp.float32)
    pieces = modulation.reshape(image_count, 6, features)[:, None]
    shift_one, scale_one, gate_one = (pieces[:, :, 0], pieces[:, :, 1], pieces[:, :, 2])
    shift_two, scale_two, gate_two = (pieces[:, :, 3], pieces[:, :, 4], pieces[:, :, 5])
    inputs = latents.astype(jnp.float32)
    normed_one, inverse_one = norm_parts(inputs)
    entry_one = (
        (normed_one * (1.0 + scale_one) + shift_one).astype(jnp.bfloat16).reshape(-1, features)
    )
    in_bias = attn_input_bias.astype(jnp.float32)
    offsets = jnp.stack([in_bias[0], jnp.zeros_like(in_bias[0]), in_bias[1]])[:, None, :]
    projected = (
        jnp.einsum("td,jde->jte", entry_one, attn_input, preferred_element_type=jnp.float32)
        + offsets
    ).astype(jnp.bfloat16)
    shaped = projected.reshape(3, image_count, positions, head_count, HEAD)
    query, keys, values = (shaped[0], shaped[1], shaped[2])
    scores = (
        jnp.einsum("gqhe,gkhe->ghqk", query, keys, preferred_element_type=jnp.float32) * score_scale
    )
    highest = jnp.max(scores, axis=-1, keepdims=True)
    log_total = highest + jnp.log(jnp.sum(jnp.exp(scores - highest), axis=-1, keepdims=True))
    probs = jnp.exp(scores - log_total)
    mixed = jnp.einsum(
        "ghqk,gkhe->gqhe", probs.astype(jnp.bfloat16), values, preferred_element_type=jnp.float32
    ).astype(jnp.bfloat16)
    mixed_flat = mixed.reshape(-1, head_count * HEAD)
    attention = lax.psum(
        jnp.dot(mixed_flat, attn_output, preferred_element_type=jnp.float32), "tensor"
    )
    attention = (attention + attn_output_bias.astype(jnp.float32)).reshape(
        image_count, positions, features
    )
    middle = inputs + gate_one * attention
    normed_two, inverse_two = norm_parts(middle)
    entry_two = (
        (normed_two * (1.0 + scale_two) + shift_two).astype(jnp.bfloat16).reshape(-1, features)
    )
    hidden = jnp.dot(
        entry_two, ffn_input, preferred_element_type=jnp.float32
    ) + ffn_input_bias.astype(jnp.float32)
    active = jax.nn.gelu(hidden, approximate=True).astype(jnp.bfloat16)
    branch = lax.psum(jnp.dot(active, ffn_output, preferred_element_type=jnp.float32), "tensor")
    branch = (branch + ffn_output_bias.astype(jnp.float32)).reshape(
        image_count, positions, features
    )
    layer_out = (middle + gate_two * branch).astype(jnp.bfloat16)
    upstream = cotangent.astype(jnp.float32)
    gate_two_grad = jnp.sum(upstream * branch, axis=1)
    branch_grad = (gate_two * upstream).astype(jnp.bfloat16).reshape(-1, features)
    grad_ffn_output = jnp.einsum(
        "tf,td->fd", active, branch_grad, preferred_element_type=jnp.float32
    )
    grad_ffn_output_bias = jnp.sum(branch_grad.astype(jnp.float32), axis=0)
    active_grad = jnp.einsum(
        "td,fd->tf", branch_grad, ffn_output, preferred_element_type=jnp.float32
    )
    gelu_pull = jax.vjp(lambda inner: jax.nn.gelu(inner, approximate=True), hidden)[1]
    hidden_grad = gelu_pull(active_grad)[0].astype(jnp.bfloat16)
    grad_ffn_input = jnp.einsum(
        "td,tf->df", entry_two, hidden_grad, preferred_element_type=jnp.float32
    )
    grad_ffn_input_bias = jnp.sum(hidden_grad.astype(jnp.float32), axis=0)
    entry_two_grad = lax.psum(
        jnp.einsum("tf,df->td", hidden_grad, ffn_input, preferred_element_type=jnp.float32),
        "tensor",
    ).reshape(image_count, positions, features)
    scale_two_grad = jnp.sum(entry_two_grad * normed_two, axis=1)
    shift_two_grad = jnp.sum(entry_two_grad, axis=1)
    middle_grad = upstream + norm_back(entry_two_grad * (1.0 + scale_two), normed_two, inverse_two)
    gate_one_grad = jnp.sum(middle_grad * attention, axis=1)
    attention_grad = (gate_one * middle_grad).astype(jnp.bfloat16).reshape(-1, features)
    grad_attn_output = jnp.einsum(
        "tc,td->cd", mixed_flat, attention_grad, preferred_element_type=jnp.float32
    )
    grad_attn_output_bias = jnp.sum(attention_grad.astype(jnp.float32), axis=0)
    mixed_grad = jnp.einsum(
        "td,cd->tc", attention_grad, attn_output, preferred_element_type=jnp.float32
    ).astype(jnp.bfloat16)
    mixed_grad = mixed_grad.reshape(image_count, positions, head_count, HEAD)
    scores_again = (
        jnp.einsum("gqhe,gkhe->ghqk", query, keys, preferred_element_type=jnp.float32) * score_scale
    )
    probs_again = jnp.exp(scores_again - log_total)
    value_grad = jnp.einsum(
        "ghqk,gqhe->gkhe",
        probs_again.astype(jnp.bfloat16),
        mixed_grad,
        preferred_element_type=jnp.float32,
    )
    probs_grad = jnp.einsum(
        "gqhe,gkhe->ghqk", mixed_grad, values, preferred_element_type=jnp.float32
    )
    scores_grad = probs_again * (
        probs_grad - jnp.sum(probs_again * probs_grad, axis=-1, keepdims=True)
    )
    scores_low = scores_grad.astype(jnp.bfloat16)
    query_grad = (
        jnp.einsum("ghqk,gkhe->gqhe", scores_low, keys, preferred_element_type=jnp.float32)
        * score_scale
    )
    key_grad = (
        jnp.einsum("ghqk,gqhe->gkhe", scores_low, query, preferred_element_type=jnp.float32)
        * score_scale
    )
    projected_grad = (
        jnp.stack([query_grad, key_grad, value_grad])
        .astype(jnp.bfloat16)
        .reshape(3, -1, head_count * HEAD)
    )
    grad_attn_input = jnp.einsum(
        "td,jte->jde", entry_one, projected_grad, preferred_element_type=jnp.float32
    )
    projected_sums = jnp.sum(projected_grad.astype(jnp.float32), axis=1)
    grad_attn_input_bias = jnp.stack([projected_sums[0], projected_sums[2]])
    entry_one_grad = lax.psum(
        jnp.einsum("jte,jde->td", projected_grad, attn_input, preferred_element_type=jnp.float32),
        "tensor",
    ).reshape(image_count, positions, features)
    scale_one_grad = jnp.sum(entry_one_grad * normed_one, axis=1)
    shift_one_grad = jnp.sum(entry_one_grad, axis=1)
    latents_grad = middle_grad + norm_back(
        entry_one_grad * (1.0 + scale_one), normed_one, inverse_one
    )
    modulation_grad = jnp.concatenate(
        [
            shift_one_grad,
            scale_one_grad,
            gate_one_grad,
            shift_two_grad,
            scale_two_grad,
            gate_two_grad,
        ],
        axis=-1,
    ).astype(jnp.bfloat16)
    grad_modulator = jnp.einsum(
        "gc,gm->cm", context_low, modulation_grad, preferred_element_type=jnp.float32
    )
    grad_modulator_bias = jnp.sum(modulation_grad.astype(jnp.float32), axis=0)
    context_grad = jnp.einsum(
        "gm,cm->gc", modulation_grad, modulator, preferred_element_type=jnp.float32
    )
    silu_pull = jax.vjp(jax.nn.silu, cond_float)[1]
    condition_grad = silu_pull(context_grad)[0]
    (
        summed_modulator,
        summed_modulator_bias,
        summed_attn_input,
        summed_attn_input_bias,
        summed_attn_output,
        summed_attn_output_bias,
        summed_ffn_input,
        summed_ffn_input_bias,
        summed_ffn_output,
        summed_ffn_output_bias,
    ) = lax.psum(
        (
            grad_modulator,
            grad_modulator_bias,
            grad_attn_input,
            grad_attn_input_bias,
            grad_attn_output,
            grad_attn_output_bias,
            grad_ffn_input,
            grad_ffn_input_bias,
            grad_ffn_output,
            grad_ffn_output_bias,
        ),
        "dp",
    )
    return (
        layer_out,
        latents_grad,
        condition_grad,
        summed_modulator,
        summed_modulator_bias,
        summed_attn_input,
        summed_attn_input_bias,
        summed_attn_output,
        summed_attn_output_bias,
        summed_ffn_input,
        summed_ffn_input_bias,
        summed_ffn_output,
        summed_ffn_output_bias,
    )


def solution(mesh):
    placed = (
        P("dp", None, None),
        P("dp", "tensor"),
        P("tensor", None),
        P(),
        P(None, None, "tensor"),
        P(None, "tensor"),
        P("tensor", None),
        P(),
        P(None, "tensor"),
        P("tensor"),
        P("tensor", None),
        P(),
        P("dp", None, None),
    )
    return jax.shard_map(
        per_device,
        mesh=mesh,
        in_specs=placed,
        out_specs=(
            P("dp", None, None),
            P("dp", None, None),
            P("dp", "tensor"),
            P("tensor", None),
            P(),
            P(None, None, "tensor"),
            P(None, "tensor"),
            P("tensor", None),
            P(),
            P(None, "tensor"),
            P("tensor"),
            P("tensor", None),
            P(),
        ),
        check_vma=False,
    )
```

profile of v0, /device:TPU:0, one launch (start us, length us, event | category | flops | bytes accessed | tf_op | source)
XLA Modules:
  0.0 522.6 jit_solution(3879437100773897354)
XLA Ops:
  8.7 1.6 fusion.13
  11.9 21.2 %psum.105 = f32[2,4608]{1,0:T(2,128)S(1)} all-reduce(f32[2,4608]{1,0:T(2,128)S(1)} %fusion.53), channel_id=1, replica_groups=mesh['dp'=8,'tensor'=4] {'tensor'}, use_global_device_ids=true, to_apply=%region_0.1 | all-reduce | flops 9216 | bytes 73728 | tf_op jit(solution)/shard_map/psum | solution.py:46
  38.1 1.6 fusion.68
  43.0 2.0 fusion.69
  45.0 62.2 %all-reduce.8.cloned.1.call-done = f32[512,768]{1,0:T(8,128)} async-done(((f32[512,768]{1,0:T(8,128)}), f32[512,768]{1,0:T(8,128)}) %all-reduce.8.cloned.1.call-update) | async-done | bytes 1572880 | tf_op jit(solution)/shard_map/psum | solution.py:76
  107.2 1.6 broadcast_add_fusion.1
  111.0 3.4 convert_reduce_fusion.2
  115.3 2.0 fusion.70
  117.5 4.0 fusion.58
  121.4 64.1 %all-reduce.10.cloned.1.call-done = f32[512,768]{1,0:T(8,128)} async-done(((f32[512,768]{1,0:T(8,128)}), f32[512,768]{1,0:T(8,128)}) %all-reduce.10.cloned.1.call-update) | async-done | bytes 1572880 | tf_op jit(solution)/shard_map/psum | solution.py:112
  185.6 1.6 fusion.24
  189.1 3.2 fusion.25
  192.3 2.5 convert_reduce_fusion.3
  196.8 1.6 reshape.172
  198.5 2.0 fusion.30
  204.7 1.7 stack.21
  206.5 1.8 copy.63
  208.3 1.7 stack.19
  210.0 1.8 copy.66
  211.8 1.7 stack.20
  217.2 3.1 convolution_bitcast_fusion.1
  221.0 3.7 fusion.72
  224.7 2.4 fusion.57
  228.6 1.8 convolution_bitcast_fusion
  230.4 110.6 %all-reduce.14.cloned.1.call-done = (f32[512,768]{1,0:T(8,128)}, f32[512,768]{1,0:T(8,128)}) async-done(((f32[512,768]{1,0:T(8,128)}, f32[512,768]{1,0:T(8,128)}), (f32[512,768]{1,0:T(8,128)}, f32[512,768]{1,0:T(8,128)})) %all-reduce.14.cloned.1.call-update) | async-done | bytes 3145744 | tf_op jit(solution)/shard_map/psum | solution.py:91
  341.0 1.6 fusion.23
  342.7 2.9 fusion.12
  348.4 1.9 multiply_reduce_fusion
  350.4 2.5 fusion.51
  354.3 27.1 %all-reduce = (f32[4608]{0:T(1024)}, f32[2,192]{1,0:T(2,128)}, f32[768]{0:T(1024)}, f32[768]{0:T(1024)}, f32[768]{0:T(1024)}) all-reduce(f32[4608]{0:T(1024)S(1)} %convert_reduce_fusion.5, f32[2,192]{1,0:T(2,128)S(1)} %pad_maximum_fusion.1, f32[768]{0:T(1024)S(1)} %copy-done.60, ...), channel_id=1, replica_groups=mesh['dp'=8,'tensor'=4] {'dp'}, use_global_device_ids=true, to_apply=%region_24.25 | all-reduce | flops 7296 | bytes 58368 | tf_op jit(solution)/shard_map/psum | solution.py:204
  384.2 121.2 %all-reduce.12.cloned.1.call-done = (f32[192,4608]{1,0:T(8,128)}, f32[3,768,192]{1,2,0:T(8,128)}, f32[192,768]{1,0:T(8,128)}, f32[768,768]{1,0:T(8,128)}, f32[768,768]{1,0:T(8,128)}) async-done(((f32[192,4608]{1,0:T(8,128)}, f32[3,768,192]{1,2,0:T(8,128)}, f32[192,768]{1,0:T(8,128)}, f32[768,768]{1,0:T(8,128)}, f32[768,768]{1,0:T(8,128)}), (f32[192,4608]{1,0:T(8,128)}, f32[3,768,192]{1,2,0:T(8,128)}, ...) | async-done | bytes 10616848 | tf_op jit(solution)/shard_map/psum | solution.py:204
  505.4 4.2 copy.127
  (235 shorter events, 41.8 us)
Async XLA Ops:
  7.2 4.3 copy-start
  7.2 3.7 copy-start.69
  7.2 4.3 copy-start.63
  7.2 4.3 copy-start.64
  7.2 100.0 %all-reduce.8.cloned.1.call-start = ((), (), s32[]{:S(2)}) async-start(), calls=%async_computation | async-start | bytes 3145728 | tf_op jit(solution)/shard_map/psum | solution.py:76
  8.7 25.1 %copy-start.3 = (bf16[2,256,768]{2,1,0:T(8,128)(2,1)S(1)}, bf16[2,256,768]{2,1,0:T(8,128)(2,1)}, u32[]{:S(2)}) copy-start(bf16[2,256,768]{2,1,0:T(8,128)(2,1)} %param.13) | copy-start | bytes 2359300
  11.5 23.4 %copy-start.34 = (bf16[3,768,192]{1,2,0:T(8,128)(2,1)S(1)}, bf16[3,768,192]{1,2,0:T(8,128)(2,1)}, u32[]{:S(2)}) copy-start(bf16[3,768,192]{1,2,0:T(8,128)(2,1)} %param.17) | copy-start | bytes 2654212
  38.1 3.5 copy-start.55
  38.1 3.5 copy-start.56
  38.1 4.1 copy-start.8
  39.7 145.9 %all-reduce.10.cloned.1.call-start = ((), (), s32[]{:S(2)}) async-start(), calls=%async_computation.1 | async-start | bytes 3145728 | tf_op jit(solution)/shard_map/psum | solution.py:112
  39.8 3.2 copy-start.76
  43.0 64.2 %copy-start.49 = (f32[768]{0:T(1024)S(1)}, f32[768]{0:T(1024)}, u32[]{:S(2)}) copy-start(f32[768]{0:T(1024)} %convert_element_type.101) | copy-start | bytes 9220
  110.2 4.2 copy-start.18
  117.3 223.7 %all-reduce.14.cloned.1.call-start = ((), (), s32[]{:S(2)}) async-start(), calls=%async_computation.3 | async-start | bytes 6291456 | tf_op jit(solution)/shard_map/psum | solution.py:91
  189.0 3.3 copy-start.7
  189.0 3.3 copy-start.9
  189.0 3.3 copy-start.40
  189.0 3.3 copy-start.44
  189.0 3.3 copy-start.48
  189.0 3.3 copy-start.53
  189.0 3.3 copy-start.66
  192.3 3.4 copy-start.33
  220.3 285.0 %all-reduce.12.cloned.1.call-start = ((), (), s32[]{:S(2)}) async-start(), calls=%async_computation.2 | async-start | bytes 21233664 | tf_op jit(solution)/shard_map/psum | solution.py:204
  221.0 3.7 copy-start.36
  221.0 3.7 copy-start.78
  230.4 112.2 %copy-start.46 = (f32[2,256]{1,0:T(2,128)S(1)}, f32[2,256]{1,0:T(2,128)}, u32[]{:S(2)}) copy-start(f32[2,256]{1,0:T(2,128)} %copy-done.45) | copy-start | bytes 6148
  230.4 112.2 %copy-start.51 = (f32[2,256]{1,0:T(2,128)S(1)}, f32[2,256]{1,0:T(2,128)}, u32[]{:S(2)}) copy-start(f32[2,256]{1,0:T(2,128)} %add_rsqrt_fusion.1) | copy-start | bytes 6148
  342.6 3.0 copy-start.10
  342.6 4.4 copy-start.16
  352.9 29.7 %copy-start.42 = (f32[2,768]{1,0:T(2,128)S(1)}, f32[2,768]{1,0:T(2,128)}, u32[]{:S(2)}) copy-start(f32[2,768]{1,0:T(2,128)} %copy-done.41) | copy-start | bytes 18436
  505.4 4.2 copy-start.23
  (51 other events, 81.1 us)
Sparse Core Ops, SparseCore 0:
  39.8 67.3 all-reduce.7
  117.4 68.1 all-reduce.9
  220.5 120.4 all-reduce.13
  353.0 152.3 all-reduce.11
where the time goes:
time: 524 us; the launch traced here: 523 us
  waiting for transfers between devices  358 us (68%)
  blocking collectives  48.3 us (9%)
  local copies, waits for them, and re-layouts  36.5 us (7%)
  matrix products  35.9 us (7%)
  other arithmetic  28.8 us (5%)
  between operations  14.6 us (3%)
    psum x1, waiting for transfers between devices, per_device(): lax.psum((grad_modulator, grad_modulator_bias, grad_attn_input, grad_attn...  121 us
    psum x1, waiting for transfers between devices, per_device(): lax.psum(jnp.dot(active, ffn_output, preferred_element_type=jnp.float32),...  111 us
    psum x1, waiting for transfers between devices, per_device(): lax.psum(jnp.einsum('tf,df->td', hidden_grad, ffn_input, preferred_elemen...  64.1 us
    psum x1, waiting for transfers between devices, per_device(): lax.psum(jnp.dot(mixed_flat, attn_output, preferred_element_type=jnp.floa...  62.2 us
    psum x1, blocking collectives, per_device(): lax.psum((grad_modulator, grad_modulator_bias, grad_attn_input, grad_attn...  27.1 us
    unnamed x174, local copies, waits for them, and re-layouts  21.9 us
    psum x1, blocking collectives, per_device(): lax.psum(jnp.dot(context_low, modulator, preferred_element_type=jnp.float...  21.2 us
  transfers between devices with their start and end apart: 4, of which 4 were waited for; matrix products, arithmetic and copies ran while one was open for 4% of the time, Pallas kernels for 0%

commit v1 on v0

v1 whole, which is shorter than its diff:
```python
import functools

import jax
import jax.numpy as jnp
from jax import lax
from jax.experimental import pallas as pl
from jax.experimental.pallas import tpu as pltpu
from jax.sharding import PartitionSpec as P

HEAD = 64
epsilon = 1e-06
SCALE = HEAD ** (-0.5)
LOW = jnp.bfloat16
FULL = jnp.float32
NN = (((1,), (0,)), ((), ()))
NT = (((1,), (1,)), ((), ()))
TN = (((0,), (0,)), ((), ()))


def mm(left, right, dims=NN):
    return lax.dot_general(left, right, dims, preferred_element_type=FULL)


def norm_parts(values):
    centre = values - jnp.mean(values, axis=-1, keepdims=True)
    inverse = lax.rsqrt(jnp.mean(centre * centre, axis=-1, keepdims=True) + epsilon)
    return (centre * inverse, inverse)


def norm_back(grad, normed, inverse):
    return (
        grad
        - jnp.mean(grad, axis=-1, keepdims=True)
        - normed * jnp.mean(grad * normed, axis=-1, keepdims=True)
    ) * inverse


def softmax_t(keys_t, query_t):
    scores = mm(keys_t, query_t, TN) * SCALE
    shifted = jnp.exp(scores - jnp.max(scores, axis=0, keepdims=True))
    return shifted * (1.0 / jnp.sum(shifted, axis=0, keepdims=True))


def forward_kernel(images, entry_ref, weight_ref, bias_ref, out_ref):
    columns = weight_ref.shape[1]
    positions = entry_ref.shape[0] // images
    entry = entry_ref[...]
    query, keys, values = (
        (mm(weight_ref[j], entry, NT) + bias_ref[j]).astype(LOW) for j in range(3)
    )
    for g in range(images):
        token = slice(g * positions, (g + 1) * positions)
        for h in range(columns // HEAD):
            row = slice(h * HEAD, (h + 1) * HEAD)
            probs = softmax_t(keys[row, token], query[row, token])
            mixed = mm(values[row, token], probs.astype(LOW))
            out_ref[row, token] = mixed.astype(LOW).astype(FULL)


def attention_forward(entry, weight_t, bias, images):
    tokens = entry.shape[0]
    columns = weight_t.shape[1]
    return pl.pallas_call(
        functools.partial(forward_kernel, images),
        out_shape=jax.ShapeDtypeStruct((columns, tokens), FULL),
        compiler_params=pltpu.CompilerParams(vmem_limit_bytes=48 * 2**20),
        name="attention_forward",
    )(entry, weight_t, bias)


def backward_kernel(heads, proj_ref, grad_ref, out_ref):
    for h in range(heads):
        row = slice(h * HEAD, (h + 1) * HEAD)
        query, keys, values = proj_ref[0, row, :], proj_ref[1, row, :], proj_ref[2, row, :]
        grad = grad_ref[row, :]
        probs = softmax_t(keys, query)
        probs_grad = mm(values, grad, TN)
        weighted = probs * probs_grad
        scores_grad = (weighted - probs * jnp.sum(weighted, axis=0, keepdims=True)).astype(LOW)
        out_ref[0, row, :] = (mm(keys, scores_grad) * SCALE).astype(LOW)
        out_ref[1, row, :] = (mm(query, scores_grad, NT) * SCALE).astype(LOW)
        out_ref[2, row, :] = mm(grad, probs.astype(LOW), NT).astype(LOW)


def attention_backward(proj_t, grad_t, images):
    width, tokens = grad_t.shape
    positions = tokens // images
    heads = width // HEAD
    step = 4 if heads % 4 == 0 else heads
    rows = step * HEAD
    return pl.pallas_call(
        functools.partial(backward_kernel, step),
        out_shape=jax.ShapeDtypeStruct((3, width, tokens), LOW),
        grid=(images, heads // step),
        in_specs=[
            pl.BlockSpec((3, rows, positions), lambda g, h: (0, h, g)),
            pl.BlockSpec((rows, positions), lambda g, h: (h, g)),
        ],
        out_specs=pl.BlockSpec((3, rows, positions), lambda g, h: (0, h, g)),
        compiler_params=pltpu.CompilerParams(vmem_limit_bytes=48 * 2**20),
        name="attention_backward",
    )(proj_t, grad_t)


def join_kernel(mixed_ref, weight_ref, bias_ref, inputs_ref, mod_ref, attention_ref, middle_ref, entry_ref, low_ref):
    weight = weight_ref[...].astype(LOW)
    low_ref[...] = weight
    attention = mm(mixed_ref[...].astype(LOW), weight, TN) + bias_ref[...].astype(FULL)
    attention_ref[...] = attention
    middle = inputs_ref[...].astype(FULL) + mod_ref[0, 2:3, :] * attention
    middle_ref[...] = middle
    normed = norm_parts(middle)[0]
    entry_ref[...] = (normed * (1.0 + mod_ref[0, 4:5, :]) + mod_ref[0, 3:4, :]).astype(LOW)


def join_heads(mixed, weight, bias, inputs, modulation):
    images = modulation.shape[0]
    tokens, width = inputs.shape
    positions = tokens // images
    by_image = pl.BlockSpec((positions, width), lambda g: (g, 0))
    whole = pl.BlockSpec(weight.shape, lambda g: (0, 0))
    return pl.pallas_call(
        join_kernel,
        out_shape=(
            jax.ShapeDtypeStruct((tokens, width), FULL),
            jax.ShapeDtypeStruct((tokens, width), FULL),
            jax.ShapeDtypeStruct((tokens, width), LOW),
            jax.ShapeDtypeStruct(weight.shape, LOW),
        ),
        grid=(images,),
        in_specs=[
            pl.BlockSpec((weight.shape[0], positions), lambda g: (0, g)),
            whole,
            pl.BlockSpec((1, width), lambda g: (0, 0)),
            by_image,
            pl.BlockSpec((1, 6, width), lambda g: (g, 0, 0)),
        ],
        out_specs=(by_image, by_image, by_image, whole),
        compiler_params=pltpu.CompilerParams(vmem_limit_bytes=48 * 2**20),
        name="join_heads",
    )(mixed, weight, bias, inputs, modulation)


def project_kernel(weight_ref, bias_ref, entry_ref, out_ref, low_ref):
    weight = weight_ref[0, 0].astype(LOW)
    low_ref[0] = weight
    out_ref[0] = (mm(weight, entry_ref[...], NT) + bias_ref[0]).astype(LOW)


def project_all(weight, bias, entry):
    groups, _, columns, width = weight.shape
    tokens = entry.shape[0]
    return pl.pallas_call(
        project_kernel,
        out_shape=(
            jax.ShapeDtypeStruct((3, groups * columns, tokens), LOW),
            jax.ShapeDtypeStruct((3, groups * columns, width), LOW),
        ),
        grid=(3, groups),
        in_specs=[
            pl.BlockSpec((1, 1, columns, width), lambda j, t: (t, j, 0, 0)),
            pl.BlockSpec((1, columns, 1), lambda j, t: (j, t, 0)),
            pl.BlockSpec((tokens, width), lambda j, t: (0, 0)),
        ],
        out_specs=(
            pl.BlockSpec((1, columns, tokens), lambda j, t: (j, t, 0)),
            pl.BlockSpec((1, columns, width), lambda j, t: (j, t, 0)),
        ),
        compiler_params=pltpu.CompilerParams(vmem_limit_bytes=48 * 2**20),
        name="project_all",
    )(weight, bias, entry)


def flip(value, axis, count, mask):
    return lax.ppermute(value, axis, [(i, i ^ mask) for i in range(count)])


def flip_sum(value, axis, count):
    parts = [value] + [flip(value, axis, count, mask) for mask in range(1, count)]
    while len(parts) > 1:
        parts = [a + b for a, b in zip(parts[::2], parts[1::2])]
    return parts[0]


def halving_sum(value, axis, count, masks):
    place = lax.axis_index(axis)
    for mask in masks:
        half = value.shape[0] // 2
        side = (place // mask) % 2
        away = lax.dynamic_slice_in_dim(value, (1 - side) * half, half, 0)
        kept = lax.dynamic_slice_in_dim(value, side * half, half, 0)
        value = kept + flip(away, axis, count, mask)
    for mask in reversed(masks):
        other = flip(value, axis, count, mask)
        lower = (place // mask) % 2 == 0
        value = jnp.concatenate([jnp.where(lower, value, other), jnp.where(lower, other, value)])
    return value


def pair_sum(one, two, axis, count):
    masks = [1 << i for i in range(count.bit_length() - 1)]
    one = halving_sum(one, axis, count, masks)
    return one, halving_sum(two, axis, count, masks[:1] + masks[:0:-1])


def gather_rows(rows, n_dp):
    share = rows.shape[0] // n_dp
    mine = lax.dynamic_slice_in_dim(rows, lax.axis_index("dp") * share, share, 0)
    return lax.all_gather(mine.astype(FULL), ("tensor", "dp"), tiled=True)


def per_device(
    n_dp,
    n_tensor,
    latents,
    condition,
    modulator,
    modulator_bias,
    attn_input,
    attn_input_bias,
    attn_output,
    attn_output_bias,
    ffn_input,
    ffn_input_bias,
    ffn_output,
    ffn_output_bias,
    cotangent,
):
    image_count, positions, features = latents.shape
    tokens = image_count * positions
    columns = attn_input.shape[2]
    place = lax.axis_index("tensor")

    weight_t = attn_input.swapaxes(1, 2)
    output_wide = gather_rows(attn_output, n_dp)
    weight_wide = gather_rows(weight_t.reshape(-1, features), n_dp)
    weight_wide = weight_wide.reshape(n_tensor, 3, columns, features)
    in_bias = attn_input_bias.astype(FULL)
    bias_own = jnp.stack([in_bias[0], jnp.zeros_like(in_bias[0]), in_bias[1]])
    bias_full = lax.all_gather(bias_own, "tensor", axis=1, tiled=True)

    cond_float = condition.astype(FULL)
    context_low = jax.nn.silu(cond_float).astype(LOW)
    modulation = flip_sum(mm(context_low, modulator), "tensor", n_tensor)
    modulation = modulation + modulator_bias.astype(FULL)
    pieces = modulation.reshape(image_count, 6, features)[:, None]
    shift_one, scale_one, gate_one = (pieces[:, :, 0], pieces[:, :, 1], pieces[:, :, 2])
    shift_two, scale_two, gate_two = (pieces[:, :, 3], pieces[:, :, 4], pieces[:, :, 5])
    inputs = latents.astype(FULL)
    normed_one, inverse_one = norm_parts(inputs)
    entry_one = (normed_one * (1.0 + scale_one) + shift_one).astype(LOW).reshape(-1, features)
    mixed_t = attention_forward(entry_one, weight_t, bias_own[:, :, None], image_count)
    mixed_full = lax.all_gather(mixed_t, "tensor", tiled=True)
    attention, middle, entry_two, output_full = join_heads(
        mixed_full,
        output_wide,
        attn_output_bias[None],
        latents.reshape(-1, features),
        modulation.reshape(image_count, 6, features),
    )
    attention = attention.reshape(latents.shape)
    middle = middle.reshape(latents.shape)
    normed_two, inverse_two = norm_parts(middle)
    hidden = mm(entry_two, ffn_input) + ffn_input_bias.astype(FULL)
    active, gelu_pull = jax.vjp(lambda inner: jax.nn.gelu(inner, approximate=True), hidden)
    active = active.astype(LOW)
    upstream = cotangent.astype(FULL)
    branch_grad = (gate_two * upstream).astype(LOW).reshape(-1, features)
    active_grad = mm(branch_grad, ffn_output, NT)
    hidden_grad = gelu_pull(active_grad)[0].astype(LOW)
    entry_two_grad = lax.psum(mm(hidden_grad, ffn_input, NT), "tensor").reshape(latents.shape)
    branch = lax.psum_scatter(mm(active, ffn_output), "tensor", tiled=True)
    branch = lax.all_gather(branch, "tensor", tiled=True)
    grad_ffn_output, grad_ffn_input = pair_sum(
        mm(active, branch_grad, TN), mm(entry_two, hidden_grad, TN), "dp", n_dp
    )
    grad_ffn_output_bias = jnp.sum(branch_grad.astype(FULL), axis=0)
    grad_ffn_input_bias = jnp.sum(hidden_grad.astype(FULL), axis=0)

    proj_full, weight_full = project_all(weight_wide, bias_full[:, :, None], entry_one)

    branch = (branch + ffn_output_bias.astype(FULL)).reshape(latents.shape)
    layer_out = (middle + gate_two * branch).astype(LOW)
    gate_two_grad = jnp.sum(upstream * branch, axis=1)

    scale_two_grad = jnp.sum(entry_two_grad * normed_two, axis=1)
    shift_two_grad = jnp.sum(entry_two_grad, axis=1)
    middle_grad = upstream + norm_back(entry_two_grad * (1.0 + scale_two), normed_two, inverse_two)
    gate_one_grad = jnp.sum(middle_grad * attention, axis=1)
    attention_grad = (gate_one * middle_grad).astype(LOW).reshape(-1, features)
    grad_attn_output = mm(mixed_t.astype(LOW), attention_grad)
    grad_attn_output_bias = jnp.sum(attention_grad.astype(FULL), axis=0)
    mixed_grad_t = mm(output_full, attention_grad, NT).astype(LOW)
    proj_grad = attention_backward(proj_full, mixed_grad_t, image_count)
    own = lax.dynamic_slice_in_dim(proj_grad, place * columns, columns, 1)
    grad_attn_input = mm(own.reshape(-1, tokens), entry_one)
    own_sums = jnp.sum(own.astype(FULL), axis=2)
    grad_attn_input_bias = jnp.stack([own_sums[0], own_sums[2]])
    attn_grads = jnp.concatenate([grad_attn_input, grad_attn_output])
    half = attn_grads.shape[0] // 2
    attn_grads = jnp.concatenate(pair_sum(attn_grads[:half], attn_grads[half:], "dp", n_dp))
    grad_attn_input = attn_grads[: 3 * columns].reshape(3, columns, features).swapaxes(1, 2)
    grad_attn_output = attn_grads[3 * columns :]

    entry_one_grad = mm(
        proj_grad.reshape(-1, tokens), weight_full.reshape(-1, features), TN
    ).reshape(latents.shape)
    scale_one_grad = jnp.sum(entry_one_grad * normed_one, axis=1)
    shift_one_grad = jnp.sum(entry_one_grad, axis=1)
    latents_grad = middle_grad + norm_back(
        entry_one_grad * (1.0 + scale_one), normed_one, inverse_one
    )
    modulation_grad = jnp.concatenate(
        [
            shift_one_grad,
            scale_one_grad,
            gate_one_grad,
            shift_two_grad,
            scale_two_grad,
            gate_two_grad,
        ],
        axis=-1,
    ).astype(LOW)
    context_grad = mm(modulation_grad, modulator, NT)
    condition_grad = jax.vjp(jax.nn.silu, cond_float)[1](context_grad)[0]

    small = jnp.concatenate(
        [
            modulation_grad.astype(FULL).reshape(-1),
            context_low.astype(FULL).reshape(-1),
            grad_ffn_output_bias,
            grad_ffn_input_bias,
            grad_attn_output_bias,
            grad_attn_input_bias.reshape(-1),
        ]
    )
    sizes = [image_count * 6 * features, image_count * condition.shape[1]]
    sizes += [features, ffn_input.shape[1], features, 2 * columns]
    spread = lax.optimization_barrier(lax.all_gather(small, "dp"))
    cuts = [sum(sizes[: i + 1]) for i in range(len(sizes) - 1)]
    every = jnp.split(spread, cuts, axis=1)
    all_modulation = every[0].reshape(-1, 6 * features)
    all_context = every[1].reshape(-1, condition.shape[1])
    grad_modulator = mm(all_context.astype(LOW), all_modulation.astype(LOW), TN)
    grad_modulator_bias = jnp.sum(all_modulation, axis=0)
    sums = [jnp.sum(part, axis=0) for part in every[2:]]
    return (
        layer_out,
        latents_grad,
        condition_grad,
        grad_modulator,
        grad_modulator_bias,
        grad_attn_input,
        sums[3].reshape(2, columns),
        grad_attn_output,
        sums[2],
        grad_ffn_input,
        sums[1],
        grad_ffn_output,
        sums[0],
    )


def solution(mesh):
    placed = (
        P("dp", None, None),
        P("dp", "tensor"),
        P("tensor", None),
        P(),
        P(None, None, "tensor"),
        P(None, "tensor"),
        P("tensor", None),
        P(),
        P(None, "tensor"),
        P("tensor"),
        P("tensor", None),
        P(),
        P("dp", None, None),
    )
    return jax.shard_map(
        functools.partial(per_device, mesh.shape["dp"], mesh.shape["tensor"]),
        mesh=mesh,
        in_specs=placed,
        out_specs=(
            P("dp", None, None),
            P("dp", None, None),
            P("dp", "tensor"),
            P("tensor", None),
            P(),
            P(None, None, "tensor"),
            P(None, "tensor"),
            P("tensor", None),
            P(),
            P(None, "tensor"),
            P("tensor"),
            P("tensor", None),
            P(),
        ),
        check_vma=False,
    )
```

time: 524 us -> 488 us (0.931)
  waiting for transfers between devices: 358 us -> 279 us
  Pallas kernels: 0 us -> 28.7 us
  starting transfers between devices: 0.34 us -> 27.8 us
  blocking collectives: 48.3 us -> 24.3 us
  other arithmetic: 28.8 us -> 40.7 us
  matrix products: 35.9 us -> 25.8 us
  local copies, waits for them, and re-layouts: 36.5 us -> 44.5 us
    psum x4 -> x1, waiting for transfers between devices: 358 us -> 33.2 us  [per_device(): lax.psum(mm(hidden_grad, ffn_input, NT), 'tensor').reshape(latents.shape)]
    all_gather x0 -> x4, waiting for transfers between devices: none -> 164 us  [the longest x2 91.5 us: gather_rows(): return lax.all_gather(mine.astype(FULL), ('tensor', 'dp'), tiled=True)]
    psum x2 -> x0, blocking collectives: 48.3 us -> none  [the longest x1 27.1 us: per_device(): lax.psum((grad_modulator, grad_modulator_bias, grad_attn_input, grad_attn...]
    ppermute x0 -> x27, waiting for transfers between devices: none -> 47 us  [flip(): return lax.ppermute(value, axis, [(i, i ^ mask) for i in range(count)])]
    reduce_scatter x0 -> x1, waiting for transfers between devices: none -> 34.3 us  [per_device(): branch = lax.psum_scatter(mm(active, ffn_output), 'tensor', tiled=True)]
    pallas_call x0 -> x4, Pallas kernels: none -> 28.7 us  [the longest x1 11.4 us: attention_backward(): pl.pallas_call(functools.partial(backward_kernel, step), out_shape=jax.Sh...]
    ppermute x0 -> x27, starting transfers between devices: none -> 27.6 us  [flip(): return lax.ppermute(value, axis, [(i, i ^ mask) for i in range(count)])]
    all_gather x0 -> x2, blocking collectives: none -> 24.3 us  [the longest x1 13.6 us: per_device(): bias_full = lax.all_gather(bias_own, 'tensor', axis=1, tiled=True)]
  transfers between devices with their start and end apart: 4 -> 33, of which waited for: 4 -> 20; matrix products, arithmetic and copies ran while one was open for 4% -> 17% of each run, Pallas kernels for 0% -> 4%
where the time goes in v1:
time: 488 us; the launch traced here: 486 us
  waiting for transfers between devices  279 us (57%)
  local copies, waits for them, and re-layouts  44.5 us (9%)
  other arithmetic  40.7 us (8%)
  Pallas kernels  28.7 us (6%)
  starting transfers between devices  27.8 us (6%)
  matrix products  25.8 us (5%)
  blocking collectives  24.3 us (5%)
  between operations  15.1 us (3%)
    all_gather x2, waiting for transfers between devices, gather_rows(): return lax.all_gather(mine.astype(FULL), ('tensor', 'dp'), tiled=True)  91.5 us
    ppermute x27, waiting for transfers between devices, flip(): return lax.ppermute(value, axis, [(i, i ^ mask) for i in range(count)])  47 us
    all_gather x1, waiting for transfers between devices, per_device(): branch = lax.all_gather(branch, 'tensor', tiled=True)  37.4 us
    all_gather x1, waiting for transfers between devices, per_device(): mixed_full = lax.all_gather(mixed_t, 'tensor', tiled=True)  35.3 us
    reduce_scatter x1, waiting for transfers between devices, per_device(): branch = lax.psum_scatter(mm(active, ffn_output), 'tensor', tiled=True)  34.3 us
    psum x1, waiting for transfers between devices, per_device(): lax.psum(mm(hidden_grad, ffn_input, NT), 'tensor').reshape(latents.shape)  33.2 us
    ppermute x27, starting transfers between devices, flip(): return lax.ppermute(value, axis, [(i, i ^ mask) for i in range(count)])  27.6 us
    dot_general x13, matrix products, mm(): return lax.dot_general(left, right, dims, preferred_element_type=FULL)  25.8 us
  transfers between devices with their start and end apart: 33, of which 20 were waited for; matrix products, arithmetic and copies ran while one was open for 17% of the time, Pallas kernels for 4%

profile of v1, /device:TPU:0, one launch (start us, length us, event | category | flops | bytes accessed | tf_op | source)
XLA Modules:
  0.0 485.9 jit_solution(11117329021652527077)
XLA Ops:
  9.7 5.1 %collective-permute-start.2 = (f32[2,4608]{1,0:T(2,128)S(1)}, f32[2,4608]{1,0:T(2,128)S(1)}, u32[]{:S(2)}, u32[]{:S(2)}) collective-permute-start(f32[2,4608]{1,0:T(2,128)S(1)} %fusion.43), channel_id=1, source_target_pairs={{0,3},{1,2},{2,1},{3,0},{4,7},{5,6},{6,5},{7,4},{8,11},{9,10},{10,... | collective-permute-start | bytes 110600 | tf_op jit(solution)/shard_map/ppermute | solution.py:175
  16.7 2.9 collective-permute-done.1
  20.9 3.5 attention_forward.1
  26.9 35.3 %all-gather.7.cloned.1.call-done.mixed_ref = f32[768,512]{1,0:T(8,128)} async-done(((f32[192,512]{1,0:T(8,128)}), f32[768,512]{1,0:T(8,128)}) %all-gather.7.cloned.1.call-update) | async-done | bytes 1572880 | tf_op jit(solution)/shard_map/all_gather | solution.py:253
  62.2 59.6 %all-gather.9.cloned.1.call-done.weight_ref = f32[768,768]{1,0:T(8,128)} async-done(((f32[24,768]{1,0:T(8,128)}), f32[768,768]{1,0:T(8,128)}) %all-gather.9.cloned.1.call-update) | async-done | bytes 2359312 | tf_op jit(solution)/shard_map/all_gather | solution.py:209
  123.0 3.6 join_heads.1
  129.5 2.2 fusion.47
  131.8 34.3 %reduce-scatter.2.cloned.1.call-done = f32[128,768]{1,0:T(8,128)} async-done(((f32[512,768]{1,0:T(8,128)}), f32[128,768]{1,0:T(8,128)}) %reduce-scatter.2.cloned.1.call-update) | async-done | bytes 393232 | tf_op jit(solution)/shard_map/reduce_scatter | solution.py:272
  166.1 37.4 %all-gather.11.cloned.1.call-done = f32[512,768]{1,0:T(8,128)} async-done(((f32[128,768]{1,0:T(8,128)}), f32[512,768]{1,0:T(8,128)}) %all-gather.11.cloned.1.call-update) | async-done | bytes 1572880 | tf_op jit(solution)/shard_map/all_gather | solution.py:273
  203.6 3.8 convert_reduce_fusion.3
  207.4 2.2 convert_reduce_fusion.2
  210.5 2.0 fusion.52
  215.0 13.6 %all-gather.1 = f32[4,192,3]{1,2,0:T(4,128)S(1)} all-gather(f32[1,192,3]{1,2,0:T(4,128)S(1)} %get-tuple-element.87), channel_id=1, replica_groups=mesh['dp'=8,'tensor'=4] {'tensor'}, dimensions={0}, use_global_device_ids=true | all-gather | bytes 11520 | tf_op jit(solution)/shard_map/all_gather | solution.py:240
  230.1 2.5 fusion.46
  247.6 33.2 %all-reduce.2.cloned.1.call-done = f32[512,768]{1,0:T(8,128)} async-done(((f32[512,768]{1,0:T(8,128)}), f32[512,768]{1,0:T(8,128)}) %all-reduce.2.cloned.1.call-update) | async-done | bytes 1572880 | tf_op jit(solution)/shard_map/psum | solution.py:271
  282.8 3.7 fusion.23
  292.1 5.8 %collective-permute-done.23 = f32[96,768]{1,0:T(8,128)S(1)} collective-permute-done((f32[96,768]{1,0:T(8,128)S(1)}, f32[96,768]{1,0:T(8,128)S(1)}, u32[]{:S(2)}, u32[]{:S(2)}) %collective-permute-start.23) | collective-permute-done | bytes 294944 | tf_op jit(solution)/shard_map/ppermute | solution.py:175
  302.1 2.6 collective-permute-done.24
  306.4 3.8 collective-permute-done.18
  310.9 2.2 fusion.28
  313.0 12.9 %collective-permute-done.25 = f32[192,768]{1,0:T(8,128)S(1)} collective-permute-done((f32[192,768]{1,0:T(8,128)S(1)}, f32[192,768]{1,0:T(8,128)S(1)}, u32[]{:S(2)}, u32[]{:S(2)}) %collective-permute-start.25) | collective-permute-done | bytes 589856 | tf_op jit(solution)/shard_map/ppermute | solution.py:175
  329.9 31.9 %all-gather.13.cloned.1.call-done = f32[2304,768]{1,0:T(8,128)} async-done(((f32[72,768]{1,0:T(8,128)}), f32[2304,768]{1,0:T(8,128)}) %all-gather.13.cloned.1.call-update) | async-done | bytes 7077904 | tf_op jit(solution)/shard_map/all_gather | solution.py:209
  363.1 10.2 %project_all.1 = (bf16[3,768,512]{2,1,0:T(8,128)(2,1)S(1)}, bf16[3,768,768]{2,1,0:T(8,128)(2,1)}) custom-call(f32[4,3,192,768]{3,2,1,0:T(8,128)} %bitcast.93, f32[3,768,1]{2,1,0:T(8,128)S(1)} %copy-done.7, bf16[512,768]{1,0:T(8,128)(2,1)S(1)} %bitcast.88), custom_call_target="tpu_custom_call" | custom-call | tf_op jit(solution)/shard_map/project_all/pallas_call | solution.py:153
  373.3 11.4 %attention_backward.1 = bf16[3,768,512]{2,1,0:T(8,128)(2,1)S(1)} custom-call(bf16[3,768,512]{2,1,0:T(8,128)(2,1)S(1)} %get-tuple-element.21.proj_ref, bf16[768,512]{1,0:T(8,128)(2,1)S(1)} %convolution_convert_fusion.grad_ref), custom_call_target="tpu_custom_call" | custom-call | tf_op jit(solution)/shard_map/attention_backward/pallas_call | solution.py:91
  388.8 4.3 copy.42
  393.2 5.2 %fusion.12 = (bf16[2,768]{1,0:T(2,128)(2,1)S(1)}, f32[2,256]{1,0:T(2,128)S(1)}, f32[2,256]{1,0:T(2,128)S(1)}, bf16[2,768]{1,0:T(2,128)(2,1)S(1)}, f32[2,256,768]{2,1,0:T(8,128)S(1)}) fusion(bf16[2,256,768]{2,1,0:T(8,128)(2,1)S(1)} %copy-done.3, f32[2,256]{1,0:T(2,128)S(1)} %add_rsqrt_fusion.1, f32[2,256]{1,0:T(2,128)S(1)} %broadcast_multiply_fusion.5, ...), kind=kOutput, calls=%fused_computation.22 | convolution fusion | flops 1815867392 | bytes 8278016 | tf_op jit(solution)/shard_map/dot_general | solution.py:21
  408.0 10.7 %all-gather = f32[98304]{0:T(1024)} all-gather(f32[12288]{0:T(1024)S(1)} %constant_dynamic-update-slice_fusion.7), channel_id=2, replica_groups=mesh['dp'=8,'tensor'=4] {'dp'}, dimensions={0}, use_global_device_ids=true | all-gather | bytes 442368 | tf_op jit(solution)/shard_map/all_gather | solution.py:339
  437.0 2.4 fusion.53
  447.2 6.0 %collective-permute-done.10 = f32[96,768]{1,0:T(8,128)S(1)} collective-permute-done((f32[96,768]{1,0:T(8,128)S(1)}, f32[96,768]{1,0:T(8,128)S(1)}, u32[]{:S(2)}, u32[]{:S(2)}) %collective-permute-start.10) | collective-permute-done | bytes 294944 | tf_op jit(solution)/shard_map/ppermute | solution.py:175
  456.4 2.2 collective-permute-done.11
  461.6 2.2 collective-permute-done.12
  468.5 3.1 collective-permute-done.13
  (286 shorter events, 108.6 us)
Async XLA Ops:
  7.2 55.0 %all-gather.7.cloned.1.call-start = ((), (), s32[]{:S(2)}) async-start(), calls=%async_computation.1 | async-start | bytes 1966080 | tf_op jit(solution)/shard_map/all_gather | solution.py:253
  9.7 7.0 %collective-permute-start.2 = (f32[2,4608]{1,0:T(2,128)S(1)}, f32[2,4608]{1,0:T(2,128)S(1)}, u32[]{:S(2)}, u32[]{:S(2)}) collective-permute-start(f32[2,4608]{1,0:T(2,128)S(1)} %fusion.43), channel_id=1, source_target_pairs={{0,3},{1,2},{2,1},{3,0},{4,7},{5,6},{6,5},{7,4},{8,11},{9,10},{10,... | collective-permute-start | bytes 110600 | tf_op jit(solution)/shard_map/ppermute | solution.py:175
  14.7 4.9 collective-permute-start.1
  14.7 4.9 collective-permute-start
  25.3 96.5 %all-gather.9.cloned.1.call-start = ((), (), s32[]{:S(2)}) async-start(), calls=%async_computation.2 | async-start | bytes 2433024 | tf_op jit(solution)/shard_map/all_gather | solution.py:209
  26.8 139.2 %reduce-scatter.2.cloned.1.call-start = ((), (), s32[]{:S(2)}) async-start(), calls=%async_computation.3 | async-start | bytes 1966080 | tf_op jit(solution)/shard_map/reduce_scatter | solution.py:272
  131.7 71.9 %all-gather.11.cloned.1.call-start = ((), (), s32[]{:S(2)}) async-start(), calls=%async_computation.4 | async-start | bytes 1966080 | tf_op jit(solution)/shard_map/all_gather | solution.py:273
  166.1 114.8 %all-reduce.2.cloned.1.call-start = ((), (), s32[]{:S(2)}) async-start(), calls=%async_computation.5 | async-start | bytes 3145728 | tf_op jit(solution)/shard_map/psum | solution.py:271
  212.5 149.3 %all-gather.13.cloned.1.call-start = ((), (), s32[]{:S(2)}) async-start(), calls=%async_computation.6 | async-start | bytes 7299072 | tf_op jit(solution)/shard_map/all_gather | solution.py:209
  234.5 4.6 collective-permute-start.21
  238.5 4.9 %collective-permute-start.15 = (f32[384,768]{1,0:T(8,128)}, f32[384,768]{1,0:T(8,128)}, u32[]{:S(2)}, u32[]{:S(2)}) collective-permute-start(f32[384,768]{1,0:T(8,128)} %constant_dynamic-slice_fusion.5), channel_id=1, source_target_pairs={{0,4},{4,0},{8,12},{12,8},{16,20},{20,16},{24,28},{28,24},{1,5},{5... | collective-permute-start | bytes 3538952 | tf_op jit(solution)/shard_map/ppermute | solution.py:175
  242.0 44.5 %collective-permute-start.22 = (f32[192,768]{1,0:T(8,128)}, f32[192,768]{1,0:T(8,128)}, u32[]{:S(2)}, u32[]{:S(2)}) collective-permute-start(f32[192,768]{1,0:T(8,128)} %constant_dynamic-slice_fusion.1), channel_id=1, source_target_pairs={{0,8},{4,12},{8,0},{12,4},{16,24},{20,28},{24,16},{28,20},{1,9},{5... | collective-permute-start | bytes 1769480 | tf_op jit(solution)/shard_map/ppermute | solution.py:175
  246.2 43.2 %collective-permute-start.16 = (f32[192,768]{1,0:T(8,128)}, f32[192,768]{1,0:T(8,128)}, u32[]{:S(2)}, u32[]{:S(2)}) collective-permute-start(f32[192,768]{1,0:T(8,128)} %constant_dynamic-slice_fusion.4), channel_id=1, source_target_pairs={{0,16},{4,20},{8,24},{12,28},{16,0},{20,4},{24,8},{28,12},{1,17},{... | collective-permute-start | bytes 1769480 | tf_op jit(solution)/shard_map/ppermute | solution.py:175
  287.8 10.1 %collective-permute-start.23 = (f32[96,768]{1,0:T(8,128)S(1)}, f32[96,768]{1,0:T(8,128)S(1)}, u32[]{:S(2)}, u32[]{:S(2)}) collective-permute-start(f32[96,768]{1,0:T(8,128)S(1)} %constant_dynamic-slice_fusion), channel_id=1, source_target_pairs={{0,16},{4,20},{8,24},{12,28},{16,0},{20,4},{24,8},{28,12},{1,17},{... | collective-permute-start | bytes 884744 | tf_op jit(solution)/shard_map/ppermute | solution.py:175
  290.6 9.5 %collective-permute-start.17 = (f32[96,768]{1,0:T(8,128)S(1)}, f32[96,768]{1,0:T(8,128)S(1)}, u32[]{:S(2)}, u32[]{:S(2)}) collective-permute-start(f32[96,768]{1,0:T(8,128)S(1)} %constant_dynamic-slice_fusion.3), channel_id=1, source_target_pairs={{0,8},{4,12},{8,0},{12,4},{16,24},{20,28},{24,16},{28,20},{1,9},{5... | collective-permute-start | bytes 884744 | tf_op jit(solution)/shard_map/ppermute | solution.py:175
  297.9 6.8 %collective-permute-start.24 = (f32[96,768]{1,0:T(8,128)S(1)}, f32[96,768]{1,0:T(8,128)S(1)}, u32[]{:S(2)}, u32[]{:S(2)}) collective-permute-start(f32[96,768]{1,0:T(8,128)S(1)} %dynamic-slice_add_fusion.5), channel_id=1, source_target_pairs={{0,16},{4,20},{8,24},{12,28},{16,0},{20,4},{24,8},{28,12},{1,17},{... | collective-permute-start | bytes 884744 | tf_op jit(solution)/shard_map/ppermute | solution.py:175
  300.2 10.0 %collective-permute-start.18 = (f32[96,768]{1,0:T(8,128)S(1)}, f32[96,768]{1,0:T(8,128)S(1)}, u32[]{:S(2)}, u32[]{:S(2)}) collective-permute-start(f32[96,768]{1,0:T(8,128)S(1)} %dynamic-slice_add_fusion.6), channel_id=1, source_target_pairs={{0,8},{4,12},{8,0},{12,4},{16,24},{20,28},{24,16},{28,20},{1,9},{5... | collective-permute-start | bytes 884744 | tf_op jit(solution)/shard_map/ppermute | solution.py:175
  304.8 21.1 %collective-permute-start.25 = (f32[192,768]{1,0:T(8,128)S(1)}, f32[192,768]{1,0:T(8,128)S(1)}, u32[]{:S(2)}, u32[]{:S(2)}) collective-permute-start(f32[192,768]{1,0:T(8,128)S(1)} %pad_maximum_fusion.8), channel_id=1, source_target_pairs={{0,8},{4,12},{8,0},{12,4},{16,24},{20,28},{24,16},{28,20},{1,9},{5... | collective-permute-start | bytes 1769480 | tf_op jit(solution)/shard_map/ppermute | solution.py:175
  310.3 17.0 %collective-permute-start.19 = (f32[192,768]{1,0:T(8,128)S(1)}, f32[192,768]{1,0:T(8,128)S(1)}, u32[]{:S(2)}, u32[]{:S(2)}) collective-permute-start(f32[192,768]{1,0:T(8,128)S(1)} %pad_maximum_fusion.7), channel_id=1, source_target_pairs={{0,16},{4,20},{8,24},{12,28},{16,0},{20,4},{24,8},{28,12},{1,17},{... | collective-permute-start | bytes 1769480 | tf_op jit(solution)/shard_map/ppermute | solution.py:175
  327.2 112.2 %collective-permute-start.26 = (f32[384,768]{1,0:T(8,128)}, f32[384,768]{1,0:T(8,128)}, u32[]{:S(2)}, u32[]{:S(2)}) collective-permute-start(f32[384,768]{1,0:T(8,128)} %pad_maximum_fusion.4), channel_id=1, source_target_pairs={{0,4},{4,0},{8,12},{12,8},{16,20},{20,16},{24,28},{28,24},{1,5},{5... | collective-permute-start | bytes 3538952 | tf_op jit(solution)/shard_map/ppermute | solution.py:175
  329.4 111.6 %collective-permute-start.20 = (f32[384,768]{1,0:T(8,128)}, f32[384,768]{1,0:T(8,128)}, u32[]{:S(2)}, u32[]{:S(2)}) collective-permute-start(f32[384,768]{1,0:T(8,128)} %pad_maximum_fusion.3), channel_id=1, source_target_pairs={{0,4},{4,0},{8,12},{12,8},{16,20},{20,16},{24,28},{28,24},{1,5},{5... | collective-permute-start | bytes 3538952 | tf_op jit(solution)/shard_map/ppermute | solution.py:175
  425.9 16.6 %collective-permute-start.9 = (f32[192,768]{1,0:T(8,128)}, f32[192,768]{1,0:T(8,128)}, u32[]{:S(2)}, u32[]{:S(2)}) collective-permute-start(f32[192,768]{1,0:T(8,128)} %fusion.25), channel_id=1, source_target_pairs={{0,4},{4,0},{8,12},{12,8},{16,20},{20,16},{24,28},{28,24},{1,5},{5... | collective-permute-start | bytes 1769480 | tf_op jit(solution)/shard_map/ppermute | solution.py:175
  427.1 17.5 %collective-permute-start.3 = (f32[192,768]{1,0:T(8,128)}, f32[192,768]{1,0:T(8,128)}, u32[]{:S(2)}, u32[]{:S(2)}) collective-permute-start(f32[192,768]{1,0:T(8,128)} %constant_dynamic-slice_fusion.10), channel_id=1, source_target_pairs={{0,4},{4,0},{8,12},{12,8},{16,20},{20,16},{24,28},{28,24},{1,5},{5... | collective-permute-start | bytes 1769480 | tf_op jit(solution)/shard_map/ppermute | solution.py:175
  443.9 9.3 %collective-permute-start.10 = (f32[96,768]{1,0:T(8,128)S(1)}, f32[96,768]{1,0:T(8,128)S(1)}, u32[]{:S(2)}, u32[]{:S(2)}) collective-permute-start(f32[96,768]{1,0:T(8,128)S(1)} %constant_dynamic-slice_fusion.7), channel_id=1, source_target_pairs={{0,16},{4,20},{8,24},{12,28},{16,0},{20,4},{24,8},{28,12},{1,17},{... | collective-permute-start | bytes 884744 | tf_op jit(solution)/shard_map/ppermute | solution.py:175
  445.7 9.0 %collective-permute-start.4 = (f32[96,768]{1,0:T(8,128)S(1)}, f32[96,768]{1,0:T(8,128)S(1)}, u32[]{:S(2)}, u32[]{:S(2)}) collective-permute-start(f32[96,768]{1,0:T(8,128)S(1)} %constant_dynamic-slice_fusion.9), channel_id=1, source_target_pairs={{0,8},{4,12},{8,0},{12,4},{16,24},{20,28},{24,16},{28,20},{1,9},{5... | collective-permute-start | bytes 884744 | tf_op jit(solution)/shard_map/ppermute | solution.py:175
  453.3 5.4 %collective-permute-start.11 = (f32[48,768]{1,0:T(8,128)S(1)}, f32[48,768]{1,0:T(8,128)S(1)}, u32[]{:S(2)}, u32[]{:S(2)}) collective-permute-start(f32[48,768]{1,0:T(8,128)S(1)} %constant_dynamic-slice_fusion.6), channel_id=1, source_target_pairs={{0,8},{4,12},{8,0},{12,4},{16,24},{20,28},{24,16},{28,20},{1,9},{5... | collective-permute-start | bytes 442376 | tf_op jit(solution)/shard_map/ppermute | solution.py:175
  454.8 5.2 %collective-permute-start.5 = (f32[48,768]{1,0:T(8,128)S(1)}, f32[48,768]{1,0:T(8,128)S(1)}, u32[]{:S(2)}, u32[]{:S(2)}) collective-permute-start(f32[48,768]{1,0:T(8,128)S(1)} %constant_dynamic-slice_fusion.8), channel_id=1, source_target_pairs={{0,16},{4,20},{8,24},{12,28},{16,0},{20,4},{24,8},{28,12},{1,17},{... | collective-permute-start | bytes 442376 | tf_op jit(solution)/shard_map/ppermute | solution.py:175
  458.7 5.2 %collective-permute-start.12 = (f32[48,768]{1,0:T(8,128)S(1)}, f32[48,768]{1,0:T(8,128)S(1)}, u32[]{:S(2)}, u32[]{:S(2)}) collective-permute-start(f32[48,768]{1,0:T(8,128)S(1)} %dynamic-slice_add_fusion.9), channel_id=1, source_target_pairs={{0,8},{4,12},{8,0},{12,4},{16,24},{20,28},{24,16},{28,20},{1,9},{5... | collective-permute-start | bytes 442376 | tf_op jit(solution)/shard_map/ppermute | solution.py:175
  460.1 6.5 %collective-permute-start.6 = (f32[48,768]{1,0:T(8,128)S(1)}, f32[48,768]{1,0:T(8,128)S(1)}, u32[]{:S(2)}, u32[]{:S(2)}) collective-permute-start(f32[48,768]{1,0:T(8,128)S(1)} %dynamic-slice_add_fusion.10), channel_id=1, source_target_pairs={{0,16},{4,20},{8,24},{12,28},{16,0},{20,4},{24,8},{28,12},{1,17},{... | collective-permute-start | bytes 442376 | tf_op jit(solution)/shard_map/ppermute | solution.py:175
  463.9 7.7 %collective-permute-start.13 = (f32[96,768]{1,0:T(8,128)S(1)}, f32[96,768]{1,0:T(8,128)S(1)}, u32[]{:S(2)}, u32[]{:S(2)}) collective-permute-start(f32[96,768]{1,0:T(8,128)S(1)} %pad_maximum_fusion.10), channel_id=1, source_target_pairs={{0,16},{4,20},{8,24},{12,28},{16,0},{20,4},{24,8},{28,12},{1,17},{... | collective-permute-start | bytes 884744 | tf_op jit(solution)/shard_map/ppermute | solution.py:175
  466.6 6.8 %collective-permute-start.7 = (f32[96,768]{1,0:T(8,128)S(1)}, f32[96,768]{1,0:T(8,128)S(1)}, u32[]{:S(2)}, u32[]{:S(2)}) collective-permute-start(f32[96,768]{1,0:T(8,128)S(1)} %pad_maximum_fusion.9), channel_id=1, source_target_pairs={{0,8},{4,12},{8,0},{12,4},{16,24},{20,28},{24,16},{28,20},{1,9},{5... | collective-permute-start | bytes 884744 | tf_op jit(solution)/shard_map/ppermute | solution.py:175
  471.7 5.0 %collective-permute-start.14 = (f32[192,768]{1,0:T(8,128)S(1)}, f32[192,768]{1,0:T(8,128)S(1)}, u32[]{:S(2)}, u32[]{:S(2)}) collective-permute-start(f32[192,768]{1,0:T(8,128)S(1)} %pad_maximum_fusion.6), channel_id=1, source_target_pairs={{0,4},{4,0},{8,12},{12,8},{16,20},{20,16},{24,28},{28,24},{1,5},{5... | collective-permute-start | bytes 1769480 | tf_op jit(solution)/shard_map/ppermute | solution.py:175
  (54 other events, 252.4 us)
Sparse Core Ops, SparseCore 0:
  25.4 36.7 all-gather.6
  65.7 56.0 all-gather.8
  131.8 34.1 reduce-scatter.1
  167.5 36.0 all-gather.10
  212.6 68.1 all-reduce.1
  283.6 78.1 all-gather.12

commit v2 on v1

--- a/solution.py
+++ b/solution.py
@@ -102,10 +102,30 @@
     )(proj_t, grad_t)
 
 
-def join_kernel(mixed_ref, weight_ref, bias_ref, inputs_ref, mod_ref, attention_ref, middle_ref, entry_ref, low_ref):
-    weight = weight_ref[...].astype(LOW)
-    low_ref[...] = weight
-    attention = mm(mixed_ref[...].astype(LOW), weight, TN) + bias_ref[...].astype(FULL)
+def put_in_order(place_ref, pieces, wide_ref):
+    groups, share = place_ref.shape[0] - 1, pieces[0].shape[2]
+    rows = wide_ref.shape[0] // groups
+    for side in range(2):
+        for half in range(2):
+            piece = pieces[2 * side + half]
+            for spot in range(4):
+                first, second = spot % 2, spot // 2
+                mask = side + (2 * first + 4 * second if half == 0 else 4 * first + 2 * second)
+                share_at = (place_ref[0] ^ mask) * share
+                for k in range(2):
+                    start = place_ref[1 + 2 * half + k] * rows + share_at
+                    wide_ref[pl.ds(pl.multiple_of(start, 8), share), :] = piece[spot, k]
+
+
+def join_kernel(place_ref, mixed_ref, bias_ref, inputs_ref, mod_ref, *refs):
+    pieces, (attention_ref, middle_ref, entry_ref, low_ref, wide_ref) = refs[:-5], refs[-5:]
+
+    @pl.when(pl.program_id(0) == 0)
+    def _():
+        put_in_order(place_ref, pieces, wide_ref)
+        low_ref[...] = wide_ref[...].astype(LOW)
+
+    attention = mm(mixed_ref[...].astype(LOW), low_ref[...], TN) + bias_ref[...].astype(FULL)
     attention_ref[...] = attention
     middle = inputs_ref[...].astype(FULL) + mod_ref[0, 2:3, :] * attention
     middle_ref[...] = middle
@@ -113,62 +133,170 @@
     entry_ref[...] = (normed * (1.0 + mod_ref[0, 4:5, :]) + mod_ref[0, 3:4, :]).astype(LOW)
 
 
-def join_heads(mixed, weight, bias, inputs, modulation):
+def join_heads(places, mixed, pieces, bias, inputs, modulation):
     images = modulation.shape[0]
     tokens, width = inputs.shape
     positions = tokens // images
+    rows = mixed.shape[0]
     by_image = pl.BlockSpec((positions, width), lambda g: (g, 0))
-    whole = pl.BlockSpec(weight.shape, lambda g: (0, 0))
+    piece = pl.BlockSpec(pieces[0].shape, lambda g: (0, 0, 0, 0))
     return pl.pallas_call(
         join_kernel,
         out_shape=(
             jax.ShapeDtypeStruct((tokens, width), FULL),
             jax.ShapeDtypeStruct((tokens, width), FULL),
             jax.ShapeDtypeStruct((tokens, width), LOW),
-            jax.ShapeDtypeStruct(weight.shape, LOW),
+            jax.ShapeDtypeStruct((rows, width), LOW),
         ),
         grid=(images,),
         in_specs=[
+            pl.BlockSpec(memory_space=pltpu.SMEM),
+            pl.BlockSpec((rows, positions), lambda g: (0, g)),
+            pl.BlockSpec((1, width), lambda g: (0, 0)),
+            by_image,
+            pl.BlockSpec((1, 6, width), lambda g: (g, 0, 0)),
+        ]
+        + [piece] * len(pieces),
+        out_specs=(by_image, by_image, by_image, pl.BlockSpec((rows, width), lambda g: (0, 0))),
+        scratch_shapes=[pltpu.VMEM((rows, width), FULL)],
+        compiler_params=pltpu.CompilerParams(vmem_limit_bytes=48 * 2**20),
+        name="join_heads",
+    )(places, mixed, bias, inputs, modulation, *pieces)
+
+
+def project_kernel(place_ref, bias_ref, entry_ref, *refs):
+    pieces, (out_ref, low_ref, wide_ref) = refs[:-3], refs[-3:]
+    groups = place_ref.shape[0] - 1
+    columns = wide_ref.shape[0] // (3 * groups)
+    put_in_order(place_ref, pieces, wide_ref)
+    entry = entry_ref[...]
+    for t in range(groups):
+        for j in range(3):
+            at = (3 * t + j) * columns
+            weight = wide_ref[at : at + columns, :].astype(LOW)
+            row = slice(t * columns, (t + 1) * columns)
+            low_ref[j, row, :] = weight
+            out_ref[j, row, :] = (mm(weight, entry, NT) + bias_ref[j, row]).astype(LOW)
+
+
+def project_all(pieces, places, bias, entry):
+    groups = places.shape[0] - 1
+    tokens, width = entry.shape
+    vmem = pl.BlockSpec(memory_space=pltpu.VMEM)
+    rows = bias.shape[1]
+    return pl.pallas_call(
+        project_kernel,
+        out_shape=(
+            jax.ShapeDtypeStruct((3, rows, tokens), LOW),
+            jax.ShapeDtypeStruct((3, rows, width), LOW),
+        ),
+        in_specs=[pl.BlockSpec(memory_space=pltpu.SMEM)] + [vmem] * (2 + len(pieces)),
+        out_specs=(vmem, vmem),
+        scratch_shapes=[pltpu.VMEM((3 * rows, width), FULL)],
+        compiler_params=pltpu.CompilerParams(vmem_limit_bytes=48 * 2**20),
+        name="project_all",
+    )(places, bias, entry, *pieces)
+
+
+def middle_kernel(
+    grad_ref, middle_ref, attention_ref, upstream_ref, mod_ref, weight_ref,
+    middle_grad_ref, low_ref, mixed_grad_ref, sums_ref,
+):
+    grad = grad_ref[...]
+    normed, inverse = norm_parts(middle_ref[...])
+    sums_ref[0, 2:3, :] = jnp.sum(grad * normed, axis=0, keepdims=True)
+    sums_ref[0, 1:2, :] = jnp.sum(grad, axis=0, keepdims=True)
+    middle_grad = upstream_ref[...].astype(FULL)
+    middle_grad = middle_grad + norm_back(grad * (1.0 + mod_ref[0, 4:5, :]), normed, inverse)
+    middle_grad_ref[...] = middle_grad
+    sums_ref[0, 0:1, :] = jnp.sum(middle_grad * attention_ref[...], axis=0, keepdims=True)
+    low = (mod_ref[0, 2:3, :] * middle_grad).astype(LOW)
+    low_ref[...] = low
+    sums_ref[0, 3:4, :] = jnp.sum(low.astype(FULL), axis=0, keepdims=True)
+    mixed_grad_ref[...] = mm(weight_ref[...], low, NT).astype(LOW)
+
+
+def middle_backward(grad, middle, attention, upstream, modulation, weight):
+    images = modulation.shape[0]
+    tokens, width = grad.shape
+    positions = tokens // images
+    by_image = pl.BlockSpec((positions, width), lambda g: (g, 0))
+    return pl.pallas_call(
+        middle_kernel,
+        out_shape=(
+            jax.ShapeDtypeStruct((tokens, width), FULL),
+            jax.ShapeDtypeStruct((tokens, width), LOW),
+            jax.ShapeDtypeStruct((weight.shape[0], tokens), LOW),
+            jax.ShapeDtypeStruct((images, 4, width), FULL),
+        ),
+        grid=(images,),
+        in_specs=[
+            by_image,
+            by_image,
+            by_image,
+            by_image,
+            pl.BlockSpec((1, 6, width), lambda g: (g, 0, 0)),
+            pl.BlockSpec(weight.shape, lambda g: (0, 0)),
+        ],
+        out_specs=(
+            by_image,
+            by_image,
             pl.BlockSpec((weight.shape[0], positions), lambda g: (0, g)),
-            whole,
-            pl.BlockSpec((1, width), lambda g: (0, 0)),
+            pl.BlockSpec((1, 4, width), lambda g: (g, 0, 0)),
+        ),
+        compiler_params=pltpu.CompilerParams(vmem_limit_bytes=48 * 2**20),
+        name="middle_backward",
+    )(grad, middle, attention, upstream, modulation, weight)
+
+
+def entry_kernel(proj_ref, weight_ref, inputs_ref, middle_grad_ref, mod_ref, out_ref, sums_ref):
+    grad = mm(proj_ref[...], weight_ref[...], TN)
+    normed, inverse = norm_parts(inputs_ref[...].astype(FULL))
+    sums_ref[0, 0:1, :] = jnp.sum(grad, axis=0, keepdims=True)
+    sums_ref[0, 1:2, :] = jnp.sum(grad * normed, axis=0, keepdims=True)
+    back = norm_back(grad * (1.0 + mod_ref[0, 1:2, :]), normed, inverse)
+    out_ref[...] = middle_grad_ref[...] + back
+
+
+def entry_backward(proj_grad, weight, inputs, middle_grad, modulation):
+    images = modulation.shape[0]
+    tokens, width = inputs.shape
+    positions = tokens // images
+    by_image = pl.BlockSpec((positions, width), lambda g: (g, 0))
+    return pl.pallas_call(
+        entry_kernel,
+        out_shape=(
+            jax.ShapeDtypeStruct((tokens, width), FULL),
+            jax.ShapeDtypeStruct((images, 2, width), FULL),
+        ),
+        grid=(images,),
+        in_specs=[
+            pl.BlockSpec((proj_grad.shape[0], positions), lambda g: (0, g)),
+            pl.BlockSpec(weight.shape, lambda g: (0, 0)),
+            by_image,
             by_image,
             pl.BlockSpec((1, 6, width), lambda g: (g, 0, 0)),
         ],
-        out_specs=(by_image, by_image, by_image, whole),
+        out_specs=(by_image, pl.BlockSpec((1, 2, width), lambda g: (g, 0, 0))),
         compiler_params=pltpu.CompilerParams(vmem_limit_bytes=48 * 2**20),
-        name="join_heads",
-    )(mixed, weight, bias, inputs, modulation)
-
-
-def project_kernel(weight_ref, bias_ref, entry_ref, out_ref, low_ref):
-    weight = weight_ref[0, 0].astype(LOW)
-    low_ref[0] = weight
-    out_ref[0] = (mm(weight, entry_ref[...], NT) + bias_ref[0]).astype(LOW)
-
-
-def project_all(weight, bias, entry):
-    groups, _, columns, width = weight.shape
-    tokens = entry.shape[0]
-    return pl.pallas_call(
-        project_kernel,
-        out_shape=(
-            jax.ShapeDtypeStruct((3, groups * columns, tokens), LOW),
-            jax.ShapeDtypeStruct((3, groups * columns, width), LOW),
-        ),
-        grid=(3, groups),
-        in_specs=[
-            pl.BlockSpec((1, 1, columns, width), lambda j, t: (t, j, 0, 0)),
-            pl.BlockSpec((1, columns, 1), lambda j, t: (j, t, 0)),
-            pl.BlockSpec((tokens, width), lambda j, t: (0, 0)),
-        ],
-        out_specs=(
-            pl.BlockSpec((1, columns, tokens), lambda j, t: (j, t, 0)),
-            pl.BlockSpec((1, columns, width), lambda j, t: (j, t, 0)),
-        ),
-        compiler_params=pltpu.CompilerParams(vmem_limit_bytes=48 * 2**20),
-        name="project_all",
-    )(weight, bias, entry)
+        name="entry_backward",
+    )(proj_grad, weight, inputs, middle_grad, modulation)
+
+
+def tie_kernel(*refs):
+    pass
+
+
+def tie(value, *others):
+    anywhere = pl.BlockSpec(memory_space=pl.ANY)
+    return pl.pallas_call(
+        tie_kernel,
+        out_shape=jax.ShapeDtypeStruct(value.shape, value.dtype),
+        in_specs=[anywhere] * (1 + len(others)),
+        out_specs=anywhere,
+        input_output_aliases={0: 0},
+        name="tie",
+    )(value, *others)
 
 
 def flip(value, axis, count, mask):
@@ -182,7 +310,12 @@
     return parts[0]
 
 
-def halving_sum(value, axis, count, masks):
+def dp_masks(count):
+    masks = [1 << i for i in range(count.bit_length() - 1)]
+    return masks, masks[:1] + masks[:0:-1]
+
+
+def halve(value, axis, count, masks):
     place = lax.axis_index(axis)
     for mask in masks:
         half = value.shape[0] // 2
@@ -190,6 +323,11 @@
         away = lax.dynamic_slice_in_dim(value, (1 - side) * half, half, 0)
         kept = lax.dynamic_slice_in_dim(value, side * half, half, 0)
         value = kept + flip(away, axis, count, mask)
+    return value
+
+
+def double(value, axis, count, masks):
+    place = lax.axis_index(axis)
     for mask in reversed(masks):
         other = flip(value, axis, count, mask)
         lower = (place // mask) % 2 == 0
@@ -197,16 +335,24 @@
     return value
 
 
-def pair_sum(one, two, axis, count):
-    masks = [1 << i for i in range(count.bit_length() - 1)]
-    one = halving_sum(one, axis, count, masks)
-    return one, halving_sum(two, axis, count, masks[:1] + masks[:0:-1])
-
-
-def gather_rows(rows, n_dp):
-    share = rows.shape[0] // n_dp
-    mine = lax.dynamic_slice_in_dim(rows, lax.axis_index("dp") * share, share, 0)
-    return lax.all_gather(mine.astype(FULL), ("tensor", "dp"), tiled=True)
+def gather_z(rows, n_tensor):
+    share = rows.shape[0] // 8
+    mine = lax.dynamic_slice_in_dim(rows, (lax.axis_index("dp") % 8) * share, share, 0).astype(FULL)
+    parts = [mine] + [flip(mine, "tensor", n_tensor, mask) for mask in range(1, n_tensor)]
+    return [jnp.stack(parts[:2])[None], jnp.stack(parts[2:])[None]]
+
+
+def gather_pieces(pieces, n_dp):
+    for masks in ((2, 4), (4, 2)):
+        moved = [flip(piece, "dp", n_dp, mask) for piece, mask in zip(pieces, masks)]
+        pieces = [jnp.concatenate(pair) for pair in zip(pieces, moved)]
+    return pieces + [flip(piece, "dp", n_dp, 1) for piece in pieces]
+
+
+def as_one(function, *operands):
+    shapes = jax.eval_shape(function, *operands)
+    nothing = lambda *_: jax.tree.map(lambda leaf: jnp.zeros(leaf.shape, leaf.dtype), shapes)
+    return lax.cond(lax.axis_index("dp") >= 0, function, nothing, *operands)
 
 
 def per_device(
@@ -232,35 +378,43 @@
     place = lax.axis_index("tensor")
 
     weight_t = attn_input.swapaxes(1, 2)
-    output_wide = gather_rows(attn_output, n_dp)
-    weight_wide = gather_rows(weight_t.reshape(-1, features), n_dp)
-    weight_wide = weight_wide.reshape(n_tensor, 3, columns, features)
+    places = [lax.axis_index("dp") % 8] + [place ^ mask for mask in range(n_tensor)]
+    places = jnp.stack(places).astype(jnp.int32)
+    orders = dp_masks(n_dp)
+    output_pieces = gather_pieces(gather_z(attn_output, n_tensor), n_dp)
     in_bias = attn_input_bias.astype(FULL)
     bias_own = jnp.stack([in_bias[0], jnp.zeros_like(in_bias[0]), in_bias[1]])
-    bias_full = lax.all_gather(bias_own, "tensor", axis=1, tiled=True)
+    bias_full = jnp.zeros((3, n_tensor * columns), FULL)
+    bias_full = lax.dynamic_update_slice_in_dim(bias_full, bias_own, place * columns, 1)
 
     cond_float = condition.astype(FULL)
     context_low = jax.nn.silu(cond_float).astype(LOW)
-    modulation = flip_sum(mm(context_low, modulator), "tensor", n_tensor)
-    modulation = modulation + modulator_bias.astype(FULL)
-    pieces = modulation.reshape(image_count, 6, features)[:, None]
-    shift_one, scale_one, gate_one = (pieces[:, :, 0], pieces[:, :, 1], pieces[:, :, 2])
-    shift_two, scale_two, gate_two = (pieces[:, :, 3], pieces[:, :, 4], pieces[:, :, 5])
+    partial = mm(context_low, modulator)
+    shared = jnp.concatenate([partial.reshape(-1), bias_full.reshape(-1)]).reshape(-1, 128)
+    shared = flip_sum(shared, "tensor", n_tensor).reshape(-1)
+    bias_full = shared[partial.size :].reshape(3, -1, 1)
+    modulation = shared[: partial.size].reshape(partial.shape) + modulator_bias.astype(FULL)
+    modulation = modulation.reshape(image_count, 6, features)
+    pieces = modulation[:, None]
+    shift_one, scale_one, gate_two = (pieces[:, :, 0], pieces[:, :, 1], pieces[:, :, 5])
     inputs = latents.astype(FULL)
-    normed_one, inverse_one = norm_parts(inputs)
+    normed_one = norm_parts(inputs)[0]
     entry_one = (normed_one * (1.0 + scale_one) + shift_one).astype(LOW).reshape(-1, features)
     mixed_t = attention_forward(entry_one, weight_t, bias_own[:, :, None], image_count)
-    mixed_full = lax.all_gather(mixed_t, "tensor", tiled=True)
+    mixed_full = jnp.zeros((n_tensor,) + mixed_t.shape, FULL)
+    for mask in range(n_tensor):
+        part = flip(mixed_t, "tensor", n_tensor, mask) if mask else mixed_t
+        mixed_full = lax.dynamic_update_index_in_dim(mixed_full, part, place ^ mask, 0)
+    mixed_full = mixed_full.reshape(-1, tokens)
     attention, middle, entry_two, output_full = join_heads(
+        places,
         mixed_full,
-        output_wide,
+        output_pieces,
         attn_output_bias[None],
         latents.reshape(-1, features),
-        modulation.reshape(image_count, 6, features),
-    )
-    attention = attention.reshape(latents.shape)
-    middle = middle.reshape(latents.shape)
-    normed_two, inverse_two = norm_parts(middle)
+        modulation,
+    )
+    weight_pieces = gather_z(tie(weight_t.reshape(-1, features), mixed_full), n_tensor)
     hidden = mm(entry_two, ffn_input) + ffn_input_bias.astype(FULL)
     active, gelu_pull = jax.vjp(lambda inner: jax.nn.gelu(inner, approximate=True), hidden)
     active = active.astype(LOW)
@@ -268,59 +422,84 @@
     branch_grad = (gate_two * upstream).astype(LOW).reshape(-1, features)
     active_grad = mm(branch_grad, ffn_output, NT)
     hidden_grad = gelu_pull(active_grad)[0].astype(LOW)
-    entry_two_grad = lax.psum(mm(hidden_grad, ffn_input, NT), "tensor").reshape(latents.shape)
-    branch = lax.psum_scatter(mm(active, ffn_output), "tensor", tiled=True)
-    branch = lax.all_gather(branch, "tensor", tiled=True)
-    grad_ffn_output, grad_ffn_input = pair_sum(
-        mm(active, branch_grad, TN), mm(entry_two, hidden_grad, TN), "dp", n_dp
-    )
+    entry_two_part = mm(tie(hidden_grad, *weight_pieces), ffn_input, NT)
+    entry_two_grad = lax.psum(entry_two_part, "tensor")
+    branch_part = mm(active, ffn_output)
+
+    def beside_entry_two(places, first, second, active, branch_grad, entry_two, hidden_grad):
+        shares = [mm(active, branch_grad, TN), mm(entry_two, hidden_grad, TN)]
+        shares = [halve(x, "dp", n_dp, order) for x, order in zip(shares, orders)]
+        weight_pieces = gather_pieces([first, second], n_dp)
+        return shares, project_all(weight_pieces, places, bias_full, entry_one)
+
+    shares, (proj_full, weight_full) = as_one(
+        beside_entry_two,
+        tie(places, entry_two_part),
+        *weight_pieces,
+        active,
+        branch_grad,
+        entry_two,
+        hidden_grad,
+    )
+    entry_two_grad = tie(entry_two_grad, proj_full)
     grad_ffn_output_bias = jnp.sum(branch_grad.astype(FULL), axis=0)
     grad_ffn_input_bias = jnp.sum(hidden_grad.astype(FULL), axis=0)
 
-    proj_full, weight_full = project_all(weight_wide, bias_full[:, :, None], entry_one)
-
+
+    middle_grad, attention_grad, mixed_grad_t, middle_sums = middle_backward(
+        entry_two_grad, middle, attention, cotangent.reshape(-1, features), modulation, output_full
+    )
+    branch_part = tie(branch_part, mixed_grad_t)
+    branch = lax.psum(branch_part, "tensor")
+
+    def beside_branch(mixed_grad_t, proj_full, weight_full, shares, attention_grad, middle_grad):
+        ffn_grads = [double(x, "dp", n_dp, order) for x, order in zip(shares, orders)]
+        proj_grad = attention_backward(proj_full, mixed_grad_t, image_count)
+        own = lax.dynamic_slice_in_dim(proj_grad, place * columns, columns, 1)
+        grad_input = mm(own.reshape(-1, tokens), entry_one)
+        grad_output = mm(mixed_t.astype(LOW), attention_grad)
+        half = 2 * columns
+        grads = [grad_input[:half], jnp.concatenate([grad_input[half:], grad_output])]
+        grads = [
+            double(halve(x, "dp", n_dp, order), "dp", n_dp, order) for x, order in zip(grads, orders)
+        ]
+        latents_grad, entry_sums = entry_backward(
+            proj_grad.reshape(-1, tokens),
+            weight_full.reshape(-1, features),
+            latents.reshape(-1, features),
+            middle_grad,
+            modulation,
+        )
+        own_sums = jnp.sum(own.astype(FULL), axis=2)
+        grad_input = jnp.concatenate([grads[0], grads[1][: 3 * columns - half]])
+        grad_output = grads[1][3 * columns - half :]
+        return ffn_grads, grad_input, grad_output, latents_grad, entry_sums, own_sums
+
+    ffn_grads, grad_attn_input, grad_attn_output, latents_grad, entry_sums, own_sums = as_one(
+        beside_branch,
+        tie(mixed_grad_t, branch_part),
+        proj_full,
+        weight_full,
+        shares,
+        attention_grad,
+        middle_grad,
+    )
+    grad_ffn_output, grad_ffn_input = ffn_grads
+    grad_attn_input = grad_attn_input.reshape(3, columns, features).swapaxes(1, 2)
+    grad_attn_input_bias = jnp.stack([own_sums[0], own_sums[2]])
+    branch = tie(branch, grad_attn_output, latents_grad)
     branch = (branch + ffn_output_bias.astype(FULL)).reshape(latents.shape)
-    layer_out = (middle + gate_two * branch).astype(LOW)
+    layer_out = (middle.reshape(latents.shape) + gate_two * branch).astype(LOW)
     gate_two_grad = jnp.sum(upstream * branch, axis=1)
-
-    scale_two_grad = jnp.sum(entry_two_grad * normed_two, axis=1)
-    shift_two_grad = jnp.sum(entry_two_grad, axis=1)
-    middle_grad = upstream + norm_back(entry_two_grad * (1.0 + scale_two), normed_two, inverse_two)
-    gate_one_grad = jnp.sum(middle_grad * attention, axis=1)
-    attention_grad = (gate_one * middle_grad).astype(LOW).reshape(-1, features)
-    grad_attn_output = mm(mixed_t.astype(LOW), attention_grad)
-    grad_attn_output_bias = jnp.sum(attention_grad.astype(FULL), axis=0)
-    mixed_grad_t = mm(output_full, attention_grad, NT).astype(LOW)
-    proj_grad = attention_backward(proj_full, mixed_grad_t, image_count)
-    own = lax.dynamic_slice_in_dim(proj_grad, place * columns, columns, 1)
-    grad_attn_input = mm(own.reshape(-1, tokens), entry_one)
-    own_sums = jnp.sum(own.astype(FULL), axis=2)
-    grad_attn_input_bias = jnp.stack([own_sums[0], own_sums[2]])
-    attn_grads = jnp.concatenate([grad_attn_input, grad_attn_output])
-    half = attn_grads.shape[0] // 2
-    attn_grads = jnp.concatenate(pair_sum(attn_grads[:half], attn_grads[half:], "dp", n_dp))
-    grad_attn_input = attn_grads[: 3 * columns].reshape(3, columns, features).swapaxes(1, 2)
-    grad_attn_output = attn_grads[3 * columns :]
-
-    entry_one_grad = mm(
-        proj_grad.reshape(-1, tokens), weight_full.reshape(-1, features), TN
-    ).reshape(latents.shape)
-    scale_one_grad = jnp.sum(entry_one_grad * normed_one, axis=1)
-    shift_one_grad = jnp.sum(entry_one_grad, axis=1)
-    latents_grad = middle_grad + norm_back(
-        entry_one_grad * (1.0 + scale_one), normed_one, inverse_one
-    )
     modulation_grad = jnp.concatenate(
         [
-            shift_one_grad,
-            scale_one_grad,
-            gate_one_grad,
-            shift_two_grad,
-            scale_two_grad,
+            entry_sums.reshape(image_count, -1),
+            middle_sums[:, :3].reshape(image_count, -1),
             gate_two_grad,
         ],
         axis=-1,
     ).astype(LOW)
+    grad_attn_output_bias = jnp.sum(middle_sums[:, 3], axis=0)
     context_grad = mm(modulation_grad, modulator, NT)
     condition_grad = jax.vjp(jax.nn.silu, cond_float)[1](context_grad)[0]
 
@@ -346,7 +525,7 @@
     sums = [jnp.sum(part, axis=0) for part in every[2:]]
     return (
         layer_out,
-        latents_grad,
+        latents_grad.reshape(latents.shape),
         condition_grad,
         grad_modulator,
         grad_modulator_bias,

time: 488 us -> 351 us (0.72)
  waiting for transfers between devices: 279 us -> 91.6 us
  starting transfers between devices: 27.8 us -> 48.6 us
  other arithmetic: 40.7 us -> 60.3 us
  local copies, waits for them, and re-layouts: 44.5 us -> 59.9 us
  blocking collectives: 24.3 us -> 10.8 us
  Pallas kernels: 28.7 us -> 39.5 us
    all_gather x4 -> x0, waiting for transfers between devices: 164 us -> none  [the longest x2 91.5 us: gather_rows(): return lax.all_gather(mine.astype(FULL), ('tensor', 'dp'), tiled=True)]
    ppermute x27 -> x48, waiting for transfers between devices: 47 us -> 90.4 us  [flip(): return lax.ppermute(value, axis, [(i, i ^ mask) for i in range(count)])]
    reduce_scatter x1 -> x0, waiting for transfers between devices: 34.3 us -> none  [per_device(): branch = lax.psum_scatter(mm(active, ffn_output), 'tensor', tiled=True)]
    psum x1 -> x2, waiting for transfers between devices: 33.2 us -> 0.02 us  [the longest x1 0.02 us: per_device(): branch = lax.psum(branch_part, 'tensor')]
    ppermute x27 -> x48, starting transfers between devices: 27.6 us -> 48.4 us  [flip(): return lax.ppermute(value, axis, [(i, i ^ mask) for i in range(count)])]
    cond x0 -> x83, local copies, waits for them, and re-layouts: none -> 17.1 us
    all_gather x1 -> x0, blocking collectives: 13.6 us -> none  [per_device(): bias_full = lax.all_gather(bias_own, 'tensor', axis=1, tiled=True)]
    unnamed x121 -> x91, local copies, waits for them, and re-layouts: 19.1 us -> 9.67 us
  transfers between devices with their start and end apart: 33 -> 50, of which waited for: 20 -> 15; matrix products, arithmetic and copies ran while one was open for 17% -> 27% of each run, Pallas kernels for 4% -> 9%
where the time goes in v2:
time: 351 us; the launch traced here: 347 us
  waiting for transfers between devices  91.6 us (26%)
  other arithmetic  60.3 us (17%)
  local copies, waits for them, and re-layouts  59.9 us (17%)
  starting transfers between devices  48.6 us (14%)
  Pallas kernels  39.5 us (11%)
  matrix products  21.5 us (6%)
  between operations  14.6 us (4%)
  blocking collectives  10.8 us (3%)
    ppermute x48, waiting for transfers between devices, flip(): return lax.ppermute(value, axis, [(i, i ^ mask) for i in range(count)])  90.4 us
    ppermute x48, starting transfers between devices, flip(): return lax.ppermute(value, axis, [(i, i ^ mask) for i in range(count)])  48.4 us
    dot_general x11, matrix products, mm(): return lax.dot_general(left, right, dims, preferred_element_type=FULL)  21.5 us
    cond x83, local copies, waits for them, and re-layouts  17.1 us
    pallas_call x1, Pallas kernels, attention_backward(): pl.pallas_call(functools.partial(backward_kernel, step), out_shape=jax.Sh...  12.3 us
    add x12, other arithmetic, halve(): value = kept + flip(away, axis, count, mask)  11.5 us
    all_gather x1, blocking collectives, per_device(): spread = lax.optimization_barrier(lax.all_gather(small, 'dp'))  10.8 us
    unnamed x91, local copies, waits for them, and re-layouts  9.67 us
  transfers between devices with their start and end apart: 50, of which 15 were waited for; matrix products, arithmetic and copies ran while one was open for 27% of the time, Pallas kernels for 9%

profile of v2, /device:TPU:0, one launch (start us, length us, event | category | flops | bytes accessed | tf_op | source)
XLA Modules:
  0.0 347.3 jit_solution(162640085244491164)
XLA Ops:
  10.6 4.0 %collective-permute-start.31 = (f32[90,128]{1,0:T(8,128)}, f32[90,128]{1,0:T(8,128)}, u32[]{:S(2)}, u32[]{:S(2)}) collective-permute-start(f32[90,128]{1,0:T(8,128)} %maximum_bitcast_fusion.4), channel_id=1, source_target_pairs={{0,2},{1,3},{2,0},{3,1},{4,6},{5,7},{6,4},{7,5},{8,10},{9,11},{10,... | collective-permute-start | bytes 138248 | tf_op jit(solution)/shard_map/ppermute | solution.py:303
  17.7 2.7 collective-permute-start.39
  39.8 3.9 %attention_forward.1 = f32[192,512]{1,0:T(8,128)S(1)} custom-call(bf16[512,768]{1,0:T(8,128)(2,1)} %bitcast.96, bf16[3,192,768]{2,1,0:T(8,128)(2,1)S(1)} %bitcast.89, f32[3,192,1]{2,1,0:T(8,128)S(1)} %copy-done.10), custom_call_target="tpu_custom_call" | custom-call | tf_op jit(solution)/shard_map/attention_forward/pallas_call | solution.py:63
  43.7 3.0 collective-permute-start.35
  58.4 11.9 %collective-permute-done.33 = f32[192,512]{1,0:T(8,128)S(1)} collective-permute-done((f32[192,512]{1,0:T(8,128)S(1)}, f32[192,512]{1,0:T(8,128)S(1)}, u32[]{:S(2)}, u32[]{:S(2)}) %collective-permute-start.33) | collective-permute-done | bytes 393248 | tf_op jit(solution)/shard_map/ppermute | solution.py:303
  71.1 7.5 %collective-permute-done.34 = f32[192,512]{1,0:T(8,128)S(1)} collective-permute-done((f32[192,512]{1,0:T(8,128)S(1)}, f32[192,512]{1,0:T(8,128)S(1)}, u32[]{:S(2)}, u32[]{:S(2)}) %collective-permute-start.34) | collective-permute-done | bytes 393248 | tf_op jit(solution)/shard_map/ppermute | solution.py:303
  84.0 2.9 collective-permute-start.45
  88.3 13.4 %collective-permute-done.45 = f32[72,768]{1,0:T(8,128)S(1)} collective-permute-done((f32[72,768]{1,0:T(8,128)S(1)}, f32[72,768]{1,0:T(8,128)S(1)}, u32[]{:S(2)}, u32[]{:S(2)}) %collective-permute-start.45) | collective-permute-done | bytes 221216 | tf_op jit(solution)/shard_map/ppermute | solution.py:303
  103.4 3.9 %join_heads.1 = (f32[512,768]{1,0:T(8,128)S(1)}, f32[512,768]{1,0:T(8,128)}, bf16[512,768]{1,0:T(8,128)(2,1)S(1)}, bf16[768,768]{1,0:T(8,128)(2,1)S(1)}) custom-call(s32[5]{0:T(128)S(1)} %copy-done.71, f32[768,512]{1,0:T(8,128)} %bitcast.18.mixed_ref.refs_1_, bf16[1,768]{1,0:T(2,128)(2,1)S(1)} %broadcast_in_dim.49.bias_ref, bf16[512,768]{1,0:T(8,128)(2,1)S(1)} %bitcast.94, ...), custom_call_target="tpu_custom_call" | custom-call | tf_op jit(solution)/shard_map/join_heads/pallas_call | solution.py:143
  107.4 2.6 convert_reduce_fusion.2
  111.2 3.5 fusion.45.refs_1_
  115.8 84.1 %conditional.2 = (f32[96,768]{1,0:T(8,128)}, f32[96,768]{1,0:T(8,128)}, bf16[3,768,512]{2,1,0:T(8,128)(2,1)}, bf16[3,768,768]{2,1,0:T(8,128)(2,1)}) conditional(s32[]{:T(128)} %convert_element_type.95, () %tuple.30, (bf16[512,768]{1,0:T(8,128)(2,1)}, bf16[512,768]{1,0:T(8,128)(2,1)}, bf16[512,768]{1,0:T(8,128)(2,1)}, bf16[512,768]{1,0:T(8,128)(2,1)}, ...), branch_computations={%region_3.4_spmd, %region_4.5_spmd} | conditional | flops 1209434112 | bytes 143402848 | solution.py:355
  115.8 2.2 fusion.40
  125.5 7.7 %collective-permute-done.8 = f32[1,2,72,768]{3,2,1,0:T(8,128)} collective-permute-done((f32[1,2,72,768]{3,2,1,0:T(8,128)}, f32[1,2,72,768]{3,2,1,0:T(8,128)}, u32[]{:S(2)}, u32[]{:S(2)}) %collective-permute-start.8) | collective-permute-done | bytes 442400 | tf_op jit(solution)/shard_map/cond/branch_1_fun/ppermute | solution.py:303
  147.6 9.5 %collective-permute-done.9 = f32[2,2,72,768]{3,2,1,0:T(8,128)S(1)} collective-permute-done((f32[2,2,72,768]{3,2,1,0:T(8,128)S(1)}, f32[2,2,72,768]{3,2,1,0:T(8,128)S(1)}, u32[]{:S(2)}, u32[]{:S(2)}) %collective-permute-start.9) | collective-permute-done | bytes 884768 | tf_op jit(solution)/shard_map/cond/branch_1_fun/ppermute | solution.py:303
  164.5 3.7 %collective-permute-done.1 = f32[192,768]{1,0:T(8,128)} collective-permute-done((f32[192,768]{1,0:T(8,128)}, f32[192,768]{1,0:T(8,128)}, u32[]{:S(2)}, u32[]{:S(2)}) %collective-permute-start.1) | collective-permute-done | bytes 589856 | tf_op jit(solution)/shard_map/cond/branch_1_fun/ppermute | solution.py:303
  171.9 7.6 %collective-permute-done.4 = f32[192,768]{1,0:T(8,128)} collective-permute-done((f32[192,768]{1,0:T(8,128)}, f32[192,768]{1,0:T(8,128)}, u32[]{:S(2)}, u32[]{:S(2)}) %collective-permute-start.4) | collective-permute-done | bytes 589856 | tf_op jit(solution)/shard_map/cond/branch_1_fun/ppermute | solution.py:303
  186.8 2.3 collective-permute-done.5
  190.9 9.1 %project_all.1 = (bf16[3,768,512]{2,1,0:T(8,128)(2,1)}, bf16[3,768,768]{2,1,0:T(8,128)(2,1)}) custom-call(s32[5]{0:T(128)S(1)} %get-tuple-element.50.place_ref, f32[3,768,1]{2,1,0:T(8,128)S(1)} %copy-done.8, bf16[512,768]{1,0:T(8,128)(2,1)S(1)} %get-tuple-element.52.entry_ref, f32[4,2,72,768]{3,2,1,0:T(8,128)} %constant_dynamic-update-slice_fusion.refs_0_, ...), custom_call_target="tpu_custom_call" | custom-call | tf_op jit(solution)/shard_map/cond/branch_1_fun/project_all/pallas_call | solution.py:187
  199.9 3.5 %fusion.43.refs_0_ = f32[512,768]{1,0:T(8,128)} fusion(bf16[512,768]{1,0:T(8,128)(2,1)} %get-tuple-element.163, bf16[768,768]{1,0:T(8,128)(2,1)} %param.27), kind=kOutput, calls=%fused_computation.167 | convolution fusion | flops 603979776 | bytes 3538944 | tf_op jit(solution)/shard_map/dot_general | solution.py:21
  207.6 4.3 %middle_backward.1 = (f32[512,768]{1,0:T(8,128)}, bf16[512,768]{1,0:T(8,128)(2,1)}, bf16[768,512]{1,0:T(8,128)(2,1)}, f32[2,4,768]{2,1,0:T(4,128)S(1)}) custom-call(f32[512,768]{1,0:T(8,128)S(1)} %copy-done.7, f32[512,768]{1,0:T(8,128)S(1)} %copy-done.5, f32[512,768]{1,0:T(8,128)} %copy-done.9, bf16[512,768]{1,0:T(8,128)(2,1)S(1)} %bitcast.91, ...), custom_call_target="tpu_custom_call" | custom-call | tf_op jit(solution)/shard_map/middle_backward/pallas_call | solution.py:224
  213.0 93.7 %conditional.3 = (f32[768,768]{1,0:T(8,128)}, f32[768,768]{1,0:T(8,128)}, f32[576,768]{1,0:T(8,128)}, f32[192,768]{1,0:T(8,128)S(1)}, f32[512,768]{1,0:T(8,128)}...) conditional(s32[]{:T(128)} %convert_element_type.95, () %tuple.32, ...), branch_computations={%region_6.7_spmd, %region_7.9_spmd} | conditional | flops 613293568 | bytes 184343488 | solution.py:355
  215.0 12.3 %attention_backward.1 = bf16[3,768,512]{2,1,0:T(8,128)(2,1)S(1)} custom-call(bf16[3,768,512]{2,1,0:T(8,128)(2,1)} %get-tuple-element.59.proj_ref, bf16[768,512]{1,0:T(8,128)(2,1)} %get-tuple-element.60.grad_ref), custom_call_target="tpu_custom_call" | custom-call | tf_op jit(solution)/shard_map/cond/branch_1_fun/attention_backward/pallas_call | solution.py:91
  247.7 16.1 %collective-permute-done.25 = f32[96,768]{1,0:T(8,128)S(1)} collective-permute-done((f32[96,768]{1,0:T(8,128)S(1)}, f32[96,768]{1,0:T(8,128)S(1)}, u32[]{:S(2)}, u32[]{:S(2)}) %collective-permute-start.25) | collective-permute-done | bytes 294944 | tf_op jit(solution)/shard_map/cond/branch_1_fun/ppermute | solution.py:303
  271.5 2.9 collective-permute-done.27
  277.5 4.9 %collective-permute-done.28 = f32[96,768]{1,0:T(8,128)S(1)} collective-permute-done((f32[96,768]{1,0:T(8,128)S(1)}, f32[96,768]{1,0:T(8,128)S(1)}, u32[]{:S(2)}, u32[]{:S(2)}) %collective-permute-start.28) | collective-permute-done | bytes 294944 | tf_op jit(solution)/shard_map/cond/branch_1_fun/ppermute | solution.py:303
  287.4 6.0 %entry_backward.1 = (f32[512,768]{1,0:T(8,128)}, f32[2,2,768]{2,1,0:T(2,128)S(1)}) custom-call(bf16[2304,512]{1,0:T(8,128)(2,1)S(1)} %bitcast.88, bf16[2304,768]{1,0:T(8,128)(2,1)} %bitcast.2.weight_ref, bf16[512,768]{1,0:T(8,128)(2,1)S(1)} %bitcast.95, f32[512,768]{1,0:T(8,128)} %get-tuple-element.67.middle_grad_ref, f32[2,6,768]{2,1,0:T(8,128)S(1)} %get-tuple-element.68.mod_ref), custom_call_target="tpu_custom_call" | custom-call | tf_op jit(solution)/shard_map/cond/branch_1_fun/entry_backward/pallas_call | solution.py:266
  293.4 2.7 copy.88
  307.5 2.8 fusion.12
  311.6 10.8 %all-gather = f32[98304]{0:T(1024)} all-gather(f32[12288]{0:T(1024)S(1)} %constant_dynamic-update-slice_fusion.6), channel_id=2, replica_groups=mesh['dp'=8,'tensor'=4] {'dp'}, dimensions={0}, use_global_device_ids=true | all-gather | bytes 442368 | tf_op jit(solution)/shard_map/all_gather | solution.py:518
  335.6 2.5 add_convert_fusion
  338.0 2.4 fusion.46
  (390 shorter events, 159.5 us)
Async XLA Ops:
  10.6 19.5 %collective-permute-start.31 = (f32[90,128]{1,0:T(8,128)}, f32[90,128]{1,0:T(8,128)}, u32[]{:S(2)}, u32[]{:S(2)}) collective-permute-start(f32[90,128]{1,0:T(8,128)} %maximum_bitcast_fusion.4), channel_id=1, source_target_pairs={{0,2},{1,3},{2,0},{3,1},{4,6},{5,7},{6,4},{7,5},{8,10},{9,11},{10,... | collective-permute-start | bytes 138248 | tf_op jit(solution)/shard_map/ppermute | solution.py:303
  14.6 16.4 %collective-permute-start.32 = (f32[90,128]{1,0:T(8,128)}, f32[90,128]{1,0:T(8,128)}, u32[]{:S(2)}, u32[]{:S(2)}) collective-permute-start(f32[90,128]{1,0:T(8,128)} %maximum_bitcast_fusion.4), channel_id=1, source_target_pairs={{0,3},{1,2},{2,1},{3,0},{4,7},{5,6},{6,5},{7,4},{8,11},{9,10},{10,... | collective-permute-start | bytes 138248 | tf_op jit(solution)/shard_map/ppermute | solution.py:303
  17.7 29.0 %collective-permute-start.39 = (f32[24,768]{1,0:T(8,128)}, f32[24,768]{1,0:T(8,128)}, u32[]{:S(2)}, u32[]{:S(2)}) collective-permute-start(f32[24,768]{1,0:T(8,128)} %get-tuple-element.167), channel_id=1, source_target_pairs={{0,2},{1,3},{2,0},{3,1},{4,6},{5,7},{6,4},{7,5},{8,10},{9,11},{10,... | collective-permute-start | bytes 221192 | tf_op jit(solution)/shard_map/ppermute | solution.py:303
  20.4 30.3 %collective-permute-start.36 = (f32[24,768]{1,0:T(8,128)}, f32[24,768]{1,0:T(8,128)}, u32[]{:S(2)}, u32[]{:S(2)}) collective-permute-start(f32[24,768]{1,0:T(8,128)} %get-tuple-element.167), channel_id=1, source_target_pairs={{0,1},{1,0},{2,3},{3,2},{4,5},{5,4},{6,7},{7,6},{8,9},{9,8},{10,11... | collective-permute-start | bytes 221192 | tf_op jit(solution)/shard_map/ppermute | solution.py:303
  30.1 18.1 %collective-permute-start.40 = (f32[24,768]{1,0:T(8,128)}, f32[24,768]{1,0:T(8,128)}, u32[]{:S(2)}, u32[]{:S(2)}) collective-permute-start(f32[24,768]{1,0:T(8,128)} %get-tuple-element.167), channel_id=1, source_target_pairs={{0,3},{1,2},{2,1},{3,0},{4,7},{5,6},{6,5},{7,4},{8,11},{9,10},{10,... | collective-permute-start | bytes 221192 | tf_op jit(solution)/shard_map/ppermute | solution.py:303
  43.7 35.6 %collective-permute-start.35 = (f32[192,512]{1,0:T(8,128)S(1)}, f32[192,512]{1,0:T(8,128)S(1)}, u32[]{:S(2)}, u32[]{:S(2)}) collective-permute-start(f32[192,512]{1,0:T(8,128)S(1)} %attention_forward.1), channel_id=1, source_target_pairs={{0,3},{1,2},{2,1},{3,0},{4,7},{5,6},{6,5},{7,4},{8,11},{9,10},{10,... | collective-permute-start | bytes 1179656 | tf_op jit(solution)/shard_map/ppermute | solution.py:303
  46.7 31.9 %collective-permute-start.34 = (f32[192,512]{1,0:T(8,128)S(1)}, f32[192,512]{1,0:T(8,128)S(1)}, u32[]{:S(2)}, u32[]{:S(2)}) collective-permute-start(f32[192,512]{1,0:T(8,128)S(1)} %attention_forward.1), channel_id=1, source_target_pairs={{0,2},{1,3},{2,0},{3,1},{4,6},{5,7},{6,4},{7,5},{8,10},{9,11},{10,... | collective-permute-start | bytes 1179656 | tf_op jit(solution)/shard_map/ppermute | solution.py:303
  46.7 23.6 %collective-permute-start.33 = (f32[192,512]{1,0:T(8,128)S(1)}, f32[192,512]{1,0:T(8,128)S(1)}, u32[]{:S(2)}, u32[]{:S(2)}) collective-permute-start(f32[192,512]{1,0:T(8,128)S(1)} %attention_forward.1), channel_id=1, source_target_pairs={{0,1},{1,0},{2,3},{3,2},{4,5},{5,4},{6,7},{7,6},{8,9},{9,8},{10,11... | collective-permute-start | bytes 1179656 | tf_op jit(solution)/shard_map/ppermute | solution.py:303
  56.0 25.3 %collective-permute-start.42 = (f32[2,2,24,768]{3,2,1,0:T(8,128)}, f32[2,2,24,768]{3,2,1,0:T(8,128)}, u32[]{:S(2)}, u32[]{:S(2)}) collective-permute-start(f32[2,2,24,768]{3,2,1,0:T(8,128)} %pad_maximum_fusion.16), channel_id=1, source_target_pairs={{0,8},{4,12},{8,0},{12,4},{16,24},{20,28},{24,16},{28,20},{1,9},{5... | collective-permute-start | bytes 884744 | tf_op jit(solution)/shard_map/ppermute | solution.py:303
  57.8 22.4 %collective-permute-start.38 = (f32[2,2,24,768]{3,2,1,0:T(8,128)S(1)}, f32[2,2,24,768]{3,2,1,0:T(8,128)}, u32[]{:S(2)}, u32[]{:S(2)}) collective-permute-start(f32[2,2,24,768]{3,2,1,0:T(8,128)S(1)} %pad_maximum_fusion.15), channel_id=1, source_target_pairs={{0,16},{4,20},{8,24},{12,28},{16,0},{20,4},{24,8},{28,12},{1,17},{... | collective-permute-start | bytes 884744 | tf_op jit(solution)/shard_map/ppermute | solution.py:303
  81.3 22.1 %collective-permute-start.43 = (f32[4,2,24,768]{3,2,1,0:T(8,128)S(1)}, f32[4,2,24,768]{3,2,1,0:T(8,128)S(1)}, u32[]{:S(2)}, u32[]{:S(2)}) collective-permute-start(f32[4,2,24,768]{3,2,1,0:T(8,128)S(1)} %pad_maximum_fusion.13.refs_0_), channel_id=1, source_target_pairs={{0,4},{4,0},{8,12},{12,8},{16,20},{20,16},{24,28},{28,24},{1,5},{5... | collective-permute-start | bytes 1769480 | tf_op jit(solution)/shard_map/ppermute | solution.py:303
  82.4 20.9 %collective-permute-start.44 = (f32[4,2,24,768]{3,2,1,0:T(8,128)S(1)}, f32[4,2,24,768]{3,2,1,0:T(8,128)S(1)}, u32[]{:S(2)}, u32[]{:S(2)}) collective-permute-start(f32[4,2,24,768]{3,2,1,0:T(8,128)S(1)} %pad_maximum_fusion.14.refs_1_), channel_id=1, source_target_pairs={{0,4},{4,0},{8,12},{12,8},{16,20},{20,16},{24,28},{28,24},{1,5},{5... | collective-permute-start | bytes 1769480 | tf_op jit(solution)/shard_map/ppermute | solution.py:303
  83.9 18.7 %collective-permute-start.46 = (f32[72,768]{1,0:T(8,128)S(1)}, f32[72,768]{1,0:T(8,128)S(1)}, u32[]{:S(2)}, u32[]{:S(2)}) collective-permute-start(f32[72,768]{1,0:T(8,128)S(1)} %get-tuple-element.165), channel_id=1, source_target_pairs={{0,2},{1,3},{2,0},{3,1},{4,6},{5,7},{6,4},{7,5},{8,10},{9,11},{10,... | collective-permute-start | bytes 663560 | tf_op jit(solution)/shard_map/ppermute | solution.py:303
  84.0 17.8 %collective-permute-start.45 = (f32[72,768]{1,0:T(8,128)S(1)}, f32[72,768]{1,0:T(8,128)S(1)}, u32[]{:S(2)}, u32[]{:S(2)}) collective-permute-start(f32[72,768]{1,0:T(8,128)S(1)} %get-tuple-element.165), channel_id=1, source_target_pairs={{0,1},{1,0},{2,3},{3,2},{4,5},{5,4},{6,7},{7,6},{8,9},{9,8},{10,11... | collective-permute-start | bytes 663560 | tf_op jit(solution)/shard_map/ppermute | solution.py:303
  114.7 88.8 %all-reduce.3.cloned.1.call-start = ((), (), s32[]{:S(2)}) async-start(), calls=%async_computation | async-start | bytes 3145728 | tf_op jit(solution)/shard_map/psum | solution.py:426
  119.1 24.6 %collective-permute-start = (f32[384,768]{1,0:T(8,128)}, f32[384,768]{1,0:T(8,128)}, u32[]{:S(2)}, u32[]{:S(2)}) collective-permute-start(f32[384,768]{1,0:T(8,128)} %constant_dynamic-slice_fusion.5), channel_id=1, source_target_pairs={{0,4},{4,0},{8,12},{12,8},{16,20},{20,16},{24,28},{28,24},{1,5},{5... | collective-permute-start | bytes 3538952 | tf_op jit(solution)/shard_map/cond/branch_1_fun/ppermute | solution.py:303
  125.5 34.2 %collective-permute-start.3 = (f32[384,768]{1,0:T(8,128)}, f32[384,768]{1,0:T(8,128)}, u32[]{:S(2)}, u32[]{:S(2)}) collective-permute-start(f32[384,768]{1,0:T(8,128)} %constant_dynamic-slice_fusion.2), channel_id=1, source_target_pairs={{0,4},{4,0},{8,12},{12,8},{16,20},{20,16},{24,28},{28,24},{1,5},{5... | collective-permute-start | bytes 3538952 | tf_op jit(solution)/shard_map/cond/branch_1_fun/ppermute | solution.py:303
  134.4 22.7 %collective-permute-start.9 = (f32[2,2,72,768]{3,2,1,0:T(8,128)S(1)}, f32[2,2,72,768]{3,2,1,0:T(8,128)S(1)}, u32[]{:S(2)}, u32[]{:S(2)}) collective-permute-start(f32[2,2,72,768]{3,2,1,0:T(8,128)S(1)} %pad_maximum_fusion.1), channel_id=1, source_target_pairs={{0,8},{4,12},{8,0},{12,4},{16,24},{20,28},{24,16},{28,20},{1,9},{5... | collective-permute-start | bytes 2654216 | tf_op jit(solution)/shard_map/cond/branch_1_fun/ppermute | solution.py:303
  136.3 21.9 %collective-permute-start.7 = (f32[2,2,72,768]{3,2,1,0:T(8,128)S(1)}, f32[2,2,72,768]{3,2,1,0:T(8,128)S(1)}, u32[]{:S(2)}, u32[]{:S(2)}) collective-permute-start(f32[2,2,72,768]{3,2,1,0:T(8,128)S(1)} %pad_maximum_fusion), channel_id=1, source_target_pairs={{0,16},{4,20},{8,24},{12,28},{16,0},{20,4},{24,8},{28,12},{1,17},{... | collective-permute-start | bytes 2654216 | tf_op jit(solution)/shard_map/cond/branch_1_fun/ppermute | solution.py:303
  146.1 22.2 %collective-permute-start.1 = (f32[192,768]{1,0:T(8,128)}, f32[192,768]{1,0:T(8,128)}, u32[]{:S(2)}, u32[]{:S(2)}) collective-permute-start(f32[192,768]{1,0:T(8,128)} %constant_dynamic-slice_fusion.4), channel_id=1, source_target_pairs={{0,8},{4,12},{8,0},{12,4},{16,24},{20,28},{24,16},{28,20},{1,9},{5... | collective-permute-start | bytes 1769480 | tf_op jit(solution)/shard_map/cond/branch_1_fun/ppermute | solution.py:303
  158.2 32.7 %collective-permute-start.11 = (f32[4,2,72,768]{3,2,1,0:T(8,128)}, f32[4,2,72,768]{3,2,1,0:T(8,128)}, u32[]{:S(2)}, u32[]{:S(2)}) collective-permute-start(f32[4,2,72,768]{3,2,1,0:T(8,128)} %constant_dynamic-update-slice_fusion.3.refs_1_), channel_id=1, source_target_pairs={{0,4},{4,0},{8,12},{12,8},{16,20},{20,16},{24,28},{28,24},{1,5},{5... | collective-permute-start | bytes 5308424 | tf_op jit(solution)/shard_map/cond/branch_1_fun/ppermute | solution.py:303
  159.2 31.7 %collective-permute-start.10 = (f32[4,2,72,768]{3,2,1,0:T(8,128)}, f32[4,2,72,768]{3,2,1,0:T(8,128)}, u32[]{:S(2)}, u32[]{:S(2)}) collective-permute-start(f32[4,2,72,768]{3,2,1,0:T(8,128)} %constant_dynamic-update-slice_fusion.refs_0_), channel_id=1, source_target_pairs={{0,4},{4,0},{8,12},{12,8},{16,20},{20,16},{24,28},{28,24},{1,5},{5... | collective-permute-start | bytes 5308424 | tf_op jit(solution)/shard_map/cond/branch_1_fun/ppermute | solution.py:303
  163.0 16.5 %collective-permute-start.4 = (f32[192,768]{1,0:T(8,128)}, f32[192,768]{1,0:T(8,128)}, u32[]{:S(2)}, u32[]{:S(2)}) collective-permute-start(f32[192,768]{1,0:T(8,128)} %constant_dynamic-slice_fusion.1), channel_id=1, source_target_pairs={{0,16},{4,20},{8,24},{12,28},{16,0},{20,4},{24,8},{28,12},{1,17},{... | collective-permute-start | bytes 1769480 | tf_op jit(solution)/shard_map/cond/branch_1_fun/ppermute | solution.py:303
  211.8 95.0 %all-reduce.5.cloned.1.call-start = ((), (), s32[]{:S(2)}) async-start(), calls=%async_computation.1 | async-start | bytes 3145728 | tf_op jit(solution)/shard_map/psum | solution.py:453
  213.0 25.6 %collective-permute-start.12 = (f32[96,768]{1,0:T(8,128)}, f32[96,768]{1,0:T(8,128)}, u32[]{:S(2)}, u32[]{:S(2)}) collective-permute-start(f32[96,768]{1,0:T(8,128)} %get-tuple-element.57), channel_id=1, source_target_pairs={{0,16},{4,20},{8,24},{12,28},{16,0},{20,4},{24,8},{28,12},{1,17},{... | collective-permute-start | bytes 884744 | tf_op jit(solution)/shard_map/cond/branch_1_fun/ppermute | solution.py:303
  214.5 26.8 %collective-permute-start.15 = (f32[96,768]{1,0:T(8,128)}, f32[96,768]{1,0:T(8,128)}, u32[]{:S(2)}, u32[]{:S(2)}) collective-permute-start(f32[96,768]{1,0:T(8,128)} %get-tuple-element.58), channel_id=1, source_target_pairs={{0,8},{4,12},{8,0},{12,4},{16,24},{20,28},{24,16},{28,20},{1,9},{5... | collective-permute-start | bytes 884744 | tf_op jit(solution)/shard_map/cond/branch_1_fun/ppermute | solution.py:303
  239.8 25.4 %collective-permute-start.13 = (f32[192,768]{1,0:T(8,128)S(1)}, f32[192,768]{1,0:T(8,128)S(1)}, u32[]{:S(2)}, u32[]{:S(2)}) collective-permute-start(f32[192,768]{1,0:T(8,128)S(1)} %pad_maximum_fusion.7), channel_id=1, source_target_pairs={{0,8},{4,12},{8,0},{12,4},{16,24},{20,28},{24,16},{28,20},{1,9},{5... | collective-permute-start | bytes 1769480 | tf_op jit(solution)/shard_map/cond/branch_1_fun/ppermute | solution.py:303
  242.5 23.9 %collective-permute-start.16 = (f32[192,768]{1,0:T(8,128)S(1)}, f32[192,768]{1,0:T(8,128)S(1)}, u32[]{:S(2)}, u32[]{:S(2)}) collective-permute-start(f32[192,768]{1,0:T(8,128)S(1)} %pad_maximum_fusion.8), channel_id=1, source_target_pairs={{0,16},{4,20},{8,24},{12,28},{16,0},{20,4},{24,8},{28,12},{1,17},{... | collective-permute-start | bytes 1769480 | tf_op jit(solution)/shard_map/cond/branch_1_fun/ppermute | solution.py:303
  244.3 19.5 %collective-permute-start.25 = (f32[96,768]{1,0:T(8,128)S(1)}, f32[96,768]{1,0:T(8,128)S(1)}, u32[]{:S(2)}, u32[]{:S(2)}) collective-permute-start(f32[96,768]{1,0:T(8,128)S(1)} %constant_dynamic-slice_fusion.7), channel_id=1, source_target_pairs={{0,16},{4,20},{8,24},{12,28},{16,0},{20,4},{24,8},{28,12},{1,17},{... | collective-permute-start | bytes 884744 | tf_op jit(solution)/shard_map/cond/branch_1_fun/ppermute | solution.py:303
  247.1 17.4 %collective-permute-start.19 = (f32[96,768]{1,0:T(8,128)S(1)}, f32[96,768]{1,0:T(8,128)S(1)}, u32[]{:S(2)}, u32[]{:S(2)}) collective-permute-start(f32[96,768]{1,0:T(8,128)S(1)} %constant_dynamic-slice_fusion.9), channel_id=1, source_target_pairs={{0,8},{4,12},{8,0},{12,4},{16,24},{20,28},{24,16},{28,20},{1,9},{5... | collective-permute-start | bytes 884744 | tf_op jit(solution)/shard_map/cond/branch_1_fun/ppermute | solution.py:303
  266.4 34.3 %collective-permute-start.14 = (f32[384,768]{1,0:T(8,128)}, f32[384,768]{1,0:T(8,128)}, u32[]{:S(2)}, u32[]{:S(2)}) collective-permute-start(f32[384,768]{1,0:T(8,128)} %pad_maximum_fusion.5), channel_id=1, source_target_pairs={{0,4},{4,0},{8,12},{12,8},{16,20},{20,16},{24,28},{28,24},{1,5},{5... | collective-permute-start | bytes 3538952 | tf_op jit(solution)/shard_map/cond/branch_1_fun/ppermute | solution.py:303
  267.8 32.9 %collective-permute-start.17 = (f32[384,768]{1,0:T(8,128)}, f32[384,768]{1,0:T(8,128)}, u32[]{:S(2)}, u32[]{:S(2)}) collective-permute-start(f32[384,768]{1,0:T(8,128)} %pad_maximum_fusion.6), channel_id=1, source_target_pairs={{0,4},{4,0},{8,12},{12,8},{16,20},{20,16},{24,28},{28,24},{1,5},{5... | collective-permute-start | bytes 3538952 | tf_op jit(solution)/shard_map/cond/branch_1_fun/ppermute | solution.py:303
  (97 other events, 573.7 us)
Sparse Core Ops, SparseCore 0:
  118.4 71.0 all-reduce.2
  215.1 70.1 all-reduce.4

commit v3 on v1

v3 whole, which is shorter than its diff:
```python
import functools

import jax
import jax.numpy as jnp
from jax import lax
from jax.experimental import pallas as pl
from jax.experimental.pallas import tpu as pltpu
from jax.sharding import PartitionSpec as P

HEAD = 64
epsilon = 1e-06
SCALE = HEAD ** (-0.5)
LOW = jnp.bfloat16
FULL = jnp.float32
NN = (((1,), (0,)), ((), ()))
NT = (((1,), (1,)), ((), ()))
TN = (((0,), (0,)), ((), ()))
GROUP = 8
CHIPS = 4


def mm(left, right, dims=NN):
    return lax.dot_general(left, right, dims, preferred_element_type=FULL)


def norm_parts(values):
    centre = values - jnp.mean(values, axis=-1, keepdims=True)
    inverse = lax.rsqrt(jnp.mean(centre * centre, axis=-1, keepdims=True) + epsilon)
    return (centre * inverse, inverse)


def norm_back(grad, normed, inverse):
    return (
        grad
        - jnp.mean(grad, axis=-1, keepdims=True)
        - normed * jnp.mean(grad * normed, axis=-1, keepdims=True)
    ) * inverse


def shape(dims, dtype=FULL):
    return jax.ShapeDtypeStruct(dims, dtype)


def rows_at(start, count, step=8):
    return pl.ds(pl.multiple_of(start, step), count)


def call(kernel, name, out_shape, operands, smem=0, grid=None, specs=None, out_specs=None, scratch=()):
    vmem = pl.BlockSpec(memory_space=pltpu.VMEM)
    in_specs = [pl.BlockSpec(memory_space=pltpu.SMEM)] * smem
    in_specs += [vmem] * (len(operands) - smem) if specs is None else specs
    if out_specs is None:
        out_specs = jax.tree.map(lambda _: vmem, out_shape)
    extra = {} if grid is None else {"grid": grid}
    return pl.pallas_call(
        kernel,
        out_shape=out_shape,
        in_specs=in_specs,
        out_specs=out_specs,
        scratch_shapes=list(scratch),
        compiler_params=pltpu.CompilerParams(vmem_limit_bytes=48 * 2**20),
        name=name,
        **extra,
    )(*operands)


def bias_columns(row, count):
    return mm(row, jnp.ones((1, count), LOW), TN)


def softmax_t(keys_t, query_t):
    scores = mm(keys_t, query_t, TN) * SCALE
    shifted = jnp.exp(scores - jnp.max(scores, axis=0, keepdims=True))
    return shifted * (1.0 / jnp.sum(shifted, axis=0, keepdims=True))


def start_kernel(
    part0, part1, part2, part3, mod_bias, latents, weight, bias,
    mixed_ref, entry_ref, mod_ref, bias_ref,
):
    images, _, width = mod_ref.shape
    columns = weight.shape[1]
    positions = latents.shape[0] // images
    shared = (part0[...] + part1[...]) + (part2[...] + part3[...])
    for j in range(3):
        bias_ref[j : j + 1, :] = shared[images : images + 1, j * width : (j + 1) * width]
    modulation = shared[:images] + mod_bias[...].astype(FULL)
    for p in range(6):
        for g in range(images):
            mod_ref[g, p : p + 1, :] = modulation[g : g + 1, p * width : (p + 1) * width]
    offsets = [bias_columns(bias[j : j + 1, :], positions) for j in range(3)]
    for g in range(images):
        token = slice(g * positions, (g + 1) * positions)
        normed = norm_parts(latents[token, :].astype(FULL))[0]
        entry = (normed * (1.0 + mod_ref[g, 1:2, :]) + mod_ref[g, 0:1, :]).astype(LOW)
        entry_ref[token, :] = entry
        query, keys, values = (
            (mm(weight[j], entry, NT) + offsets[j]).astype(LOW) for j in range(3)
        )
        for h in range(columns // HEAD):
            row = slice(h * HEAD, (h + 1) * HEAD)
            probs = softmax_t(keys[row], query[row])
            mixed_ref[row, token] = mm(values[row], probs.astype(LOW)).astype(LOW).astype(FULL)


def probs_kernel(proj_ref, out_ref):
    for h in range(out_ref.shape[1]):
        row = slice(h * HEAD, (h + 1) * HEAD)
        out_ref[0, h] = softmax_t(proj_ref[1, row, :], proj_ref[0, row, :])


def all_probs(proj_t, images):
    _, width, tokens = proj_t.shape
    positions = tokens // images
    heads = width // HEAD
    step = 4 if heads % 4 == 0 else heads
    return call(
        probs_kernel,
        "all_probs",
        shape((images, heads, positions, positions)),
        (proj_t,),
        grid=(images, heads // step),
        specs=[pl.BlockSpec((2, step * HEAD, positions), lambda g, h: (0, h, g))],
        out_specs=pl.BlockSpec((1, step, positions, positions), lambda g, h: (g, h, 0, 0)),
    )


def backward_kernel(probs_ref, proj_ref, grad_ref, out_ref):
    for h in range(probs_ref.shape[1]):
        row = slice(h * HEAD, (h + 1) * HEAD)
        query, keys, values = proj_ref[0, row, :], proj_ref[1, row, :], proj_ref[2, row, :]
        grad = grad_ref[row, :]
        probs = probs_ref[0, h]
        probs_grad = mm(values, grad, TN)
        weighted = probs * probs_grad
        scores_grad = (weighted - probs * jnp.sum(weighted, axis=0, keepdims=True)).astype(LOW)
        out_ref[0, row, :] = (mm(keys, scores_grad) * SCALE).astype(LOW)
        out_ref[1, row, :] = (mm(query, scores_grad, NT) * SCALE).astype(LOW)
        out_ref[2, row, :] = mm(grad, probs.astype(LOW), NT).astype(LOW)


def attention_backward(probs, proj_t, grad_t):
    images, heads, positions, _ = probs.shape
    width, tokens = grad_t.shape
    step = 4 if heads % 4 == 0 else heads
    rows = step * HEAD
    block = pl.BlockSpec((3, rows, positions), lambda g, h: (0, h, g))
    return call(
        backward_kernel,
        "attention_backward",
        shape((3, width, tokens), LOW),
        (probs, proj_t, grad_t),
        grid=(images, heads // step),
        specs=[
            pl.BlockSpec((1, step, positions, positions), lambda g, h: (g, h, 0, 0)),
            block,
            pl.BlockSpec((rows, positions), lambda g, h: (h, g)),
        ],
        out_specs=block,
    )


def put_in_order(place, pieces, wide_ref):
    core, chip, z = place[0], place[1], place[2]
    groups, share, _ = pieces[0].shape
    rows = wide_ref.shape[0] // groups
    for m, piece in enumerate(pieces):
        owner = 2 * (chip ^ (m % CHIPS)) + (core ^ (m // CHIPS))
        for k in range(groups):
            start = (z ^ k) * rows + owner * share
            wide_ref[rows_at(start, share), :] = piece[k]


def join_kernel(place, mixed0, mixed1, mixed2, mixed3, bias, inputs, mod, *refs):
    pieces, (attention_ref, middle_ref, entry_ref, low_ref, wide_ref, mixed_ref) = refs[:-6], refs[-6:]

    @pl.when(pl.program_id(0) == 0)
    def _():
        put_in_order(place, pieces, wide_ref)
        low_ref[...] = wide_ref[...].astype(LOW)

    for k, mixed in enumerate((mixed0, mixed1, mixed2, mixed3)):
        columns = mixed.shape[0]
        mixed_ref[rows_at((place[2] ^ k) * columns, columns, 16), :] = mixed[...].astype(LOW)
    attention = mm(mixed_ref[...], low_ref[...], TN) + bias[...].astype(FULL)
    attention_ref[...] = attention
    middle = inputs[...].astype(FULL) + mod[0, 2:3, :] * attention
    middle_ref[...] = middle
    normed = norm_parts(middle)[0]
    entry_ref[...] = (normed * (1.0 + mod[0, 4:5, :]) + mod[0, 3:4, :]).astype(LOW)


def join_heads(place, mixed, pieces, bias, inputs, modulation):
    images = modulation.shape[0]
    tokens, width = inputs.shape
    positions = tokens // images
    columns = mixed[0].shape[0]
    rows = columns * len(mixed)
    by_image = pl.BlockSpec((positions, width), lambda g: (g, 0))
    specs = [pl.BlockSpec((columns, positions), lambda g: (0, g))] * len(mixed)
    specs += [pl.BlockSpec((1, width), lambda g: (0, 0)), by_image]
    specs += [pl.BlockSpec((1, 6, width), lambda g: (g, 0, 0))]
    specs += [pl.BlockSpec(pieces[0].shape, lambda g: (0, 0, 0))] * len(pieces)
    return call(
        join_kernel,
        "join_heads",
        (
            shape((tokens, width)),
            shape((tokens, width)),
            shape((tokens, width), LOW),
            shape((rows, width), LOW),
        ),
        (place, *mixed, bias, inputs, modulation, *pieces),
        smem=1,
        grid=(images,),
        specs=specs,
        out_specs=(by_image, by_image, by_image, pl.BlockSpec((rows, width), lambda g: (0, 0))),
        scratch=[pltpu.VMEM((rows, width), FULL), pltpu.VMEM((rows, positions), LOW)],
    )


def project_kernel(weight_ref, bias, entry, out_ref, low_ref):
    groups, _, columns, _ = weight_ref.shape
    for j in range(3):
        offsets = bias_columns(bias[j : j + 1, :].astype(LOW), entry.shape[0])
        for t in range(groups):
            weight = weight_ref[t, j].astype(LOW)
            row = slice(t * columns, (t + 1) * columns)
            low_ref[j, row, :] = weight
            out_ref[j, row, :] = (mm(weight, entry[...], NT) + offsets[row]).astype(LOW)


def project_all(weight, bias, entry):
    tokens, width = entry.shape
    rows = bias.shape[1]
    return call(
        project_kernel,
        "project_all",
        (shape((3, rows, tokens), LOW), shape((3, rows, width), LOW)),
        (weight, bias, entry),
    )


def middle_kernel(
    grad_ref, middle_ref, attention_ref, upstream_ref, mod_ref, weight_ref,
    middle_grad_ref, low_ref, mixed_grad_ref, sums_ref,
):
    grad = grad_ref[...]
    normed, inverse = norm_parts(middle_ref[...])
    sums_ref[0, 2:3, :] = jnp.sum(grad * normed, axis=0, keepdims=True)
    sums_ref[0, 1:2, :] = jnp.sum(grad, axis=0, keepdims=True)
    middle_grad = upstream_ref[...].astype(FULL)
    middle_grad = middle_grad + norm_back(grad * (1.0 + mod_ref[0, 4:5, :]), normed, inverse)
    middle_grad_ref[...] = middle_grad
    sums_ref[0, 0:1, :] = jnp.sum(middle_grad * attention_ref[...], axis=0, keepdims=True)
    low = (mod_ref[0, 2:3, :] * middle_grad).astype(LOW)
    low_ref[...] = low
    sums_ref[0, 3:4, :] = jnp.sum(low.astype(FULL), axis=0, keepdims=True)
    mixed_grad_ref[...] = mm(weight_ref[...], low, NT).astype(LOW)


def middle_backward(grad, middle, attention, upstream, modulation, weight):
    images = modulation.shape[0]
    tokens, width = grad.shape
    positions = tokens // images
    by_image = pl.BlockSpec((positions, width), lambda g: (g, 0))
    return call(
        middle_kernel,
        "middle_backward",
        (
            shape((tokens, width)),
            shape((tokens, width), LOW),
            shape((weight.shape[0], tokens), LOW),
            shape((images, 4, width)),
        ),
        (grad, middle, attention, upstream, modulation, weight),
        grid=(images,),
        specs=[by_image] * 4
        + [
            pl.BlockSpec((1, 6, width), lambda g: (g, 0, 0)),
            pl.BlockSpec(weight.shape, lambda g: (0, 0)),
        ],
        out_specs=(
            by_image,
            by_image,
            pl.BlockSpec((weight.shape[0], positions), lambda g: (0, g)),
            pl.BlockSpec((1, 4, width), lambda g: (g, 0, 0)),
        ),
    )


def entry_kernel(proj_ref, weight_ref, inputs_ref, middle_grad_ref, mod_ref, out_ref, sums_ref):
    grad = mm(proj_ref[...], weight_ref[...], TN)
    normed, inverse = norm_parts(inputs_ref[...].astype(FULL))
    sums_ref[0, 0:1, :] = jnp.sum(grad, axis=0, keepdims=True)
    sums_ref[0, 1:2, :] = jnp.sum(grad * normed, axis=0, keepdims=True)
    back = norm_back(grad * (1.0 + mod_ref[0, 1:2, :]), normed, inverse)
    out_ref[...] = middle_grad_ref[...] + back


def entry_backward(proj_grad, weight, inputs, middle_grad, modulation):
    images = modulation.shape[0]
    tokens, width = inputs.shape
    positions = tokens // images
    by_image = pl.BlockSpec((positions, width), lambda g: (g, 0))
    return call(
        entry_kernel,
        "entry_backward",
        (shape((tokens, width)), shape((images, 2, width))),
        (proj_grad, weight, inputs, middle_grad, modulation),
        grid=(images,),
        specs=[
            pl.BlockSpec((proj_grad.shape[0], positions), lambda g: (0, g)),
            pl.BlockSpec(weight.shape, lambda g: (0, 0)),
            by_image,
            by_image,
            pl.BlockSpec((1, 6, width), lambda g: (g, 0, 0)),
        ],
        out_specs=(by_image, pl.BlockSpec((1, 2, width), lambda g: (g, 0, 0))),
    )


def end_kernel(branch_ref, bias_ref, middle_ref, upstream_ref, mod_ref, out_ref, sums_ref):
    branch = branch_ref[...] + bias_ref[...].astype(FULL)
    out_ref[...] = (middle_ref[...] + mod_ref[0, 5:6, :] * branch).astype(LOW)
    sums_ref[0] = jnp.sum(upstream_ref[...].astype(FULL) * branch, axis=0, keepdims=True)


def end_forward(branch, bias, middle, upstream, modulation):
    images = modulation.shape[0]
    tokens, width = middle.shape
    by_image = pl.BlockSpec((tokens // images, width), lambda g: (g, 0))
    return call(
        end_kernel,
        "end_forward",
        (shape((tokens, width), LOW), shape((images, 1, width))),
        (branch, bias, middle, upstream, modulation),
        grid=(images,),
        specs=[
            by_image,
            pl.BlockSpec((1, width), lambda g: (0, 0)),
            by_image,
            by_image,
            pl.BlockSpec((1, 6, width), lambda g: (g, 0, 0)),
        ],
        out_specs=(by_image, pl.BlockSpec((1, 1, width), lambda g: (g, 0, 0))),
    )


def modulator_kernel(every_ref, context_ref, out_ref, sums_ref):
    part = every_ref[...]
    sums_ref[...] = jnp.sum(part, axis=0, keepdims=True)
    out_ref[...] = mm(context_ref[...].astype(LOW), part.astype(LOW), TN)


def modulator_backward(every, context, width):
    images = every.shape[0]
    total = every.shape[1]
    rows = context.shape[1]
    return call(
        modulator_kernel,
        "modulator_backward",
        (shape((rows, total)), shape((1, total))),
        (every, context),
        grid=(total // width,),
        specs=[
            pl.BlockSpec((images, width), lambda p: (0, p)),
            pl.BlockSpec((images, rows), lambda p: (0, 0)),
        ],
        out_specs=(
            pl.BlockSpec((rows, width), lambda p: (0, p)),
            pl.BlockSpec((1, width), lambda p: (0, p)),
        ),
    )


def mlp_grads_kernel(place, active, branch_grad, entry, hidden_grad, away_ref, kept_ref):
    half = active.shape[1] // 2
    for ref, core in ((away_ref, 1 - place[0]), (kept_ref, place[0])):
        column = rows_at(core * half, half, 128)
        ref[:half, :] = mm(active[:, column], branch_grad[...], TN)
        ref[half:, :] = mm(entry[:, column], hidden_grad[...], TN)


def mlp_grads(place, active, branch_grad, entry, hidden_grad):
    width = entry.shape[1]
    half = shape((width, width))
    operands = (place, active, branch_grad, entry, hidden_grad)
    return call(mlp_grads_kernel, "mlp_grads", (half, half), operands, smem=1)


def attn_grads_kernel(place, proj, entry, mixed, grad, away_ref, kept_ref, sums_ref, own_ref):
    columns = mixed.shape[0]
    for j in range(3):
        own_ref[j * columns : (j + 1) * columns, :] = proj[j, rows_at(place[2] * columns, columns, 16), :]
    sums_ref[...] = mm(jnp.ones((8, own_ref.shape[1]), LOW), own_ref[...], NT)
    inner, outer = 3 * columns // 2, columns // 2
    for ref, core in ((away_ref, 1 - place[0]), (kept_ref, place[0])):
        ref[:inner, :] = mm(own_ref[rows_at(core * inner, inner, 16), :], entry[...])
        ref[inner:, :] = mm(mixed[rows_at(core * outer, outer), :].astype(LOW), grad[...])


def attn_grads(place, proj, entry, mixed, grad):
    columns, tokens = mixed.shape
    width = entry.shape[1]
    half = shape((2 * columns, width))
    return call(
        attn_grads_kernel,
        "attn_grads",
        (half, half, shape((8, 3 * columns))),
        (place, proj, entry, mixed, grad),
        smem=1,
        scratch=[pltpu.VMEM((3 * columns, tokens), LOW)],
    )


def cut_kernel(shares, place, kept, other, *outs):
    for k, out in enumerate(outs):
        base, at = 0, 0
        for share in shares:
            row = rows_at(base + (place[1] ^ k) * share, share)
            out[at : at + share, :] = kept[row, :] + other[row, :]
            base, at = base + CHIPS * share, at + share


def place_kernel(shares, place, *refs):
    parts, out = refs[:-1], refs[-1]
    for k, part in enumerate(parts):
        base, at = 0, 0
        for share in shares:
            out[rows_at(base + (place[1] ^ k) * share, share), :] = part[at : at + share, :]
            base, at = base + CHIPS * share, at + share


def whole_kernel(shares, place, mine, other, *outs):
    base = 0
    for share, out in zip(shares, outs):
        half = CHIPS * share
        out[rows_at(place[0] * half, half), :] = mine[base : base + half, :]
        out[rows_at((1 - place[0]) * half, half), :] = other[base : base + half, :]
        base += half


def flip(value, axis, count, mask):
    return lax.ppermute(value, axis, [(i, i ^ mask) for i in range(count)])


def sum_shares(place, away, kept, shares, n_dp, *others):
    other = flip(away, "dp", n_dp, 1)
    part = shape((sum(shares), kept.shape[1]))
    parts = call(
        functools.partial(cut_kernel, shares), "cut", (part,) * CHIPS, (place, kept, other), smem=1
    )
    moved = [flip(parts[k], "dp", n_dp, 2 * k) for k in range(1, CHIPS)]
    total = (tie(parts[0], *others) if others else parts[0]) + moved[0] + moved[1] + moved[2]
    masks = [1 << i for i in range(3, n_dp.bit_length() - 1)]
    return double(halve(total, n_dp, masks), n_dp, masks)


def spread_chips(share, n_dp):
    return [share] + [flip(share, "dp", n_dp, 2 * k) for k in range(1, CHIPS)]


def spread_shares(place, parts, shares, n_dp):
    width = parts[0].shape[1]
    half = shape((CHIPS * sum(shares), width))
    mine = call(functools.partial(place_kernel, shares), "place", half, (place, *parts), smem=1)
    other = flip(mine, "dp", n_dp, 1)
    outs = tuple(shape((GROUP * count, width)) for count in shares)
    return call(
        functools.partial(whole_kernel, shares), "whole", outs, (place, mine, other), smem=1
    )


def halve(value, count, masks):
    index = lax.axis_index("dp")
    for mask in masks:
        half = value.shape[0] // 2
        side = (index // mask) % 2
        away = lax.dynamic_slice_in_dim(value, (1 - side) * half, half, 0)
        kept = lax.dynamic_slice_in_dim(value, side * half, half, 0)
        value = kept + flip(away, "dp", count, mask)
    return value


def double(value, count, masks):
    index = lax.axis_index("dp")
    for mask in reversed(masks):
        other = flip(value, "dp", count, mask)
        lower = (index // mask) % 2 == 0
        value = jnp.concatenate([jnp.where(lower, value, other), jnp.where(lower, other, value)])
    return value


def gather_rows(rows, n_dp):
    share = rows.shape[0] // n_dp
    mine = lax.dynamic_slice_in_dim(rows, lax.axis_index("dp") * share, share, 0)
    return lax.all_gather(mine.astype(FULL), ("tensor", "dp"), tiled=True)


def gather_z(rows, n_tensor):
    share = rows.shape[0] // GROUP
    start = (lax.axis_index("dp") % GROUP) * share
    mine = lax.dynamic_slice_in_dim(rows, start, share, 0).astype(FULL)
    return [mine] + [flip(mine, "tensor", n_tensor, k) for k in range(1, n_tensor)]


def gather_pieces(parts, n_dp):
    stacked = jnp.stack(parts)
    pieces = [stacked] + [flip(stacked, "dp", n_dp, 2 * k) for k in range(1, CHIPS)]
    return pieces + [flip(piece, "dp", n_dp, 1) for piece in pieces]


def tie_kernel(*refs):
    pass


def tie(value, *others):
    anywhere = pl.BlockSpec(memory_space=pl.ANY)
    return pl.pallas_call(
        tie_kernel,
        out_shape=jax.ShapeDtypeStruct(value.shape, value.dtype),
        in_specs=[anywhere] * (1 + len(others)),
        out_specs=anywhere,
        input_output_aliases={0: 0},
        name="tie",
    )(value, *others)


def as_one(function, *operands):
    shapes = jax.eval_shape(function, *operands)
    nothing = lambda *_: jax.tree.map(lambda leaf: jnp.zeros(leaf.shape, leaf.dtype), shapes)
    return lax.cond(lax.axis_index("dp") >= 0, function, nothing, *operands)


def per_device(
    n_dp,
    n_tensor,
    latents,
    condition,
    modulator,
    modulator_bias,
    attn_input,
    attn_input_bias,
    attn_output,
    attn_output_bias,
    ffn_input,
    ffn_input_bias,
    ffn_output,
    ffn_output_bias,
    cotangent,
):
    image_count, positions, features = latents.shape
    tokens = image_count * positions
    columns = attn_input.shape[2]
    z = lax.axis_index("tensor")
    member = lax.axis_index("dp") % GROUP
    place = jnp.stack([member % 2, member // 2, z]).astype(jnp.int32)
    inputs = latents.reshape(tokens, features)
    upstream = cotangent.reshape(tokens, features)
    weight_t = attn_input.swapaxes(1, 2)

    weight_wide = gather_rows(weight_t.reshape(-1, features), n_dp)
    weight_wide = weight_wide.reshape(n_tensor, 3, columns, features)
    cond_float = condition.astype(FULL)
    context_low = jax.nn.silu(cond_float).astype(LOW)

    def forward(context_low):
        def start(context_low):
            partial = mm(context_low, modulator)
            bias_own = jnp.stack(
                [attn_input_bias[0], jnp.zeros_like(attn_input_bias[0]), attn_input_bias[1]]
            )
            bias_row = jnp.zeros((3, n_tensor * columns), FULL)
            bias_row = lax.dynamic_update_slice_in_dim(bias_row, bias_own.astype(FULL), z * columns, 1)
            bias_row = bias_row.reshape(1, -1)
            bias_row = jnp.pad(bias_row, ((0, 0), (0, partial.shape[1] - bias_row.shape[1])))
            shared = jnp.concatenate([partial, bias_row])
            shared = [shared] + [flip(shared, "tensor", n_tensor, k) for k in range(1, n_tensor)]
            return call(
                start_kernel,
                "start",
                (
                    shape((columns, tokens)),
                    shape((tokens, features), LOW),
                    shape((image_count, 6, features)),
                    shape((3, n_tensor * columns)),
                ),
                (*shared, modulator_bias[None], inputs, weight_t, bias_own),
            )

        output_parts = gather_z(attn_output, n_tensor)
        mixed_t, entry_one, modulation, bias_full = start(context_low)
        mixed = [mixed_t] + [flip(mixed_t, "tensor", n_tensor, k) for k in range(1, n_tensor)]
        output_pieces = gather_pieces(output_parts, n_dp)
        attention, middle, entry_two, output_full = join_heads(
            place, mixed, output_pieces, attn_output_bias[None], inputs, modulation
        )
        hidden = mm(entry_two, ffn_input) + ffn_input_bias.astype(FULL)
        active, gelu_pull = jax.vjp(lambda inner: jax.nn.gelu(inner, approximate=True), hidden)
        active = active.astype(LOW)
        gate_two = modulation[:, None, 5]
        branch_grad = (gate_two * cotangent.astype(FULL)).astype(LOW).reshape(tokens, features)
        hidden_grad = gelu_pull(mm(branch_grad, ffn_output, NT))[0].astype(LOW)
        part = mm(hidden_grad, ffn_input, NT)
        first = mixed_t, entry_one, modulation, bias_full, attention, middle, output_full
        return first, (active, branch_grad, entry_two, hidden_grad), part

    first, mlp, part = as_one(forward, context_low)
    mixed_t, entry_one, modulation, bias_full, attention, middle, output_full = first
    entry_two_grad = lax.psum(part, "tensor")
    mlp_shares = (ffn_output.shape[0] // GROUP, features // GROUP)

    def beside_entry_two(place, weight_wide, mlp):
        active, branch_grad, entry_two, hidden_grad = mlp
        away, kept = mlp_grads(place, active, branch_grad, entry_two, hidden_grad)
        share = sum_shares(place, away, kept, mlp_shares, n_dp)
        proj_full, weight_full = project_all(weight_wide, bias_full, entry_one)
        mlp_parts = spread_chips(share, n_dp)
        probs = all_probs(proj_full, image_count)
        branch_part = mm(active, ffn_output)
        sums = [jnp.sum(x.astype(FULL), axis=0) for x in (branch_grad, hidden_grad)]
        return mlp_parts, probs, proj_full, weight_full, branch_part, sums

    mlp_parts, probs, proj_full, weight_full, branch_part, mlp_sums = as_one(
        beside_entry_two, tie(place, part), weight_wide, mlp
    )
    entry_two_grad = tie(entry_two_grad, branch_part)
    branch_part = tie(branch_part, entry_two_grad)
    branch = lax.psum(branch_part, "tensor")
    attn_shares = (3 * columns // GROUP, columns // GROUP)

    def beside_branch(entry_two_grad, probs, proj_full, weight_full, mlp_parts):
        def heads(entry_two_grad, probs, proj_full):
            middle_grad, attention_grad, mixed_grad_t, middle_sums = middle_backward(
                entry_two_grad, middle, attention, upstream, modulation, output_full
            )
            proj_grad = attention_backward(probs, proj_full, mixed_grad_t)
            parts = attn_grads(place, proj_grad, entry_one, mixed_t, attention_grad)
            return middle_grad, middle_sums, proj_grad, parts

        middle_grad, middle_sums, proj_grad, (away, kept, own_sums) = as_one(
            heads, entry_two_grad, probs, proj_full
        )
        latents_grad, entry_sums = entry_backward(
            proj_grad.reshape(-1, tokens),
            weight_full.reshape(-1, features),
            inputs,
            middle_grad,
            modulation,
        )
        attn_share = sum_shares(place, away, kept, attn_shares, n_dp, latents_grad)
        mlp_whole = spread_shares(place, mlp_parts, mlp_shares, n_dp)
        attn_parts = spread_chips(attn_share, n_dp)
        attn_parts[0] = tie(attn_parts[0], *mlp_whole)
        attn_whole = spread_shares(place, attn_parts, attn_shares, n_dp)
        return mlp_whole, attn_whole, latents_grad, entry_sums, own_sums, middle_sums

    mlp_whole, attn_whole, latents_grad, entry_sums, own_sums, middle_sums = as_one(
        beside_branch, tie(entry_two_grad, branch_part), probs, proj_full, weight_full, mlp_parts
    )
    layer_out, gate_two_grad = end_forward(
        tie(branch, entry_sums), ffn_output_bias[None], middle, upstream, modulation
    )
    modulation_grad = jnp.concatenate([entry_sums, middle_sums[:, :3], gate_two_grad], axis=1)
    modulation_grad = modulation_grad.reshape(image_count, -1).astype(LOW)
    context_grad = mm(modulation_grad, modulator, NT)
    condition_grad = jax.vjp(jax.nn.silu, cond_float)[1](context_grad)[0]

    sums = [mlp_sums[0], mlp_sums[1], jnp.sum(middle_sums[:, 3], axis=0), own_sums[0]]
    sizes = [part.shape[0] for part in sums]
    sums = jnp.pad(jnp.concatenate(sums)[None], ((0, image_count - 1), (0, 0)))
    small = [modulation_grad.astype(FULL), sums, context_low.astype(FULL)]
    every = lax.all_gather(jnp.concatenate(small, axis=1), "dp", tiled=True)
    every_rows = 6 * features
    context_at = every_rows + sum(sizes)
    grad_modulator, grad_modulator_bias = modulator_backward(
        every[:, :every_rows], every[:, context_at:], features
    )
    sums = jnp.split(jnp.sum(every[:, every_rows:context_at], axis=0), [sum(sizes[:i]) for i in (1, 2, 3)])
    input_bias = sums[3].reshape(3, columns)
    return (
        layer_out.reshape(latents.shape),
        latents_grad.reshape(latents.shape),
        condition_grad,
        grad_modulator,
        grad_modulator_bias[0],
        attn_whole[0].reshape(3, columns, features).swapaxes(1, 2),
        jnp.stack([input_bias[0], input_bias[2]]),
        attn_whole[1],
        sums[2],
        mlp_whole[1],
        sums[1],
        mlp_whole[0],
        sums[0],
    )


def solution(mesh):
    placed = (
        P("dp", None, None),
        P("dp", "tensor"),
        P("tensor", None),
        P(),
        P(None, None, "tensor"),
        P(None, "tensor"),
        P("tensor", None),
        P(),
        P(None, "tensor"),
        P("tensor"),
        P("tensor", None),
        P(),
        P("dp", None, None),
    )
    return jax.shard_map(
        functools.partial(per_device, mesh.shape["dp"], mesh.shape["tensor"]),
        mesh=mesh,
        in_specs=placed,
        out_specs=(
            P("dp", None, None),
            P("dp", None, None),
            P("dp", "tensor"),
            P("tensor", None),
            P(),
            P(None, None, "tensor"),
            P(None, "tensor"),
            P("tensor", None),
            P(),
            P(None, "tensor"),
            P("tensor"),
            P("tensor", None),
            P(),
        ),
        check_vma=False,
    )
```

time: 488 us -> 288 us (0.59)
  waiting for transfers between devices: 279 us -> 117 us
  Pallas kernels: 28.7 us -> 69.9 us
  local copies, waits for them, and re-layouts: 44.5 us -> 15.3 us
  other arithmetic: 40.7 us -> 14.2 us
  blocking collectives: 24.3 us -> 9.77 us
  matrix products: 25.8 us -> 11.4 us
  starting transfers between devices: 27.8 us -> 33.5 us
    all_gather x2 -> x1, waiting for transfers between devices: 91.5 us -> 18 us  [gather_rows(): return lax.all_gather(mine.astype(FULL), ('tensor', 'dp'), tiled=True)]
    all_gather x2 -> x0, waiting for transfers between devices: 72.7 us -> none  [the longest x1 37.4 us: per_device(): branch = lax.all_gather(branch, 'tensor', tiled=True)]
    ppermute x27 -> x32, waiting for transfers between devices: 47 us -> 98.1 us  [flip(): return lax.ppermute(value, axis, [(i, i ^ mask) for i in range(count)])]
    pallas_call x4 -> x24, Pallas kernels: 28.7 us -> 69.9 us  [the longest x17 69.9 us: call(): pl.pallas_call(kernel, out_shape=out_shape, in_specs=in_specs, out_specs=...]
    reduce_scatter x1 -> x0, waiting for transfers between devices: 34.3 us -> none  [per_device(): branch = lax.psum_scatter(mm(active, ffn_output), 'tensor', tiled=True)]
    psum x1 -> x2, waiting for transfers between devices: 33.2 us -> 0.03 us  [the longest x1 0.03 us: per_device(): branch = lax.psum(branch_part, 'tensor')]
    all_gather x2 -> x1, blocking collectives: 24.3 us -> 9.77 us  [per_device(): every = lax.all_gather(jnp.concatenate(small, axis=1), 'dp', tiled=True)]
    dot_general x13 -> x6, matrix products: 25.8 us -> 11.4 us  [mm(): return lax.dot_general(left, right, dims, preferred_element_type=FULL)]
  transfers between devices with their start and end apart: 33 -> 35, of which waited for: 20 -> 19; matrix products, arithmetic and copies ran while one was open for 17% -> 9% of each run, Pallas kernels for 4% -> 22%
where the time goes in v3:
time: 288 us; the launch traced here: 287 us
  waiting for transfers between devices  117 us (41%)
  Pallas kernels  69.9 us (24%)
  starting transfers between devices  33.5 us (12%)
  between operations  15.7 us (5%)
  local copies, waits for them, and re-layouts  15.3 us (5%)
  other arithmetic  14.2 us (5%)
  matrix products  11.4 us (4%)
  blocking collectives  9.77 us (3%)
    ppermute x32, waiting for transfers between devices, flip(): return lax.ppermute(value, axis, [(i, i ^ mask) for i in range(count)])  98.1 us
    pallas_call x17, Pallas kernels, call(): pl.pallas_call(kernel, out_shape=out_shape, in_specs=in_specs, out_specs=...  69.9 us
    ppermute x32, starting transfers between devices, flip(): return lax.ppermute(value, axis, [(i, i ^ mask) for i in range(count)])  33.2 us
    all_gather x1, waiting for transfers between devices, gather_rows(): return lax.all_gather(mine.astype(FULL), ('tensor', 'dp'), tiled=True)  18 us
    dot_general x6, matrix products, mm(): return lax.dot_general(left, right, dims, preferred_element_type=FULL)  11.4 us
    all_gather x1, blocking collectives, per_device(): every = lax.all_gather(jnp.concatenate(small, axis=1), 'dp', tiled=True)  9.77 us
    unnamed x23, local copies, waits for them, and re-layouts  6.36 us
  transfers between devices with their start and end apart: 35, of which 19 were waited for; matrix products, arithmetic and copies ran while one was open for 9% of the time, Pallas kernels for 22%

profile of v3, /device:TPU:0, one launch (start us, length us, event | category | flops | bytes accessed | tf_op | source)
XLA Modules:
  0.0 286.7 jit_solution(16615821810890096993)
XLA Ops:
  11.6 81.4 %conditional.4 = (f32[192,512]{1,0:T(8,128)S(1)}, bf16[512,768]{1,0:T(8,128)(2,1)S(1)}, f32[2,6,768]{2,1,0:T(8,128)}, f32[3,768]{1,0:T(4,128)S(1)}, f32[512,768]...) conditional(s32[]{:T(128)} %convert_element_type.58, () %tuple.53, ...), branch_computations={%region_0.1_spmd, %region_1.2_spmd} | conditional | flops 1825987840 | bytes 49992288 | solution.py:533
  12.4 3.1 %collective-permute-start.15 = (f32[24,768]{1,0:T(8,128)S(1)}, f32[24,768]{1,0:T(8,128)S(1)}, u32[]{:S(2)}, u32[]{:S(2)}) collective-permute-start(f32[24,768]{1,0:T(8,128)S(1)} %get-tuple-element.306), channel_id=1, source_target_pairs={{0,1},{1,0},{2,3},{3,2},{4,5},{5,4},{6,7},{7,6},{8,9},{9,8},{10,11... | collective-permute-start | bytes 221192 | tf_op jit(solution)/shard_map/cond/branch_1_fun/ppermute | solution.py:445
  15.5 2.6 collective-permute-start.16
  31.1 6.1 %collective-permute-done.10.part2 = f32[3,4608]{1,0:T(4,128)S(1)} collective-permute-done((f32[3,4608]{1,0:T(4,128)S(1)}, f32[3,4608]{1,0:T(4,128)S(1)}, u32[]{:S(2)}, u32[]{:S(2)}) %collective-permute-start.10) | collective-permute-done | bytes 55328 | tf_op jit(solution)/shard_map/cond/branch_1_fun/ppermute | solution.py:445
  38.3 4.9 %start.1 = (f32[192,512]{1,0:T(8,128)S(1)}, bf16[512,768]{1,0:T(8,128)(2,1)S(1)}, f32[2,6,768]{2,1,0:T(8,128)}, f32[3,768]{1,0:T(4,128)S(1)}) custom-call(f32[3,4608]{1,0:T(4,128)S(1)} %select_maximum_fusion.part0, f32[3,4608]{1,0:T(4,128)S(1)} %collective-permute-done.9.part1, f32[3,4608]{1,0:T(4,128)S(1)} %collective-permute-done.10.part2, ...), custom_call_target="tpu_custom_call" | custom-call | tf_op jit(solution)/shard_map/cond/branch_1_fun/start/pallas_call | solution.py:55
  50.3 6.6 %collective-permute-done.20.refs_3_ = f32[4,24,768]{2,1,0:T(8,128)S(1)} collective-permute-done((f32[4,24,768]{2,1,0:T(8,128)S(1)}, f32[4,24,768]{2,1,0:T(8,128)S(1)}, u32[]{:S(2)}, u32[]{:S(2)}) %collective-permute-start.20) | collective-permute-done | bytes 294944 | tf_op jit(solution)/shard_map/cond/branch_1_fun/ppermute | solution.py:445
  57.4 7.3 %collective-permute-done.12.mixed1 = f32[192,512]{1,0:T(8,128)S(1)} collective-permute-done((f32[192,512]{1,0:T(8,128)S(1)}, f32[192,512]{1,0:T(8,128)S(1)}, u32[]{:S(2)}, u32[]{:S(2)}) %collective-permute-start.12) | collective-permute-done | bytes 393248 | tf_op jit(solution)/shard_map/cond/branch_1_fun/ppermute | solution.py:445
  66.7 16.3 %collective-permute-done.13.mixed2 = f32[192,512]{1,0:T(8,128)S(1)} collective-permute-done((f32[192,512]{1,0:T(8,128)S(1)}, f32[192,512]{1,0:T(8,128)S(1)}, u32[]{:S(2)}, u32[]{:S(2)}) %collective-permute-start.13) | collective-permute-done | bytes 393248 | tf_op jit(solution)/shard_map/cond/branch_1_fun/ppermute | solution.py:445
  83.0 4.3 %join_heads.1 = (f32[512,768]{1,0:T(8,128)}, f32[512,768]{1,0:T(8,128)}, bf16[512,768]{1,0:T(8,128)(2,1)}, bf16[768,768]{1,0:T(8,128)(2,1)}) custom-call(s32[3]{0:T(128)S(1)} %get-tuple-element.120.place, f32[192,512]{1,0:T(8,128)S(1)} %get-tuple-element.342.mixed0, f32[192,512]{1,0:T(8,128)S(1)} %collective-permute-done.12.mixed1, ...), custom_call_target="tpu_custom_call" | custom-call | tf_op jit(solution)/shard_map/cond/branch_1_fun/join_heads/pallas_call | solution.py:55
  87.2 3.7 %fusion.6 = (bf16[512,768]{1,0:T(8,128)(2,1)}, bf16[512,768]{1,0:T(8,128)(2,1)S(1)}) fusion(f32[512,768]{1,0:T(8,128)S(1)} %fusion.20, f32[768]{0:T(1024)S(1)} %convert_element_type.43, bf16[512,768]{1,0:T(8,128)(2,1)} %get-tuple-element.351, bf16[768,768]{1,0:T(8,128)(2,1)S(1)} %copy-done.31), kind=kOutput, calls=%fused_computation.8 | convolution fusion | flops 613023744 | bytes 5114880 | tf_op jit(solution)/shard_map/cond/branch_1_fun/dot_general | solution.py:23
  94.1 18.0 %all-gather.3.cloned.1.call-done = f32[2304,768]{1,0:T(8,128)} async-done(((f32[72,768]{1,0:T(8,128)}), f32[2304,768]{1,0:T(8,128)}) %all-gather.3.cloned.1.call-update) | async-done | bytes 7077904 | tf_op jit(solution)/shard_map/all_gather | solution.py:498
  112.2 69.4 %conditional.5 = (f32[192,768]{1,0:T(8,128)}, f32[192,768]{1,0:T(8,128)}, f32[192,768]{1,0:T(8,128)}, f32[192,768]{1,0:T(8,128)}, f32[2,12,256,256]{3,2,1,0:T(8,...) conditional(s32[]{:T(128)} %convert_element_type.58, () %tuple.52, ...), branch_computations={%region_2.3_spmd, %region_3.6_spmd} | conditional | flops 605993472 | bytes 74127880 | solution.py:533
  112.2 3.0 %mlp_grads.1 = (f32[768,768]{1,0:T(8,128)S(1)}, f32[768,768]{1,0:T(8,128)S(1)}) custom-call(s32[3]{0:T(128)} %get-tuple-element.131.place, bf16[512,768]{1,0:T(8,128)(2,1)S(1)} %get-tuple-element.132.active, bf16[512,768]{1,0:T(8,128)(2,1)} %get-tuple-element.133.branch_grad, bf16[512,768]{1,0:T(8,128)(2,1)} %get-tuple-element.134.entry, ...), custom_call_target="tpu_custom_call" | custom-call | tf_op jit(solution)/shard_map/cond/branch_1_fun/mlp_grads/pallas_call | solution.py:55
  115.5 4.3 %collective-permute-done.25.other = f32[768,768]{1,0:T(8,128)S(1)} collective-permute-done((f32[768,768]{1,0:T(8,128)S(1)}, f32[768,768]{1,0:T(8,128)S(1)}, u32[]{:S(2)}, u32[]{:S(2)}) %collective-permute-start.25) | collective-permute-done | bytes 2359328 | tf_op jit(solution)/shard_map/cond/branch_1_fun/ppermute | solution.py:445
  126.9 12.7 %collective-permute-done.26 = f32[192,768]{1,0:T(8,128)S(1)} collective-permute-done((f32[192,768]{1,0:T(8,128)S(1)}, f32[192,768]{1,0:T(8,128)S(1)}, u32[]{:S(2)}, u32[]{:S(2)}) %collective-permute-start.26) | collective-permute-done | bytes 589856 | tf_op jit(solution)/shard_map/cond/branch_1_fun/ppermute | solution.py:445
  139.5 13.2 %collective-permute-done.27 = f32[192,768]{1,0:T(8,128)S(1)} collective-permute-done((f32[192,768]{1,0:T(8,128)S(1)}, f32[192,768]{1,0:T(8,128)S(1)}, u32[]{:S(2)}, u32[]{:S(2)}) %collective-permute-start.27) | collective-permute-done | bytes 589856 | tf_op jit(solution)/shard_map/cond/branch_1_fun/ppermute | solution.py:445
  157.1 5.5 %project_all.1 = (bf16[3,768,512]{2,1,0:T(8,128)(2,1)}, bf16[3,768,768]{2,1,0:T(8,128)(2,1)}) custom-call(f32[4,3,192,768]{3,2,1,0:T(8,128)S(1)} %bitcast.47, f32[3,768]{1,0:T(4,128)S(1)} %get-tuple-element.143.bias, bf16[512,768]{1,0:T(8,128)(2,1)S(1)} %get-tuple-element.144.entry), custom_call_target="tpu_custom_call" | custom-call | tf_op jit(solution)/shard_map/cond/branch_1_fun/project_all/pallas_call | solution.py:55
  162.6 7.0 %all_probs.1 = f32[2,12,256,256]{3,2,1,0:T(8,128)} custom-call(bf16[3,768,512]{2,1,0:T(8,128)(2,1)} %get-tuple-element.369.proj_ref), custom_call_target="tpu_custom_call" | custom-call | tf_op jit(solution)/shard_map/cond/branch_1_fun/all_probs/pallas_call | solution.py:55
  172.8 8.8 %collective-permute-done.30 = f32[192,768]{1,0:T(8,128)} collective-permute-done((f32[192,768]{1,0:T(8,128)}, f32[192,768]{1,0:T(8,128)}, u32[]{:S(2)}, u32[]{:S(2)}) %collective-permute-start.30) | collective-permute-done | bytes 589856 | tf_op jit(solution)/shard_map/cond/branch_1_fun/ppermute | solution.py:445
  184.2 71.5 %conditional.6 = (f32[768,768]{1,0:T(8,128)}, f32[768,768]{1,0:T(8,128)}, f32[576,768]{1,0:T(8,128)}, f32[192,768]{1,0:T(8,128)}, f32[2,2,768]{2,1,0:T(2,128)S(1...) conditional(s32[]{:T(128)} %convert_element_type.58, () %tuple.56, ...), branch_computations={%region_8.9_spmd, %region_9.13_spmd} | conditional | flops 225029 | bytes 49997164 | solution.py:533
  187.3 23.8 %conditional = (f32[512,768]{1,0:T(8,128)}, f32[2,4,768]{2,1,0:T(4,128)}, f32[384,768]{1,0:T(8,128)}, f32[384,768]{1,0:T(8,128)}, bf16[2304,512]{1,0:T(8,128)(2,...) conditional(s32[]{:T(128)} %convert_element_type.50, () %tuple.41, (f32[512,768]{1,0:T(8,128)}, ...), branch_computations={%region_10.10_spmd, %region_11.11_spmd} | conditional | flops 768 | bytes 6330722 | solution.py:533
  187.3 5.9 %middle_backward.1 = (f32[512,768]{1,0:T(8,128)}, bf16[512,768]{1,0:T(8,128)(2,1)S(1)}, bf16[768,512]{1,0:T(8,128)(2,1)S(1)}, f32[2,4,768]{2,1,0:T(4,128)}) custom-call(f32[512,768]{1,0:T(8,128)} %get-tuple-element.148.grad_ref, f32[512,768]{1,0:T(8,128)} %get-tuple-element.149.middle_ref, f32[512,768]{1,0:T(8,128)} %get-tuple-element.150.attention_ref, ...), custom_call_target="tpu_custom_call" | custom-call | tf_op jit(solution)/shard_map/cond/branch_1_fun/cond/branch_1_fun/middle_backward/pallas_call | solution.py:55
  193.2 10.6 %attention_backward.1.proj = bf16[3,768,512]{2,1,0:T(8,128)(2,1)} custom-call(f32[2,12,256,256]{3,2,1,0:T(8,128)} %get-tuple-element.157.probs_ref, bf16[3,768,512]{2,1,0:T(8,128)(2,1)} %get-tuple-element.158.proj_ref, bf16[768,512]{1,0:T(8,128)(2,1)S(1)} %get-tuple-element.159.grad_ref), custom_call_target="tpu_custom_call" | custom-call | tf_op jit(solution)/shard_map/cond/branch_1_fun/cond/branch_1_fun/attention_backward/pallas_call | solution.py:55
  203.8 3.9 %attn_grads.1 = (f32[384,768]{1,0:T(8,128)}, f32[384,768]{1,0:T(8,128)}, f32[8,576]{1,0:T(8,128)S(1)}) custom-call(s32[3]{0:T(128)S(1)} %get-tuple-element.156.place, bf16[3,768,512]{2,1,0:T(8,128)(2,1)} %attention_backward.1.proj, bf16[512,768]{1,0:T(8,128)(2,1)S(1)} %get-tuple-element.160.entry, f32[192,512]{1,0:T(8,128)S(1)} %get-tuple-element.161.mixed, ...), custom_call_target="tpu_custom_call" | custom-call | tf_op jit(solution)/shard_map/cond/branch_1_fun/cond/branch_1_fun/attn_grads/pallas_call | solution.py:55
  211.6 2.7 collective-permute-done.1.other
  219.3 6.6 %entry_backward.1 = (f32[512,768]{1,0:T(8,128)}, f32[2,2,768]{2,1,0:T(2,128)S(1)}) custom-call(bf16[2304,512]{1,0:T(8,128)(2,1)} %get-tuple-element.186.proj_ref, bf16[2304,768]{1,0:T(8,128)(2,1)} %bitcast.7.weight_ref, bf16[512,768]{1,0:T(8,128)(2,1)S(1)} %copy-done.15, f32[512,768]{1,0:T(8,128)} %get-tuple-element.189.middle_grad_ref, ...), custom_call_target="tpu_custom_call" | custom-call | tf_op jit(solution)/shard_map/cond/branch_1_fun/entry_backward/pallas_call | solution.py:55
  225.9 6.4 %collective-permute-done.3 = f32[96,768]{1,0:T(8,128)} collective-permute-done((f32[96,768]{1,0:T(8,128)S(1)}, f32[96,768]{1,0:T(8,128)}, u32[]{:S(2)}, u32[]{:S(2)}) %collective-permute-start.3) | collective-permute-done | bytes 294944 | tf_op jit(solution)/shard_map/cond/branch_1_fun/ppermute | solution.py:445
  237.1 4.1 %whole.2 = (f32[768,768]{1,0:T(8,128)}, f32[768,768]{1,0:T(8,128)}) custom-call(s32[3]{0:T(128)} %copy-done.21, f32[768,768]{1,0:T(8,128)S(1)} %place.2.mine, f32[768,768]{1,0:T(8,128)} %collective-permute-done.other), custom_call_target="tpu_custom_call" | custom-call | tf_op jit(solution)/shard_map/cond/branch_1_fun/whole/pallas_call | solution.py:55
  243.6 3.9 %collective-permute-done.6.refs_2_ = f32[96,768]{1,0:T(8,128)S(1)} collective-permute-done((f32[96,768]{1,0:T(8,128)S(1)}, f32[96,768]{1,0:T(8,128)S(1)}, u32[]{:S(2)}, u32[]{:S(2)}) %collective-permute-start.6) | collective-permute-done | bytes 294944 | tf_op jit(solution)/shard_map/cond/branch_1_fun/ppermute | solution.py:445
  259.1 2.4 end_forward.1
  262.5 9.8 %all-gather = f32[8,2,7680]{2,1,0:T(2,128)S(1)} all-gather(f32[1,2,7680]{2,1,0:T(2,128)S(1)} %bitcast.54), channel_id=1, replica_groups=mesh['dp'=8,'tensor'=4] {'dp'}, dimensions={0}, use_global_device_ids=true | all-gather | bytes 552960 | tf_op jit(solution)/shard_map/all_gather | solution.py:674
  275.1 3.5 %modulator_backward.1 = (f32[192,4608]{1,0:T(8,128)}, f32[1,4608]{1,0:T(1,128)S(1)}) custom-call(f32[16,4608]{1,0:T(8,128)S(1)} %slice.62.every_ref, f32[16,192]{1,0:T(8,128)S(1)} %slice.63.context_ref), custom_call_target="tpu_custom_call" | custom-call | tf_op jit(solution)/shard_map/modulator_backward/pallas_call | solution.py:55
  (186 shorter events, 83.6 us)
Async XLA Ops:
  8.0 104.1 %all-gather.3.cloned.1.call-start = ((), (), s32[]{:S(2)}) async-start(), calls=%async_computation | async-start | bytes 7299072 | tf_op jit(solution)/shard_map/all_gather | solution.py:498
  12.4 8.7 %collective-permute-start.15 = (f32[24,768]{1,0:T(8,128)S(1)}, f32[24,768]{1,0:T(8,128)S(1)}, u32[]{:S(2)}, u32[]{:S(2)}) collective-permute-start(f32[24,768]{1,0:T(8,128)S(1)} %get-tuple-element.306), channel_id=1, source_target_pairs={{0,1},{1,0},{2,3},{3,2},{4,5},{5,4},{6,7},{7,6},{8,9},{9,8},{10,11... | collective-permute-start | bytes 221192 | tf_op jit(solution)/shard_map/cond/branch_1_fun/ppermute | solution.py:445
  15.5 7.8 %collective-permute-start.16 = (f32[24,768]{1,0:T(8,128)S(1)}, f32[24,768]{1,0:T(8,128)S(1)}, u32[]{:S(2)}, u32[]{:S(2)}) collective-permute-start(f32[24,768]{1,0:T(8,128)S(1)} %get-tuple-element.306), channel_id=1, source_target_pairs={{0,2},{1,3},{2,0},{3,1},{4,6},{5,7},{6,4},{7,5},{8,10},{9,11},{10,... | collective-permute-start | bytes 221192 | tf_op jit(solution)/shard_map/cond/branch_1_fun/ppermute | solution.py:445
  18.1 6.3 %collective-permute-start.17 = (f32[24,768]{1,0:T(8,128)S(1)}, f32[24,768]{1,0:T(8,128)S(1)}, u32[]{:S(2)}, u32[]{:S(2)}) collective-permute-start(f32[24,768]{1,0:T(8,128)S(1)} %get-tuple-element.306), channel_id=1, source_target_pairs={{0,3},{1,2},{2,1},{3,0},{4,7},{5,6},{6,5},{7,4},{8,11},{9,10},{10,... | collective-permute-start | bytes 221192 | tf_op jit(solution)/shard_map/cond/branch_1_fun/ppermute | solution.py:445
  24.4 21.9 %collective-permute-start.18 = (f32[4,24,768]{2,1,0:T(8,128)S(1)}, f32[4,24,768]{2,1,0:T(8,128)S(1)}, u32[]{:S(2)}, u32[]{:S(2)}) collective-permute-start(f32[4,24,768]{2,1,0:T(8,128)S(1)} %pad_maximum_fusion.refs_0_), channel_id=1, source_target_pairs={{0,8},{4,12},{8,0},{12,4},{16,24},{20,28},{24,16},{28,20},{1,9},{5... | collective-permute-start | bytes 884744 | tf_op jit(solution)/shard_map/cond/branch_1_fun/ppermute | solution.py:445
  26.0 21.2 %collective-permute-start.19 = (f32[4,24,768]{2,1,0:T(8,128)S(1)}, f32[4,24,768]{2,1,0:T(8,128)S(1)}, u32[]{:S(2)}, u32[]{:S(2)}) collective-permute-start(f32[4,24,768]{2,1,0:T(8,128)S(1)} %pad_maximum_fusion.refs_0_), channel_id=1, source_target_pairs={{0,16},{4,20},{8,24},{12,28},{16,0},{20,4},{24,8},{28,12},{1,17},{... | collective-permute-start | bytes 884744 | tf_op jit(solution)/shard_map/cond/branch_1_fun/ppermute | solution.py:445
  27.5 9.7 %collective-permute-start.10 = (f32[3,4608]{1,0:T(4,128)S(1)}, f32[3,4608]{1,0:T(4,128)S(1)}, u32[]{:S(2)}, u32[]{:S(2)}) collective-permute-start(f32[3,4608]{1,0:T(4,128)S(1)} %select_maximum_fusion.part0), channel_id=1, source_target_pairs={{0,2},{1,3},{2,0},{3,1},{4,6},{5,7},{6,4},{7,5},{8,10},{9,11},{10,... | collective-permute-start | bytes 165896 | tf_op jit(solution)/shard_map/cond/branch_1_fun/ppermute | solution.py:445
  29.7 8.2 %collective-permute-start.11 = (f32[3,4608]{1,0:T(4,128)S(1)}, f32[3,4608]{1,0:T(4,128)S(1)}, u32[]{:S(2)}, u32[]{:S(2)}) collective-permute-start(f32[3,4608]{1,0:T(4,128)S(1)} %select_maximum_fusion.part0), channel_id=1, source_target_pairs={{0,3},{1,2},{2,1},{3,0},{4,7},{5,6},{6,5},{7,4},{8,11},{9,10},{10,... | collective-permute-start | bytes 165896 | tf_op jit(solution)/shard_map/cond/branch_1_fun/ppermute | solution.py:445
  31.0 7.2 %collective-permute-start.9 = (f32[3,4608]{1,0:T(4,128)S(1)}, f32[3,4608]{1,0:T(4,128)S(1)}, u32[]{:S(2)}, u32[]{:S(2)}) collective-permute-start(f32[3,4608]{1,0:T(4,128)S(1)} %select_maximum_fusion.part0), channel_id=1, source_target_pairs={{0,1},{1,0},{2,3},{3,2},{4,5},{5,4},{6,7},{7,6},{8,9},{9,8},{10,11... | collective-permute-start | bytes 165896 | tf_op jit(solution)/shard_map/cond/branch_1_fun/ppermute | solution.py:445
  43.2 21.5 %collective-permute-start.12 = (f32[192,512]{1,0:T(8,128)S(1)}, f32[192,512]{1,0:T(8,128)S(1)}, u32[]{:S(2)}, u32[]{:S(2)}) collective-permute-start(f32[192,512]{1,0:T(8,128)S(1)} %get-tuple-element.342.mixed0), channel_id=1, source_target_pairs={{0,1},{1,0},{2,3},{3,2},{4,5},{5,4},{6,7},{7,6},{8,9},{9,8},{10,11... | collective-permute-start | bytes 1179656 | tf_op jit(solution)/shard_map/cond/branch_1_fun/ppermute | solution.py:445
  44.2 12.7 %collective-permute-start.20 = (f32[4,24,768]{2,1,0:T(8,128)S(1)}, f32[4,24,768]{2,1,0:T(8,128)S(1)}, u32[]{:S(2)}, u32[]{:S(2)}) collective-permute-start(f32[4,24,768]{2,1,0:T(8,128)S(1)} %pad_maximum_fusion.refs_0_), channel_id=1, source_target_pairs={{0,24},{4,28},{8,16},{12,20},{16,8},{20,12},{24,0},{28,4},{1,25},{... | collective-permute-start | bytes 884744 | tf_op jit(solution)/shard_map/cond/branch_1_fun/ppermute | solution.py:445
  45.5 11.4 %collective-permute-start.21 = (f32[4,24,768]{2,1,0:T(8,128)S(1)}, f32[4,24,768]{2,1,0:T(8,128)S(1)}, u32[]{:S(2)}, u32[]{:S(2)}) collective-permute-start(f32[4,24,768]{2,1,0:T(8,128)S(1)} %pad_maximum_fusion.refs_0_), channel_id=1, source_target_pairs={{0,4},{4,0},{8,12},{12,8},{16,20},{20,16},{24,28},{28,24},{1,5},{5... | collective-permute-start | bytes 884744 | tf_op jit(solution)/shard_map/cond/branch_1_fun/ppermute | solution.py:445
  46.3 36.6 %collective-permute-start.13 = (f32[192,512]{1,0:T(8,128)S(1)}, f32[192,512]{1,0:T(8,128)S(1)}, u32[]{:S(2)}, u32[]{:S(2)}) collective-permute-start(f32[192,512]{1,0:T(8,128)S(1)} %get-tuple-element.342.mixed0), channel_id=1, source_target_pairs={{0,2},{1,3},{2,0},{3,1},{4,6},{5,7},{6,4},{7,5},{8,10},{9,11},{10,... | collective-permute-start | bytes 1179656 | tf_op jit(solution)/shard_map/cond/branch_1_fun/ppermute | solution.py:445
  47.1 35.8 %collective-permute-start.14 = (f32[192,512]{1,0:T(8,128)S(1)}, f32[192,512]{1,0:T(8,128)S(1)}, u32[]{:S(2)}, u32[]{:S(2)}) collective-permute-start(f32[192,512]{1,0:T(8,128)S(1)} %get-tuple-element.342.mixed0), channel_id=1, source_target_pairs={{0,3},{1,2},{2,1},{3,0},{4,7},{5,6},{6,5},{7,4},{8,11},{9,10},{10,... | collective-permute-start | bytes 1179656 | tf_op jit(solution)/shard_map/cond/branch_1_fun/ppermute | solution.py:445
  56.9 26.0 %collective-permute-start.22 = (f32[4,24,768]{2,1,0:T(8,128)S(1)}, f32[4,24,768]{2,1,0:T(8,128)S(1)}, u32[]{:S(2)}, u32[]{:S(2)}) collective-permute-start(f32[4,24,768]{2,1,0:T(8,128)S(1)} %collective-permute-done.18.refs_1_), channel_id=1, source_target_pairs={{0,4},{4,0},{8,12},{12,8},{16,20},{20,16},{24,28},{28,24},{1,5},{5... | collective-permute-start | bytes 884744 | tf_op jit(solution)/shard_map/cond/branch_1_fun/ppermute | solution.py:445
  56.9 26.0 %collective-permute-start.23 = (f32[4,24,768]{2,1,0:T(8,128)S(1)}, f32[4,24,768]{2,1,0:T(8,128)S(1)}, u32[]{:S(2)}, u32[]{:S(2)}) collective-permute-start(f32[4,24,768]{2,1,0:T(8,128)S(1)} %collective-permute-done.19.refs_2_), channel_id=1, source_target_pairs={{0,4},{4,0},{8,12},{12,8},{16,20},{20,16},{24,28},{28,24},{1,5},{5... | collective-permute-start | bytes 884744 | tf_op jit(solution)/shard_map/cond/branch_1_fun/ppermute | solution.py:445
  64.7 18.2 %collective-permute-start.24 = (f32[4,24,768]{2,1,0:T(8,128)S(1)}, f32[4,24,768]{2,1,0:T(8,128)S(1)}, u32[]{:S(2)}, u32[]{:S(2)}) collective-permute-start(f32[4,24,768]{2,1,0:T(8,128)S(1)} %collective-permute-done.20.refs_3_), channel_id=1, source_target_pairs={{0,4},{4,0},{8,12},{12,8},{16,20},{20,16},{24,28},{28,24},{1,5},{5... | collective-permute-start | bytes 884744 | tf_op jit(solution)/shard_map/cond/branch_1_fun/ppermute | solution.py:445
  93.0 88.5 %all-reduce.5.cloned.1.call-start = ((), (), s32[]{:S(2)}) async-start(), calls=%async_computation.1 | async-start | bytes 3145728 | tf_op jit(solution)/shard_map/psum | solution.py:611
  123.3 16.2 %collective-permute-start.26 = (f32[192,768]{1,0:T(8,128)S(1)}, f32[192,768]{1,0:T(8,128)S(1)}, u32[]{:S(2)}, u32[]{:S(2)}) collective-permute-start(f32[192,768]{1,0:T(8,128)S(1)} %get-tuple-element.139), channel_id=1, source_target_pairs={{0,8},{4,12},{8,0},{12,4},{16,24},{20,28},{24,16},{28,20},{1,9},{5... | collective-permute-start | bytes 1769480 | tf_op jit(solution)/shard_map/cond/branch_1_fun/ppermute | solution.py:445
  124.8 27.9 %collective-permute-start.27 = (f32[192,768]{1,0:T(8,128)S(1)}, f32[192,768]{1,0:T(8,128)S(1)}, u32[]{:S(2)}, u32[]{:S(2)}) collective-permute-start(f32[192,768]{1,0:T(8,128)S(1)} %get-tuple-element.140), channel_id=1, source_target_pairs={{0,16},{4,20},{8,24},{12,28},{16,0},{20,4},{24,8},{28,12},{1,17},{... | collective-permute-start | bytes 1769480 | tf_op jit(solution)/shard_map/cond/branch_1_fun/ppermute | solution.py:445
  125.6 27.1 %collective-permute-start.28 = (f32[192,768]{1,0:T(8,128)S(1)}, f32[192,768]{1,0:T(8,128)S(1)}, u32[]{:S(2)}, u32[]{:S(2)}) collective-permute-start(f32[192,768]{1,0:T(8,128)S(1)} %get-tuple-element.141), channel_id=1, source_target_pairs={{0,24},{4,28},{8,16},{12,20},{16,8},{20,12},{24,0},{28,4},{1,25},{... | collective-permute-start | bytes 1769480 | tf_op jit(solution)/shard_map/cond/branch_1_fun/ppermute | solution.py:445
  153.6 19.1 %collective-permute-start.29 = (f32[192,768]{1,0:T(8,128)}, f32[192,768]{1,0:T(8,128)}, u32[]{:S(2)}, u32[]{:S(2)}) collective-permute-start(f32[192,768]{1,0:T(8,128)} %add_add_fusion), channel_id=1, source_target_pairs={{0,8},{4,12},{8,0},{12,4},{16,24},{20,28},{24,16},{28,20},{1,9},{5... | collective-permute-start | bytes 1769480 | tf_op jit(solution)/shard_map/cond/branch_1_fun/ppermute | solution.py:445
  154.2 27.3 %collective-permute-start.30 = (f32[192,768]{1,0:T(8,128)}, f32[192,768]{1,0:T(8,128)}, u32[]{:S(2)}, u32[]{:S(2)}) collective-permute-start(f32[192,768]{1,0:T(8,128)} %add_add_fusion), channel_id=1, source_target_pairs={{0,16},{4,20},{8,24},{12,28},{16,0},{20,4},{24,8},{28,12},{1,17},{... | collective-permute-start | bytes 1769480 | tf_op jit(solution)/shard_map/cond/branch_1_fun/ppermute | solution.py:445
  155.7 25.9 %collective-permute-start.31 = (f32[192,768]{1,0:T(8,128)}, f32[192,768]{1,0:T(8,128)}, u32[]{:S(2)}, u32[]{:S(2)}) collective-permute-start(f32[192,768]{1,0:T(8,128)} %add_add_fusion), channel_id=1, source_target_pairs={{0,24},{4,28},{8,16},{12,20},{16,8},{20,12},{24,0},{28,4},{1,25},{... | collective-permute-start | bytes 1769480 | tf_op jit(solution)/shard_map/cond/branch_1_fun/ppermute | solution.py:445
  183.5 73.0 %all-reduce.7.cloned.1.call-start = ((), (), s32[]{:S(2)}) async-start(), calls=%async_computation.2 | async-start | bytes 3145728 | tf_op jit(solution)/shard_map/psum | solution.py:630
  187.2 49.9 %collective-permute-start = (f32[768,768]{1,0:T(8,128)S(1)}, f32[768,768]{1,0:T(8,128)}, u32[]{:S(2)}, u32[]{:S(2)}) collective-permute-start(f32[768,768]{1,0:T(8,128)S(1)} %place.2.mine), channel_id=1, source_target_pairs={{0,4},{4,0},{8,12},{12,8},{16,20},{20,16},{24,28},{28,24},{1,5},{5... | collective-permute-start | bytes 7077896 | tf_op jit(solution)/shard_map/cond/branch_1_fun/ppermute | solution.py:445
  215.7 10.2 %collective-permute-start.2 = (f32[96,768]{1,0:T(8,128)S(1)}, f32[96,768]{1,0:T(8,128)S(1)}, u32[]{:S(2)}, u32[]{:S(2)}) collective-permute-start(f32[96,768]{1,0:T(8,128)S(1)} %get-tuple-element.191), channel_id=1, source_target_pairs={{0,8},{4,12},{8,0},{12,4},{16,24},{20,28},{24,16},{28,20},{1,9},{5... | collective-permute-start | bytes 884744 | tf_op jit(solution)/shard_map/cond/branch_1_fun/ppermute | solution.py:445
  216.9 15.4 %collective-permute-start.3 = (f32[96,768]{1,0:T(8,128)S(1)}, f32[96,768]{1,0:T(8,128)}, u32[]{:S(2)}, u32[]{:S(2)}) collective-permute-start(f32[96,768]{1,0:T(8,128)S(1)} %get-tuple-element.192), channel_id=1, source_target_pairs={{0,16},{4,20},{8,24},{12,28},{16,0},{20,4},{24,8},{28,12},{1,17},{... | collective-permute-start | bytes 884744 | tf_op jit(solution)/shard_map/cond/branch_1_fun/ppermute | solution.py:445
  217.2 15.1 %collective-permute-start.4 = (f32[96,768]{1,0:T(8,128)S(1)}, f32[96,768]{1,0:T(8,128)}, u32[]{:S(2)}, u32[]{:S(2)}) collective-permute-start(f32[96,768]{1,0:T(8,128)S(1)} %get-tuple-element.193), channel_id=1, source_target_pairs={{0,24},{4,28},{8,16},{12,20},{16,8},{20,12},{24,0},{28,4},{1,25},{... | collective-permute-start | bytes 884744 | tf_op jit(solution)/shard_map/cond/branch_1_fun/ppermute | solution.py:445
  233.6 10.0 %collective-permute-start.5 = (f32[96,768]{1,0:T(8,128)S(1)}, f32[96,768]{1,0:T(8,128)S(1)}, u32[]{:S(2)}, u32[]{:S(2)}) collective-permute-start(f32[96,768]{1,0:T(8,128)S(1)} %add_add_fusion.1.refs_0_), channel_id=1, source_target_pairs={{0,8},{4,12},{8,0},{12,4},{16,24},{20,28},{24,16},{28,20},{1,9},{5... | collective-permute-start | bytes 884744 | tf_op jit(solution)/shard_map/cond/branch_1_fun/ppermute | solution.py:445
  234.5 12.9 %collective-permute-start.6 = (f32[96,768]{1,0:T(8,128)S(1)}, f32[96,768]{1,0:T(8,128)S(1)}, u32[]{:S(2)}, u32[]{:S(2)}) collective-permute-start(f32[96,768]{1,0:T(8,128)S(1)} %add_add_fusion.1.refs_0_), channel_id=1, source_target_pairs={{0,16},{4,20},{8,24},{12,28},{16,0},{20,4},{24,8},{28,12},{1,17},{... | collective-permute-start | bytes 884744 | tf_op jit(solution)/shard_map/cond/branch_1_fun/ppermute | solution.py:445
  235.7 12.8 %collective-permute-start.7 = (f32[96,768]{1,0:T(8,128)S(1)}, f32[96,768]{1,0:T(8,128)S(1)}, u32[]{:S(2)}, u32[]{:S(2)}) collective-permute-start(f32[96,768]{1,0:T(8,128)S(1)} %add_add_fusion.1.refs_0_), channel_id=1, source_target_pairs={{0,24},{4,28},{8,16},{12,20},{16,8},{20,12},{24,0},{28,4},{1,25},{... | collective-permute-start | bytes 884744 | tf_op jit(solution)/shard_map/cond/branch_1_fun/ppermute | solution.py:445
  (37 other events, 373.7 us)
Sparse Core Ops, SparseCore 0:
  12.3 99.7 all-gather.2
Sparse Core Ops, SparseCore 1:
  96.4 83.5 all-reduce.4
  186.4 66.5 all-reduce.6

commit v4 on v3

--- a/solution.py
+++ b/solution.py
@@ -171,7 +171,7 @@
             wide_ref[rows_at(start, share), :] = piece[k]
 
 
-def join_kernel(place, mixed0, mixed1, mixed2, mixed3, bias, inputs, mod, *refs):
+def join_kernel(place, mixed0, mixed1, mixed2, inner, outer, bias, inputs, mod, *refs):
     pieces, (attention_ref, middle_ref, entry_ref, low_ref, wide_ref, mixed_ref) = refs[:-6], refs[-6:]
 
     @pl.when(pl.program_id(0) == 0)
@@ -179,9 +179,10 @@
         put_in_order(place, pieces, wide_ref)
         low_ref[...] = wide_ref[...].astype(LOW)
 
-    for k, mixed in enumerate((mixed0, mixed1, mixed2, mixed3)):
-        columns = mixed.shape[0]
-        mixed_ref[rows_at((place[2] ^ k) * columns, columns, 16), :] = mixed[...].astype(LOW)
+    mixed = (mixed0[...], mixed1[...], mixed2[...], inner[...] + outer[...])
+    for k, part in enumerate(mixed):
+        columns = part.shape[0]
+        mixed_ref[rows_at((place[2] ^ k) * columns, columns, 16), :] = part.astype(LOW)
     attention = mm(mixed_ref[...], low_ref[...], TN) + bias[...].astype(FULL)
     attention_ref[...] = attention
     middle = inputs[...].astype(FULL) + mod[0, 2:3, :] * attention
@@ -195,7 +196,7 @@
     tokens, width = inputs.shape
     positions = tokens // images
     columns = mixed[0].shape[0]
-    rows = columns * len(mixed)
+    rows = columns * (len(mixed) - 1)
     by_image = pl.BlockSpec((positions, width), lambda g: (g, 0))
     specs = [pl.BlockSpec((columns, positions), lambda g: (0, g))] * len(mixed)
     specs += [pl.BlockSpec((1, width), lambda g: (0, 0)), by_image]
@@ -320,52 +321,50 @@
     )
 
 
-def end_kernel(branch_ref, bias_ref, middle_ref, upstream_ref, mod_ref, out_ref, sums_ref):
+def end_kernel(branch_ref, bias_ref, middle_ref, mod_ref, out_ref):
     branch = branch_ref[...] + bias_ref[...].astype(FULL)
     out_ref[...] = (middle_ref[...] + mod_ref[0, 5:6, :] * branch).astype(LOW)
-    sums_ref[0] = jnp.sum(upstream_ref[...].astype(FULL) * branch, axis=0, keepdims=True)
-
-
-def end_forward(branch, bias, middle, upstream, modulation):
+
+
+def end_forward(branch, bias, middle, modulation):
     images = modulation.shape[0]
     tokens, width = middle.shape
     by_image = pl.BlockSpec((tokens // images, width), lambda g: (g, 0))
     return call(
         end_kernel,
         "end_forward",
-        (shape((tokens, width), LOW), shape((images, 1, width))),
-        (branch, bias, middle, upstream, modulation),
+        shape((tokens, width), LOW),
+        (branch, bias, middle, modulation),
         grid=(images,),
         specs=[
             by_image,
             pl.BlockSpec((1, width), lambda g: (0, 0)),
             by_image,
-            by_image,
             pl.BlockSpec((1, 6, width), lambda g: (g, 0, 0)),
         ],
-        out_specs=(by_image, pl.BlockSpec((1, 1, width), lambda g: (g, 0, 0))),
+        out_specs=by_image,
     )
 
 
 def modulator_kernel(every_ref, context_ref, out_ref, sums_ref):
     part = every_ref[...]
     sums_ref[...] = jnp.sum(part, axis=0, keepdims=True)
-    out_ref[...] = mm(context_ref[...].astype(LOW), part.astype(LOW), TN)
-
-
-def modulator_backward(every, context, width):
+    context = context_ref[:, : out_ref.shape[0]].astype(LOW)
+    out_ref[...] = mm(context, part.astype(LOW), TN)
+
+
+def modulator_backward(every, rows, context_width, width):
     images = every.shape[0]
-    total = every.shape[1]
-    rows = context.shape[1]
+    at = 6 * width // context_width
     return call(
         modulator_kernel,
         "modulator_backward",
-        (shape((rows, total)), shape((1, total))),
-        (every, context),
-        grid=(total // width,),
+        (shape((rows, 6 * width)), shape((1, 6 * width))),
+        (every, every),
+        grid=(6,),
         specs=[
             pl.BlockSpec((images, width), lambda p: (0, p)),
-            pl.BlockSpec((images, rows), lambda p: (0, 0)),
+            pl.BlockSpec((images, context_width), lambda p: (0, at)),
         ],
         out_specs=(
             pl.BlockSpec((rows, width), lambda p: (0, p)),
@@ -432,43 +431,62 @@
             base, at = base + CHIPS * share, at + share
 
 
-def whole_kernel(shares, place, mine, other, *outs):
-    base = 0
+def whole_kernel(shares, place, mine, other, *refs):
+    outs, sems = refs[:-1], refs[-1]
+    base, copies = 0, []
     for share, out in zip(shares, outs):
         half = CHIPS * share
-        out[rows_at(place[0] * half, half), :] = mine[base : base + half, :]
-        out[rows_at((1 - place[0]) * half, half), :] = other[base : base + half, :]
+        for part, core in ((mine, place[0]), (other, 1 - place[0])):
+            target = out.at[rows_at(core * half, half), :]
+            source = part.at[pl.ds(base, half), :]
+            copies.append(pltpu.make_async_copy(source, target, sems.at[len(copies)]))
         base += half
+    for copy in copies:
+        copy.start()
+    for copy in copies:
+        copy.wait()
 
 
 def flip(value, axis, count, mask):
     return lax.ppermute(value, axis, [(i, i ^ mask) for i in range(count)])
 
 
-def sum_shares(place, away, kept, shares, n_dp, *others):
+def cut_shares(place, away, kept, shares, n_dp):
     other = flip(away, "dp", n_dp, 1)
     part = shape((sum(shares), kept.shape[1]))
-    parts = call(
+    return call(
         functools.partial(cut_kernel, shares), "cut", (part,) * CHIPS, (place, kept, other), smem=1
     )
+
+
+def sum_shares(parts, n_dp, *others):
     moved = [flip(parts[k], "dp", n_dp, 2 * k) for k in range(1, CHIPS)]
     total = (tie(parts[0], *others) if others else parts[0]) + moved[0] + moved[1] + moved[2]
     masks = [1 << i for i in range(3, n_dp.bit_length() - 1)]
-    return double(halve(total, n_dp, masks), n_dp, masks)
+    return double(halve(total, n_dp, masks), n_dp, masks), moved
 
 
 def spread_chips(share, n_dp):
     return [share] + [flip(share, "dp", n_dp, 2 * k) for k in range(1, CHIPS)]
 
 
-def spread_shares(place, parts, shares, n_dp):
-    width = parts[0].shape[1]
-    half = shape((CHIPS * sum(shares), width))
-    mine = call(functools.partial(place_kernel, shares), "place", half, (place, *parts), smem=1)
-    other = flip(mine, "dp", n_dp, 1)
-    outs = tuple(shape((GROUP * count, width)) for count in shares)
-    return call(
-        functools.partial(whole_kernel, shares), "whole", outs, (place, mine, other), smem=1
+def own_half(place, parts, shares):
+    half = shape((CHIPS * sum(shares), parts[0].shape[1]))
+    return call(functools.partial(place_kernel, shares), "place", half, (place, *parts), smem=1)
+
+
+def both_halves(place, mine, other, shares):
+    outs = tuple(shape((GROUP * count, mine.shape[1])) for count in shares)
+    anywhere = pl.BlockSpec(memory_space=pl.ANY)
+    return call(
+        functools.partial(whole_kernel, shares),
+        "whole",
+        outs,
+        (place, mine, other),
+        smem=1,
+        specs=[pl.BlockSpec(memory_space=pltpu.VMEM)] * 2,
+        out_specs=(anywhere,) * len(outs),
+        scratch=[pltpu.SemaphoreType.DMA((2 * len(outs),))],
     )
 
 
@@ -490,6 +508,23 @@
         lower = (index // mask) % 2 == 0
         value = jnp.concatenate([jnp.where(lower, value, other), jnp.where(lower, other, value)])
     return value
+
+
+def core_pair(rows, n_dp):
+    other = flip(rows, "dp", n_dp, 1)
+    first = lax.axis_index("dp") % 2 == 0
+    return jnp.concatenate([jnp.where(first, rows, other), jnp.where(first, other, rows)])
+
+
+def all_pairs(pair, n_dp):
+    if n_dp != GROUP:
+        pairs = lax.all_gather(pair, "dp").reshape(n_dp // 2, 2, *pair.shape)
+        return pairs[:, 0].reshape(-1, pair.shape[1])
+    chip = lax.axis_index("dp") // 2
+    parts = [pair] + [flip(pair, "dp", n_dp, 2 * k) for k in range(1, CHIPS)]
+    for bit in (1, 2):
+        parts = [jnp.where(chip & bit != 0, parts[k ^ bit], parts[k]) for k in range(CHIPS)]
+    return jnp.concatenate(parts)
 
 
 def gather_rows(rows, n_dp):
@@ -577,7 +612,7 @@
             bias_row = jnp.pad(bias_row, ((0, 0), (0, partial.shape[1] - bias_row.shape[1])))
             shared = jnp.concatenate([partial, bias_row])
             shared = [shared] + [flip(shared, "tensor", n_tensor, k) for k in range(1, n_tensor)]
-            return call(
+            results = call(
                 start_kernel,
                 "start",
                 (
@@ -588,10 +623,15 @@
                 ),
                 (*shared, modulator_bias[None], inputs, weight_t, bias_own),
             )
+            return results, shared
 
         output_parts = gather_z(attn_output, n_tensor)
-        mixed_t, entry_one, modulation, bias_full = start(context_low)
-        mixed = [mixed_t] + [flip(mixed_t, "tensor", n_tensor, k) for k in range(1, n_tensor)]
+        (mixed_t, entry_one, modulation, bias_full), shared = start(context_low)
+        output_parts = [tie(x, shared[-1]) for x in output_parts]
+        near, far = (flip(mixed_t, "tensor", n_tensor, k) for k in (1, 2))
+        inner = lax.ppermute(mixed_t, "tensor", [(1, 2), (2, 1)])
+        outer = lax.ppermute(far, "tensor", [(1, 0), (2, 3)])
+        mixed = [mixed_t, near, far, inner, outer]
         output_pieces = gather_pieces(output_parts, n_dp)
         attention, middle, entry_two, output_full = join_heads(
             place, mixed, output_pieces, attn_output_bias[None], inputs, modulation
@@ -611,26 +651,40 @@
     entry_two_grad = lax.psum(part, "tensor")
     mlp_shares = (ffn_output.shape[0] // GROUP, features // GROUP)
 
-    def beside_entry_two(place, weight_wide, mlp):
+    def beside_entry_two(place, mlp):
         active, branch_grad, entry_two, hidden_grad = mlp
         away, kept = mlp_grads(place, active, branch_grad, entry_two, hidden_grad)
-        share = sum_shares(place, away, kept, mlp_shares, n_dp)
+        mlp_share = sum_shares(cut_shares(place, away, kept, mlp_shares, n_dp), n_dp)[0]
+        branch_part = mm(active, ffn_output)
+        weights = cotangent.astype(FULL)
+        gate_part = jnp.sum(weights * branch_part.reshape(latents.shape), axis=1)
+        parts = [gate_part] + [flip(gate_part, "tensor", n_tensor, k) for k in range(1, n_tensor)]
+        gate_grad = (parts[0] + parts[1]) + (parts[2] + parts[3])
+        gate_grad = gate_grad + ffn_output_bias.astype(FULL) * jnp.sum(weights, axis=1)
+        sums = [jnp.sum(x.astype(FULL), axis=0) for x in (branch_grad, hidden_grad)]
+        return mlp_share, branch_part, gate_grad, sums
+
+    mlp_share, branch_part, gate_two_grad, mlp_sums = as_one(
+        beside_entry_two, tie(place, part), mlp
+    )
+
+    def still_beside_entry_two(weight_wide, mlp_share):
+        mlp_parts = spread_chips(mlp_share, n_dp)
         proj_full, weight_full = project_all(weight_wide, bias_full, entry_one)
-        mlp_parts = spread_chips(share, n_dp)
-        probs = all_probs(proj_full, image_count)
-        branch_part = mm(active, ffn_output)
-        sums = [jnp.sum(x.astype(FULL), axis=0) for x in (branch_grad, hidden_grad)]
-        return mlp_parts, probs, proj_full, weight_full, branch_part, sums
-
-    mlp_parts, probs, proj_full, weight_full, branch_part, mlp_sums = as_one(
-        beside_entry_two, tie(place, part), weight_wide, mlp
-    )
+        return mlp_parts, all_probs(proj_full, image_count), proj_full, weight_full
+
+    mlp_parts, probs, proj_full, weight_full = as_one(
+        still_beside_entry_two, tie(weight_wide, branch_part), mlp_share
+    )
+    entry_two_grad = tie(entry_two_grad, probs)
     entry_two_grad = tie(entry_two_grad, branch_part)
     branch_part = tie(branch_part, entry_two_grad)
     branch = lax.psum(branch_part, "tensor")
     attn_shares = (3 * columns // GROUP, columns // GROUP)
 
-    def beside_branch(entry_two_grad, probs, proj_full, weight_full, mlp_parts):
+    def beside_branch(
+        entry_two_grad, probs, proj_full, weight_full, gate_two_grad, mlp_sums, mlp_parts
+    ):
         def heads(entry_two_grad, probs, proj_full):
             middle_grad, attention_grad, mixed_grad_t, middle_sums = middle_backward(
                 entry_two_grad, middle, attention, upstream, modulation, output_full
@@ -642,42 +696,69 @@
         middle_grad, middle_sums, proj_grad, (away, kept, own_sums) = as_one(
             heads, entry_two_grad, probs, proj_full
         )
-        latents_grad, entry_sums = entry_backward(
-            proj_grad.reshape(-1, tokens),
-            weight_full.reshape(-1, features),
-            inputs,
-            middle_grad,
-            modulation,
+        parts = cut_shares(place, away, kept, attn_shares, n_dp)
+
+        def entry(proj_grad, weight_full, middle_grad):
+            return entry_backward(
+                proj_grad.reshape(-1, tokens),
+                weight_full.reshape(-1, features),
+                inputs,
+                middle_grad,
+                modulation,
+            )
+
+        latents_grad, entry_sums = as_one(
+            entry, tie(proj_grad, parts[0]), weight_full, middle_grad
         )
-        attn_share = sum_shares(place, away, kept, attn_shares, n_dp, latents_grad)
-        mlp_whole = spread_shares(place, mlp_parts, mlp_shares, n_dp)
-        attn_parts = spread_chips(attn_share, n_dp)
-        attn_parts[0] = tie(attn_parts[0], *mlp_whole)
-        attn_whole = spread_shares(place, attn_parts, attn_shares, n_dp)
-        return mlp_whole, attn_whole, latents_grad, entry_sums, own_sums, middle_sums
-
-    mlp_whole, attn_whole, latents_grad, entry_sums, own_sums, middle_sums = as_one(
-        beside_branch, tie(entry_two_grad, branch_part), probs, proj_full, weight_full, mlp_parts
-    )
-    layer_out, gate_two_grad = end_forward(
-        tie(branch, entry_sums), ffn_output_bias[None], middle, upstream, modulation
-    )
-    modulation_grad = jnp.concatenate([entry_sums, middle_sums[:, :3], gate_two_grad], axis=1)
-    modulation_grad = modulation_grad.reshape(image_count, -1).astype(LOW)
-    context_grad = mm(modulation_grad, modulator, NT)
-    condition_grad = jax.vjp(jax.nn.silu, cond_float)[1](context_grad)[0]
-
-    sums = [mlp_sums[0], mlp_sums[1], jnp.sum(middle_sums[:, 3], axis=0), own_sums[0]]
-    sizes = [part.shape[0] for part in sums]
-    sums = jnp.pad(jnp.concatenate(sums)[None], ((0, image_count - 1), (0, 0)))
-    small = [modulation_grad.astype(FULL), sums, context_low.astype(FULL)]
-    every = lax.all_gather(jnp.concatenate(small, axis=1), "dp", tiled=True)
-    every_rows = 6 * features
-    context_at = every_rows + sum(sizes)
-    grad_modulator, grad_modulator_bias = modulator_backward(
-        every[:, :every_rows], every[:, context_at:], features
-    )
-    sums = jnp.split(jnp.sum(every[:, every_rows:context_at], axis=0), [sum(sizes[:i]) for i in (1, 2, 3)])
+        mlp_mine = own_half(place, [tie(mlp_parts[0], away), *mlp_parts[1:]], mlp_shares)
+        mlp_other = flip(mlp_mine, "dp", n_dp, 1)
+        modulation_grad = jnp.concatenate(
+            [entry_sums, middle_sums[:, :3], gate_two_grad[:, None]], axis=1
+        )
+        modulation_grad = modulation_grad.reshape(image_count, -1).astype(LOW)
+        attn_share, moved = sum_shares(parts, n_dp, entry_sums)
+        sums = [mlp_sums[0], mlp_sums[1], jnp.sum(middle_sums[:, 3], axis=0), own_sums[0]]
+        sizes = [x.shape[0] for x in sums]
+        sums = jnp.pad(jnp.concatenate(sums)[None], ((0, image_count - 1), (0, 0)))
+        context_wide = jnp.pad(context_low.astype(FULL), ((0, 0), (0, -context_low.shape[1] % 256)))
+        small = [modulation_grad.astype(FULL), context_wide, sums]
+        pair = core_pair(tie(jnp.concatenate(small, axis=1), *moved), n_dp)
+        every = all_pairs(pair, n_dp)
+        attn_parts = spread_chips(tie(attn_share, pair), n_dp)
+
+        def finish(every, modulation_grad, mlp_mine, mlp_other):
+            grad_modulator, grad_modulator_bias = modulator_backward(
+                every, context_low.shape[1], context_wide.shape[1], features
+            )
+            sums = jnp.sum(every[:, 6 * features + context_wide.shape[1] :], axis=0)
+            sums = jnp.split(sums, [sum(sizes[:i]) for i in (1, 2, 3)])
+            context_grad = mm(modulation_grad, modulator, NT)
+            condition_grad = jax.vjp(jax.nn.silu, cond_float)[1](context_grad)[0]
+            mlp_whole = both_halves(place, mlp_mine, mlp_other, mlp_shares)
+            return (grad_modulator, grad_modulator_bias), sums, condition_grad, mlp_whole
+
+        modulator_grads, sums, condition_grad, mlp_whole = as_one(
+            finish, every, modulation_grad, mlp_mine, mlp_other
+        )
+        attn_parts[0] = tie(attn_parts[0], condition_grad)
+        attn_mine = own_half(place, attn_parts, attn_shares)
+        attn_whole = both_halves(place, attn_mine, flip(attn_mine, "dp", n_dp, 1), attn_shares)
+        return mlp_whole, attn_whole, latents_grad, condition_grad, modulator_grads, sums
+
+    mlp_whole, attn_whole, latents_grad, condition_grad, modulator_grads, sums = as_one(
+        beside_branch,
+        tie(entry_two_grad, branch_part),
+        probs,
+        proj_full,
+        weight_full,
+        gate_two_grad,
+        mlp_sums,
+        mlp_parts,
+    )
+    grad_modulator, grad_modulator_bias = modulator_grads
+    layer_out = end_forward(
+        tie(branch, condition_grad), ffn_output_bias[None], middle, modulation
+    )
     input_bias = sums[3].reshape(3, columns)
     return (
         layer_out.reshape(latents.shape),

time: 288 us -> 274 us (0.951)
  waiting for transfers between devices: 117 us -> 93.3 us
  blocking collectives: 9.77 us -> 0 us
  other arithmetic: 14.2 us -> 19.8 us
  starting transfers between devices: 33.5 us -> 39.1 us
  local copies, waits for them, and re-layouts: 15.3 us -> 20.5 us
    ppermute x32 -> x38, waiting for transfers between devices: 98.1 us -> 70.6 us  [flip(): return lax.ppermute(value, axis, [(i, i ^ mask) for i in range(count)])]
    ppermute x0 -> x2, waiting for transfers between devices: none -> 22.4 us  [the longest x1 22.4 us: forward(): outer = lax.ppermute(far, 'tensor', [(1, 0), (2, 3)])]
    all_gather x1, waiting for transfers between devices: 18 us -> 0.01 us  [gather_rows(): return lax.all_gather(mine.astype(FULL), ('tensor', 'dp'), tiled=True)]
    all_gather x1 -> x0, blocking collectives: 9.77 us -> none  [per_device(): every = lax.all_gather(jnp.concatenate(small, axis=1), 'dp', tiled=True)]
    cond x50 -> x78, local copies, waits for them, and re-layouts: 4.28 us -> 9.9 us
    ppermute x32 -> x38, starting transfers between devices: 33.2 us -> 36.6 us  [flip(): return lax.ppermute(value, axis, [(i, i ^ mask) for i in range(count)])]
    unnamed x23 -> x15, local copies, waits for them, and re-layouts: 6.36 us -> 4.86 us
  transfers between devices with their start and end apart: 35 -> 43, of which waited for: 19 -> 17; matrix products, arithmetic and copies ran while one was open for 9% -> 14% of each run, Pallas kernels for 22% -> 25%
where the time goes in v4:
time: 274 us; the launch traced here: 272 us
  waiting for transfers between devices  93.3 us (34%)
  Pallas kernels  71.5 us (26%)
  starting transfers between devices  39.1 us (14%)
  local copies, waits for them, and re-layouts  20.5 us (7%)
  other arithmetic  19.8 us (7%)
  between operations  15.6 us (6%)
  matrix products  11.8 us (4%)
    pallas_call x17, Pallas kernels, call(): pl.pallas_call(kernel, out_shape=out_shape, in_specs=in_specs, out_specs=...  71.5 us
    ppermute x38, waiting for transfers between devices, flip(): return lax.ppermute(value, axis, [(i, i ^ mask) for i in range(count)])  70.6 us
    ppermute x38, starting transfers between devices, flip(): return lax.ppermute(value, axis, [(i, i ^ mask) for i in range(count)])  36.6 us
    ppermute x1, waiting for transfers between devices, forward(): outer = lax.ppermute(far, 'tensor', [(1, 0), (2, 3)])  22.4 us
    dot_general x6, matrix products, mm(): return lax.dot_general(left, right, dims, preferred_element_type=FULL)  11.8 us
    cond x78, local copies, waits for them, and re-layouts  9.9 us
  transfers between devices with their start and end apart: 43, of which 17 were waited for; matrix products, arithmetic and copies ran while one was open for 14% of the time, Pallas kernels for 25%

profile of v4, /device:TPU:0, one launch (start us, length us, event | category | flops | bytes accessed | tf_op | source)
XLA Modules:
  0.0 272.3 jit_solution(9239939424490923464)
XLA Ops:
  11.6 97.2 %conditional.7 = (f32[192,512]{1,0:T(8,128)S(1)}, bf16[512,768]{1,0:T(8,128)(2,1)S(1)}, f32[2,6,768]{2,1,0:T(8,128)}, f32[3,768]{1,0:T(4,128)S(1)}, f32[512,768]...) conditional(s32[]{:T(128)} %convert_element_type.67, () %tuple.83, ...), branch_computations={%region_0.1_spmd, %region_1.2_spmd} | conditional | flops 1825987840 | bytes 56038192 | solution.py:568
  14.6 5.2 %collective-permute-start.5 = (f32[3,4608]{1,0:T(4,128)S(1)}, f32[3,4608]{1,0:T(4,128)S(1)}, u32[]{:S(2)}, u32[]{:S(2)}) collective-permute-start(f32[3,4608]{1,0:T(4,128)S(1)} %select_maximum_fusion.part0), channel_id=1, source_target_pairs={{0,3},{1,2},{2,1},{3,0},{4,7},{5,6},{6,5},{7,4},{8,11},{9,10},{10,... | collective-permute-start | bytes 165896 | tf_op jit(solution)/shard_map/cond/branch_1_fun/ppermute | solution.py:451
  21.2 3.8 %collective-permute-start.12 = (f32[24,768]{1,0:T(8,128)S(1)}, f32[24,768]{1,0:T(8,128)S(1)}, u32[]{:S(2)}, u32[]{:S(2)}) collective-permute-start(f32[24,768]{1,0:T(8,128)S(1)} %dynamic-slice_convert_fusion.refs_0_), channel_id=1, source_target_pairs={{0,3},{1,2},{2,1},{3,0},{4,7},{5,6},{6,5},{7,4},{8,11},{9,10},{10,... | collective-permute-start | bytes 221192 | tf_op jit(solution)/shard_map/cond/branch_1_fun/ppermute | solution.py:451
  25.6 5.3 %collective-permute-done.3.part1 = f32[3,4608]{1,0:T(4,128)S(1)} collective-permute-done((f32[3,4608]{1,0:T(4,128)S(1)}, f32[3,4608]{1,0:T(4,128)S(1)}, u32[]{:S(2)}, u32[]{:S(2)}) %collective-permute-start.3) | collective-permute-done | bytes 55328 | tf_op jit(solution)/shard_map/cond/branch_1_fun/ppermute | solution.py:451
  30.9 6.6 %collective-permute-done.4.part2 = f32[3,4608]{1,0:T(4,128)S(1)} collective-permute-done((f32[3,4608]{1,0:T(4,128)S(1)}, f32[3,4608]{1,0:T(4,128)S(1)}, u32[]{:S(2)}, u32[]{:S(2)}) %collective-permute-start.4) | collective-permute-done | bytes 55328 | tf_op jit(solution)/shard_map/cond/branch_1_fun/ppermute | solution.py:451
  37.5 4.8 %start.1 = (f32[192,512]{1,0:T(8,128)S(1)}, bf16[512,768]{1,0:T(8,128)(2,1)S(1)}, f32[2,6,768]{2,1,0:T(8,128)}, f32[3,768]{1,0:T(4,128)S(1)}) custom-call(f32[3,4608]{1,0:T(4,128)S(1)} %select_maximum_fusion.part0, f32[3,4608]{1,0:T(4,128)S(1)} %collective-permute-done.3.part1, f32[3,4608]{1,0:T(4,128)S(1)} %collective-permute-done.4.part2, ...), custom_call_target="tpu_custom_call" | custom-call | tf_op jit(solution)/shard_map/cond/branch_1_fun/start/pallas_call | solution.py:55
  51.7 7.9 %collective-permute-done.13.refs_1_ = f32[4,24,768]{2,1,0:T(8,128)S(1)} collective-permute-done((f32[4,24,768]{2,1,0:T(8,128)S(1)}, f32[4,24,768]{2,1,0:T(8,128)S(1)}, u32[]{:S(2)}, u32[]{:S(2)}) %collective-permute-start.13) | collective-permute-done | bytes 294944 | tf_op jit(solution)/shard_map/cond/branch_1_fun/ppermute | solution.py:451
  61.1 9.8 %collective-permute-done.7.mixed2 = f32[192,512]{1,0:T(8,128)S(1)} collective-permute-done((f32[192,512]{1,0:T(8,128)S(1)}, f32[192,512]{1,0:T(8,128)S(1)}, u32[]{:S(2)}, u32[]{:S(2)}) %collective-permute-start.7) | collective-permute-done | bytes 393248 | tf_op jit(solution)/shard_map/cond/branch_1_fun/ppermute | solution.py:451
  75.9 22.4 %collective-permute-done.9.outer = f32[192,512]{1,0:T(8,128)S(1)} collective-permute-done((f32[192,512]{1,0:T(8,128)S(1)}, f32[192,512]{1,0:T(8,128)S(1)}, u32[]{:S(2)}, u32[]{:S(2)}) %collective-permute-start.9) | collective-permute-done | bytes 393248 | tf_op jit(solution)/shard_map/cond/branch_1_fun/ppermute | solution.py:633
  98.3 4.3 %join_heads.1 = (f32[512,768]{1,0:T(8,128)}, f32[512,768]{1,0:T(8,128)}, bf16[512,768]{1,0:T(8,128)(2,1)}, bf16[768,768]{1,0:T(8,128)(2,1)}) custom-call(s32[3]{0:T(128)S(1)} %get-tuple-element.180.place, f32[192,512]{1,0:T(8,128)S(1)} %get-tuple-element.465.mixed0, f32[192,512]{1,0:T(8,128)S(1)} %collective-permute-done.6.mixed1, ...), custom_call_target="tpu_custom_call" | custom-call | tf_op jit(solution)/shard_map/cond/branch_1_fun/join_heads/pallas_call | solution.py:55
  102.6 4.1 %fusion.6 = (bf16[512,768]{1,0:T(8,128)(2,1)}, bf16[512,768]{1,0:T(8,128)(2,1)}) fusion(f32[512,768]{1,0:T(8,128)S(1)} %fusion.17, f32[768]{0:T(1024)S(1)} %convert_element_type.37, bf16[512,768]{1,0:T(8,128)(2,1)} %get-tuple-element.474, bf16[768,768]{1,0:T(8,128)(2,1)S(1)} %copy-done.41), kind=kOutput, calls=%fused_computation.8 | convolution fusion | flops 613023744 | bytes 5114880 | tf_op jit(solution)/shard_map/cond/branch_1_fun/dot_general | solution.py:23
  109.9 42.1 %conditional.8 = (f32[192,768]{1,0:T(8,128)}, f32[512,768]{1,0:T(8,128)S(1)}, bf16[2,768]{1,0:T(2,128)(2,1)}, f32[768]{0:T(1024)}, f32[768]{0:T(1024)}) conditional(s32[]{:T(128)} %convert_element_type.67, () %tuple.82, (s32[3]{0:T(128)}, bf16[512,768]{1,0:T(8,128)(2,1)}, bf16[512,768]{1,0:T(8,128)(2,1)S(1)}, bf16[512,768]{1,0:T(8,128)(2,1)}, ...), branch_computations={%region_2.3_spmd, %region_3.8_spmd} | conditional | flops 607573248 | bytes 42804220 | solution.py:568
  109.9 3.0 %mlp_grads.1 = (f32[768,768]{1,0:T(8,128)S(1)}, f32[768,768]{1,0:T(8,128)S(1)}) custom-call(s32[3]{0:T(128)} %get-tuple-element.191.place, bf16[512,768]{1,0:T(8,128)(2,1)} %get-tuple-element.192.active, bf16[512,768]{1,0:T(8,128)(2,1)S(1)} %get-tuple-element.193.branch_grad, bf16[512,768]{1,0:T(8,128)(2,1)} %get-tuple-element.194.entry, ...), custom_call_target="tpu_custom_call" | custom-call | tf_op jit(solution)/shard_map/cond/branch_1_fun/mlp_grads/pallas_call | solution.py:55
  113.1 4.5 %collective-permute-done.20.other = f32[768,768]{1,0:T(8,128)S(1)} collective-permute-done((f32[768,768]{1,0:T(8,128)S(1)}, f32[768,768]{1,0:T(8,128)S(1)}, u32[]{:S(2)}, u32[]{:S(2)}) %collective-permute-start.20) | collective-permute-done | bytes 2359328 | tf_op jit(solution)/shard_map/cond/branch_1_fun/ppermute | solution.py:451
  127.2 4.4 %collective-permute-done.24 = f32[2,768]{1,0:T(2,128)S(1)} collective-permute-done((f32[2,768]{1,0:T(2,128)S(1)}, f32[2,768]{1,0:T(2,128)S(1)}, u32[]{:S(2)}, u32[]{:S(2)}) %collective-permute-start.24) | collective-permute-done | bytes 6176 | tf_op jit(solution)/shard_map/cond/branch_1_fun/ppermute | solution.py:451
  133.6 3.8 %collective-permute-done.26 = f32[2,768]{1,0:T(2,128)S(1)} collective-permute-done((f32[2,768]{1,0:T(2,128)S(1)}, f32[2,768]{1,0:T(2,128)S(1)}, u32[]{:S(2)}, u32[]{:S(2)}) %collective-permute-start.26) | collective-permute-done | bytes 6176 | tf_op jit(solution)/shard_map/cond/branch_1_fun/ppermute | solution.py:451
  138.0 13.1 %collective-permute-done.22 = f32[192,768]{1,0:T(8,128)S(1)} collective-permute-done((f32[192,768]{1,0:T(8,128)S(1)}, f32[192,768]{1,0:T(8,128)S(1)}, u32[]{:S(2)}, u32[]{:S(2)}) %collective-permute-start.22) | collective-permute-done | bytes 589856 | tf_op jit(solution)/shard_map/cond/branch_1_fun/ppermute | solution.py:451
  152.0 28.7 %conditional.9 = (f32[192,768]{1,0:T(8,128)}, f32[192,768]{1,0:T(8,128)}, f32[192,768]{1,0:T(8,128)}, f32[192,768]{1,0:T(8,128)}, f32[2,12,256,256]{3,2,1,0:T(8,...) conditional(s32[]{:T(128)} %convert_element_type.67, () %tuple.86, (f32[192,768]{1,0:T(8,128)}, ...), branch_computations={%region_9.10_spmd, %region_10.11_spmd} | conditional | bytes 14549072 | solution.py:568
  157.5 8.5 %project_all.1 = (bf16[3,768,512]{2,1,0:T(8,128)(2,1)}, bf16[3,768,768]{2,1,0:T(8,128)(2,1)}) custom-call(f32[4,3,192,768]{3,2,1,0:T(8,128)} %get-tuple-element.206.weight_ref, f32[3,768]{1,0:T(4,128)S(1)} %get-tuple-element.207.bias, bf16[512,768]{1,0:T(8,128)(2,1)S(1)} %get-tuple-element.208.entry), custom_call_target="tpu_custom_call" | custom-call | tf_op jit(solution)/shard_map/cond/branch_1_fun/project_all/pallas_call | solution.py:55
  166.0 7.0 %all_probs.1 = f32[2,12,256,256]{3,2,1,0:T(8,128)} custom-call(bf16[3,768,512]{2,1,0:T(8,128)(2,1)} %get-tuple-element.499.proj_ref), custom_call_target="tpu_custom_call" | custom-call | tf_op jit(solution)/shard_map/cond/branch_1_fun/all_probs/pallas_call | solution.py:55
  173.0 7.7 %collective-permute-done.1 = f32[192,768]{1,0:T(8,128)} collective-permute-done((f32[192,768]{1,0:T(8,128)}, f32[192,768]{1,0:T(8,128)}, u32[]{:S(2)}, u32[]{:S(2)}) %collective-permute-start.1) | collective-permute-done | bytes 589856 | tf_op jit(solution)/shard_map/cond/branch_1_fun/ppermute | solution.py:451
  184.0 75.9 %conditional.10 = (f32[768,768]{1,0:T(8,128)}, f32[768,768]{1,0:T(8,128)}, f32[576,768]{1,0:T(8,128)}, f32[192,768]{1,0:T(8,128)}, f32[2,192]{1,0:T(2,128)}, /*i...) conditional(s32[]{:T(128)} %convert_element_type.67, () %tuple.88, ...), branch_computations={%region_12.13_spmd, %region_13.22_spmd} | conditional | flops 4658717 | bytes 68740384 | solution.py:568
  184.5 19.9 %conditional = (f32[512,768]{1,0:T(8,128)}, bf16[3,768,512]{2,1,0:T(8,128)(2,1)}, f32[384,768]{1,0:T(8,128)}, f32[384,768]{1,0:T(8,128)}, f32[768]{0:T(1024)S(1)...) conditional(s32[]{:T(128)} %convert_element_type.60, () %tuple.67, (bf16[2,256,768]{2,1,0:T(8,128)(2,1)}, ...), branch_computations={%region_14.14_spmd, %region_15.16_spmd} | conditional | flops 768 | bytes 6306128 | solution.py:568
  184.5 5.2 %middle_backward.2 = (f32[512,768]{1,0:T(8,128)}, bf16[512,768]{1,0:T(8,128)(2,1)S(1)}, bf16[768,512]{1,0:T(8,128)(2,1)S(1)}, f32[2,4,768]{2,1,0:T(4,128)S(1)}) custom-call(f32[512,768]{1,0:T(8,128)S(1)} %get-tuple-element.211.grad_ref, f32[512,768]{1,0:T(8,128)} %get-tuple-element.212.middle_ref, f32[512,768]{1,0:T(8,128)} %get-tuple-element.213.attention_ref, ...), custom_call_target="tpu_custom_call" | custom-call | tf_op jit(solution)/shard_map/cond/branch_1_fun/cond/branch_1_fun/middle_backward/pallas_call | solution.py:55
  189.7 10.7 %attention_backward.1.proj = bf16[3,768,512]{2,1,0:T(8,128)(2,1)} custom-call(f32[2,12,256,256]{3,2,1,0:T(8,128)} %get-tuple-element.218.probs_ref, bf16[3,768,512]{2,1,0:T(8,128)(2,1)} %get-tuple-element.219.proj_ref, bf16[768,512]{1,0:T(8,128)(2,1)S(1)} %get-tuple-element.220.grad_ref), custom_call_target="tpu_custom_call" | custom-call | tf_op jit(solution)/shard_map/cond/branch_1_fun/cond/branch_1_fun/attention_backward/pallas_call | solution.py:55
  200.4 3.9 %attn_grads.2 = (f32[384,768]{1,0:T(8,128)}, f32[384,768]{1,0:T(8,128)}, f32[8,576]{1,0:T(8,128)S(1)}) custom-call(s32[3]{0:T(128)S(1)} %get-tuple-element.221.place, bf16[3,768,512]{2,1,0:T(8,128)(2,1)} %attention_backward.1.proj, bf16[512,768]{1,0:T(8,128)(2,1)S(1)} %copy-done.8, f32[192,512]{1,0:T(8,128)S(1)} %get-tuple-element.223.mixed, ...), custom_call_target="tpu_custom_call" | custom-call | tf_op jit(solution)/shard_map/cond/branch_1_fun/cond/branch_1_fun/attn_grads/pallas_call | solution.py:55
  216.1 6.9 %conditional.1 = (f32[2,2,768]{2,1,0:T(2,128)}, f32[2,256,768]{2,1,0:T(8,128)}, bf16[2,2,768]{2,1,0:T(2,128)(2,1)S(1)}) conditional(s32[]{:T(128)} %convert_element_type.60, () %tuple.66, (bf16[3,768,512]{2,1,0:T(8,128)(2,1)}, bf16[3,768,768]{2,1,0:T(8,128)(2,1)}, bf16[512,768]{1,0:T(8,128)(2,1)S(1)}, f32[512,768]{1,0:T(8,128)S(1)}, ...), branch_computations={%region_17.17_spmd, %region_18.18_spmd} | conditional | flops 3072 | bytes 1591330 | solution.py:568
  216.1 6.2 %entry_backward.1 = (f32[512,768]{1,0:T(8,128)}, f32[2,2,768]{2,1,0:T(2,128)}) custom-call(bf16[2304,512]{1,0:T(8,128)(2,1)} %bitcast.7.proj_ref, bf16[2304,768]{1,0:T(8,128)(2,1)} %bitcast.8.weight_ref, bf16[512,768]{1,0:T(8,128)(2,1)S(1)} %get-tuple-element.231.inputs_ref, f32[512,768]{1,0:T(8,128)S(1)} %get-tuple-element.232.middle_grad_ref, ...), custom_call_target="tpu_custom_call" | custom-call | tf_op jit(solution)/shard_map/cond/branch_1_fun/cond/branch_1_fun/entry_backward/pallas_call | solution.py:55
  242.6 10.8 %conditional.2 = (f32[192,4608]{1,0:T(8,128)}, f32[768]{0:T(1024)}, f32[768]{0:T(1024)}, f32[768]{0:T(1024)}, f32[576]{0:T(1024)}, /*index=5*/f32[2,192]{1,0:T(2...) conditional(s32[]{:T(128)} %convert_element_type.60, () %tuple.65, (f32[16,7744]{1,0:T(8,128)S(1)}, ...), branch_computations={%region_19.19_spmd, %region_20.21_spmd} | conditional | flops 3585600 | bytes 9124712 | solution.py:568
  243.2 3.7 %modulator_backward.1 = (f32[192,4608]{1,0:T(8,128)}, f32[1,4608]{1,0:T(1,128)S(1)}) custom-call(f32[16,7744]{1,0:T(8,128)S(1)} %get-tuple-element.236.every_ref.context_ref, f32[16,7744]{1,0:T(8,128)S(1)} %get-tuple-element.236.every_ref.context_ref), custom_call_target="tpu_custom_call" | custom-call | tf_op jit(solution)/shard_map/cond/branch_1_fun/cond/branch_1_fun/modulator_backward/pallas_call | solution.py:55
  248.2 4.0 %whole.2 = (f32[768,768]{1,0:T(8,128)}, f32[768,768]{1,0:T(8,128)}) custom-call(s32[3]{0:T(128)S(1)} %get-tuple-element.241.place, f32[768,768]{1,0:T(8,128)S(1)} %get-tuple-element.242.mine, f32[768,768]{1,0:T(8,128)} %get-tuple-element.243.other), custom_call_target="tpu_custom_call" | custom-call | tf_op jit(solution)/shard_map/cond/branch_1_fun/cond/branch_1_fun/whole/pallas_call | solution.py:55
  255.0 2.8 %collective-permute-done.39.other = f32[384,768]{1,0:T(8,128)S(1)} collective-permute-done((f32[384,768]{1,0:T(8,128)S(1)}, f32[384,768]{1,0:T(8,128)S(1)}, u32[]{:S(2)}, u32[]{:S(2)}) %collective-permute-start.39) | collective-permute-done | bytes 1179680 | tf_op jit(solution)/shard_map/cond/branch_1_fun/ppermute | solution.py:451
  (241 shorter events, 93.5 us)
Async XLA Ops:
  8.0 144.0 %all-gather.2.cloned.1.call-start = ((), (), s32[]{:S(2)}) async-start(), calls=%async_computation.1 | async-start | bytes 7299072 | tf_op jit(solution)/shard_map/all_gather | solution.py:533
  14.6 10.4 %collective-permute-start.5 = (f32[3,4608]{1,0:T(4,128)S(1)}, f32[3,4608]{1,0:T(4,128)S(1)}, u32[]{:S(2)}, u32[]{:S(2)}) collective-permute-start(f32[3,4608]{1,0:T(4,128)S(1)} %select_maximum_fusion.part0), channel_id=1, source_target_pairs={{0,3},{1,2},{2,1},{3,0},{4,7},{5,6},{6,5},{7,4},{8,11},{9,10},{10,... | collective-permute-start | bytes 165896 | tf_op jit(solution)/shard_map/cond/branch_1_fun/ppermute | solution.py:451
  20.5 21.8 %collective-permute-start.10 = (f32[24,768]{1,0:T(8,128)S(1)}, f32[24,768]{1,0:T(8,128)S(1)}, u32[]{:S(2)}, u32[]{:S(2)}) collective-permute-start(f32[24,768]{1,0:T(8,128)S(1)} %dynamic-slice_convert_fusion.refs_0_), channel_id=1, source_target_pairs={{0,1},{1,0},{2,3},{3,2},{4,5},{5,4},{6,7},{7,6},{8,9},{9,8},{10,11... | collective-permute-start | bytes 221192 | tf_op jit(solution)/shard_map/cond/branch_1_fun/ppermute | solution.py:451
  20.6 22.4 %collective-permute-start.11 = (f32[24,768]{1,0:T(8,128)S(1)}, f32[24,768]{1,0:T(8,128)S(1)}, u32[]{:S(2)}, u32[]{:S(2)}) collective-permute-start(f32[24,768]{1,0:T(8,128)S(1)} %dynamic-slice_convert_fusion.refs_0_), channel_id=1, source_target_pairs={{0,2},{1,3},{2,0},{3,1},{4,6},{5,7},{6,4},{7,5},{8,10},{9,11},{10,... | collective-permute-start | bytes 221192 | tf_op jit(solution)/shard_map/cond/branch_1_fun/ppermute | solution.py:451
  21.2 22.5 %collective-permute-start.12 = (f32[24,768]{1,0:T(8,128)S(1)}, f32[24,768]{1,0:T(8,128)S(1)}, u32[]{:S(2)}, u32[]{:S(2)}) collective-permute-start(f32[24,768]{1,0:T(8,128)S(1)} %dynamic-slice_convert_fusion.refs_0_), channel_id=1, source_target_pairs={{0,3},{1,2},{2,1},{3,0},{4,7},{5,6},{6,5},{7,4},{8,11},{9,10},{10,... | collective-permute-start | bytes 221192 | tf_op jit(solution)/shard_map/cond/branch_1_fun/ppermute | solution.py:451
  25.0 12.5 %collective-permute-start.4 = (f32[3,4608]{1,0:T(4,128)S(1)}, f32[3,4608]{1,0:T(4,128)S(1)}, u32[]{:S(2)}, u32[]{:S(2)}) collective-permute-start(f32[3,4608]{1,0:T(4,128)S(1)} %select_maximum_fusion.part0), channel_id=1, source_target_pairs={{0,2},{1,3},{2,0},{3,1},{4,6},{5,7},{6,4},{7,5},{8,10},{9,11},{10,... | collective-permute-start | bytes 165896 | tf_op jit(solution)/shard_map/cond/branch_1_fun/ppermute | solution.py:451
  42.3 28.5 %collective-permute-start.7 = (f32[192,512]{1,0:T(8,128)S(1)}, f32[192,512]{1,0:T(8,128)S(1)}, u32[]{:S(2)}, u32[]{:S(2)}) collective-permute-start(f32[192,512]{1,0:T(8,128)S(1)} %get-tuple-element.465.mixed0), channel_id=1, source_target_pairs={{0,2},{1,3},{2,0},{3,1},{4,6},{5,7},{6,4},{7,5},{8,10},{9,11},{10,... | collective-permute-start | bytes 1179656 | tf_op jit(solution)/shard_map/cond/branch_1_fun/ppermute | solution.py:451
  45.4 14.1 %collective-permute-start.13 = (f32[4,24,768]{2,1,0:T(8,128)S(1)}, f32[4,24,768]{2,1,0:T(8,128)S(1)}, u32[]{:S(2)}, u32[]{:S(2)}) collective-permute-start(f32[4,24,768]{2,1,0:T(8,128)S(1)} %pad_maximum_fusion.refs_0_), channel_id=1, source_target_pairs={{0,8},{4,12},{8,0},{12,4},{16,24},{20,28},{24,16},{28,20},{1,9},{5... | collective-permute-start | bytes 884744 | tf_op jit(solution)/shard_map/cond/branch_1_fun/ppermute | solution.py:451
  47.0 13.4 %collective-permute-start.14 = (f32[4,24,768]{2,1,0:T(8,128)S(1)}, f32[4,24,768]{2,1,0:T(8,128)S(1)}, u32[]{:S(2)}, u32[]{:S(2)}) collective-permute-start(f32[4,24,768]{2,1,0:T(8,128)S(1)} %pad_maximum_fusion.refs_0_), channel_id=1, source_target_pairs={{0,16},{4,20},{8,24},{12,28},{16,0},{20,4},{24,8},{28,12},{1,17},{... | collective-permute-start | bytes 884744 | tf_op jit(solution)/shard_map/cond/branch_1_fun/ppermute | solution.py:451
  48.5 25.8 %collective-permute-start.6 = (f32[192,512]{1,0:T(8,128)S(1)}, f32[192,512]{1,0:T(8,128)S(1)}, u32[]{:S(2)}, u32[]{:S(2)}) collective-permute-start(f32[192,512]{1,0:T(8,128)S(1)} %get-tuple-element.465.mixed0), channel_id=1, source_target_pairs={{0,1},{1,0},{2,3},{3,2},{4,5},{5,4},{6,7},{7,6},{8,9},{9,8},{10,11... | collective-permute-start | bytes 1179656 | tf_op jit(solution)/shard_map/cond/branch_1_fun/ppermute | solution.py:451
  51.3 22.1 %collective-permute-start.15 = (f32[4,24,768]{2,1,0:T(8,128)S(1)}, f32[4,24,768]{2,1,0:T(8,128)S(1)}, u32[]{:S(2)}, u32[]{:S(2)}) collective-permute-start(f32[4,24,768]{2,1,0:T(8,128)S(1)} %pad_maximum_fusion.refs_0_), channel_id=1, source_target_pairs={{0,24},{4,28},{8,16},{12,20},{16,8},{20,12},{24,0},{28,4},{1,25},{... | collective-permute-start | bytes 884744 | tf_op jit(solution)/shard_map/cond/branch_1_fun/ppermute | solution.py:451
  59.5 14.0 %collective-permute-start.16 = (f32[4,24,768]{2,1,0:T(8,128)S(1)}, f32[4,24,768]{2,1,0:T(8,128)S(1)}, u32[]{:S(2)}, u32[]{:S(2)}) collective-permute-start(f32[4,24,768]{2,1,0:T(8,128)S(1)} %pad_maximum_fusion.refs_0_), channel_id=1, source_target_pairs={{0,4},{4,0},{8,12},{12,8},{16,20},{20,16},{24,28},{28,24},{1,5},{5... | collective-permute-start | bytes 884744 | tf_op jit(solution)/shard_map/cond/branch_1_fun/ppermute | solution.py:451
  60.4 14.8 %collective-permute-start.8 = (f32[192,512]{1,0:T(8,128)S(1)}, f32[192,512]{1,0:T(8,128)S(1)}, u32[]{:S(2)}, u32[]{:S(2)}) collective-permute-start(f32[192,512]{1,0:T(8,128)S(1)} %get-tuple-element.465.mixed0), channel_id=1, source_target_pairs={{1,2},{2,1},{5,6},{6,5},{9,10},{10,9},{13,14},{14,13},{17,18},{18,... | collective-permute-start | bytes 1179656 | tf_op jit(solution)/shard_map/cond/branch_1_fun/ppermute | solution.py:632
  70.8 27.5 %collective-permute-start.9 = (f32[192,512]{1,0:T(8,128)S(1)}, f32[192,512]{1,0:T(8,128)S(1)}, u32[]{:S(2)}, u32[]{:S(2)}) collective-permute-start(f32[192,512]{1,0:T(8,128)S(1)} %collective-permute-done.7.mixed2), channel_id=1, source_target_pairs={{1,0},{2,3},{5,4},{6,7},{9,8},{10,11},{13,12},{14,15},{17,16},{18,... | collective-permute-start | bytes 1179656 | tf_op jit(solution)/shard_map/cond/branch_1_fun/ppermute | solution.py:633
  108.8 71.9 %all-reduce.6.cloned.1.call-start = ((), (), s32[]{:S(2)}) async-start(), calls=%async_computation | async-start | bytes 3145728 | tf_op jit(solution)/shard_map/psum | solution.py:651
  121.1 16.9 %collective-permute-start.21 = (f32[192,768]{1,0:T(8,128)S(1)}, f32[192,768]{1,0:T(8,128)S(1)}, u32[]{:S(2)}, u32[]{:S(2)}) collective-permute-start(f32[192,768]{1,0:T(8,128)S(1)} %get-tuple-element.199), channel_id=1, source_target_pairs={{0,8},{4,12},{8,0},{12,4},{16,24},{20,28},{24,16},{28,20},{1,9},{5... | collective-permute-start | bytes 1769480 | tf_op jit(solution)/shard_map/cond/branch_1_fun/ppermute | solution.py:451
  122.6 28.4 %collective-permute-start.22 = (f32[192,768]{1,0:T(8,128)S(1)}, f32[192,768]{1,0:T(8,128)S(1)}, u32[]{:S(2)}, u32[]{:S(2)}) collective-permute-start(f32[192,768]{1,0:T(8,128)S(1)} %get-tuple-element.200), channel_id=1, source_target_pairs={{0,16},{4,20},{8,24},{12,28},{16,0},{20,4},{24,8},{28,12},{1,17},{... | collective-permute-start | bytes 1769480 | tf_op jit(solution)/shard_map/cond/branch_1_fun/ppermute | solution.py:451
  125.1 26.0 %collective-permute-start.23 = (f32[192,768]{1,0:T(8,128)S(1)}, f32[192,768]{1,0:T(8,128)S(1)}, u32[]{:S(2)}, u32[]{:S(2)}) collective-permute-start(f32[192,768]{1,0:T(8,128)S(1)} %get-tuple-element.201), channel_id=1, source_target_pairs={{0,24},{4,28},{8,16},{12,20},{16,8},{20,12},{24,0},{28,4},{1,25},{... | collective-permute-start | bytes 1769480 | tf_op jit(solution)/shard_map/cond/branch_1_fun/ppermute | solution.py:451
  152.0 21.0 %collective-permute-start = (f32[192,768]{1,0:T(8,128)}, f32[192,768]{1,0:T(8,128)}, u32[]{:S(2)}, u32[]{:S(2)}) collective-permute-start(f32[192,768]{1,0:T(8,128)} %get-tuple-element.494), channel_id=1, source_target_pairs={{0,8},{4,12},{8,0},{12,4},{16,24},{20,28},{24,16},{28,20},{1,9},{5... | collective-permute-start | bytes 1769480 | tf_op jit(solution)/shard_map/cond/branch_1_fun/ppermute | solution.py:451
  153.5 27.2 %collective-permute-start.1 = (f32[192,768]{1,0:T(8,128)}, f32[192,768]{1,0:T(8,128)}, u32[]{:S(2)}, u32[]{:S(2)}) collective-permute-start(f32[192,768]{1,0:T(8,128)} %get-tuple-element.494), channel_id=1, source_target_pairs={{0,16},{4,20},{8,24},{12,28},{16,0},{20,4},{24,8},{28,12},{1,17},{... | collective-permute-start | bytes 1769480 | tf_op jit(solution)/shard_map/cond/branch_1_fun/ppermute | solution.py:451
  154.1 26.6 %collective-permute-start.2 = (f32[192,768]{1,0:T(8,128)}, f32[192,768]{1,0:T(8,128)}, u32[]{:S(2)}, u32[]{:S(2)}) collective-permute-start(f32[192,768]{1,0:T(8,128)} %get-tuple-element.494), channel_id=1, source_target_pairs={{0,24},{4,28},{8,16},{12,20},{16,8},{20,12},{24,0},{28,4},{1,25},{... | collective-permute-start | bytes 1769480 | tf_op jit(solution)/shard_map/cond/branch_1_fun/ppermute | solution.py:451
  182.7 78.5 %all-reduce.8.cloned.1.call-start = ((), (), s32[]{:S(2)}) async-start(), calls=%async_computation.2 | async-start | bytes 3145728 | tf_op jit(solution)/shard_map/psum | solution.py:682
  210.9 14.3 %collective-permute-start.28 = (f32[96,768]{1,0:T(8,128)S(1)}, f32[96,768]{1,0:T(8,128)S(1)}, u32[]{:S(2)}, u32[]{:S(2)}) collective-permute-start(f32[96,768]{1,0:T(8,128)S(1)} %get-tuple-element.273), channel_id=1, source_target_pairs={{0,8},{4,12},{8,0},{12,4},{16,24},{20,28},{24,16},{28,20},{1,9},{5... | collective-permute-start | bytes 884744 | tf_op jit(solution)/shard_map/cond/branch_1_fun/ppermute | solution.py:451
  212.5 15.6 %collective-permute-start.29 = (f32[96,768]{1,0:T(8,128)S(1)}, f32[96,768]{1,0:T(8,128)}, u32[]{:S(2)}, u32[]{:S(2)}) collective-permute-start(f32[96,768]{1,0:T(8,128)S(1)} %get-tuple-element.274), channel_id=1, source_target_pairs={{0,16},{4,20},{8,24},{12,28},{16,0},{20,4},{24,8},{28,12},{1,17},{... | collective-permute-start | bytes 884744 | tf_op jit(solution)/shard_map/cond/branch_1_fun/ppermute | solution.py:451
  214.0 14.1 %collective-permute-start.30 = (f32[96,768]{1,0:T(8,128)S(1)}, f32[96,768]{1,0:T(8,128)}, u32[]{:S(2)}, u32[]{:S(2)}) collective-permute-start(f32[96,768]{1,0:T(8,128)S(1)} %get-tuple-element.275), channel_id=1, source_target_pairs={{0,24},{4,28},{8,16},{12,20},{16,8},{20,12},{24,0},{28,4},{1,25},{... | collective-permute-start | bytes 884744 | tf_op jit(solution)/shard_map/cond/branch_1_fun/ppermute | solution.py:451
  229.9 12.6 %collective-permute-start.35 = (f32[768,768]{1,0:T(8,128)S(1)}, f32[768,768]{1,0:T(8,128)}, u32[]{:S(2)}, u32[]{:S(2)}) collective-permute-start(f32[768,768]{1,0:T(8,128)S(1)} %place.2), channel_id=1, source_target_pairs={{0,4},{4,0},{8,12},{12,8},{16,20},{20,16},{24,28},{28,24},{1,5},{5... | collective-permute-start | bytes 7077896 | tf_op jit(solution)/shard_map/cond/branch_1_fun/ppermute | solution.py:451
  230.6 7.3 %collective-permute-start.32 = (f32[4,7744]{1,0:T(4,128)S(1)}, f32[4,7744]{1,0:T(4,128)}, u32[]{:S(2)}, u32[]{:S(2)}) collective-permute-start(f32[4,7744]{1,0:T(4,128)S(1)} %pad_maximum_fusion.3.refs_1_), channel_id=1, source_target_pairs={{0,24},{4,28},{8,16},{12,20},{16,8},{20,12},{24,0},{28,4},{1,25},{... | collective-permute-start | bytes 371720 | tf_op jit(solution)/shard_map/cond/branch_1_fun/ppermute | solution.py:451
  232.1 7.6 %collective-permute-start.33 = (f32[4,7744]{1,0:T(4,128)S(1)}, f32[4,7744]{1,0:T(4,128)}, u32[]{:S(2)}, u32[]{:S(2)}) collective-permute-start(f32[4,7744]{1,0:T(4,128)S(1)} %pad_maximum_fusion.3.refs_1_), channel_id=1, source_target_pairs={{0,16},{4,20},{8,24},{12,28},{16,0},{20,4},{24,8},{28,12},{1,17},{... | collective-permute-start | bytes 371720 | tf_op jit(solution)/shard_map/cond/branch_1_fun/ppermute | solution.py:451
  233.3 7.9 %collective-permute-start.34 = (f32[4,7744]{1,0:T(4,128)S(1)}, f32[4,7744]{1,0:T(4,128)}, u32[]{:S(2)}, u32[]{:S(2)}) collective-permute-start(f32[4,7744]{1,0:T(4,128)S(1)} %pad_maximum_fusion.3.refs_1_), channel_id=1, source_target_pairs={{0,8},{4,12},{8,0},{12,4},{16,24},{20,28},{24,16},{28,20},{1,9},{5... | collective-permute-start | bytes 371720 | tf_op jit(solution)/shard_map/cond/branch_1_fun/ppermute | solution.py:451
  236.1 17.2 %collective-permute-start.36 = (f32[96,768]{1,0:T(8,128)}, f32[96,768]{1,0:T(8,128)S(1)}, u32[]{:S(2)}, u32[]{:S(2)}) collective-permute-start(f32[96,768]{1,0:T(8,128)} %tie.25.refs_0_), channel_id=1, source_target_pairs={{0,8},{4,12},{8,0},{12,4},{16,24},{20,28},{24,16},{28,20},{1,9},{5... | collective-permute-start | bytes 884744 | tf_op jit(solution)/shard_map/cond/branch_1_fun/ppermute | solution.py:451
  237.9 15.4 %collective-permute-start.37 = (f32[96,768]{1,0:T(8,128)}, f32[96,768]{1,0:T(8,128)S(1)}, u32[]{:S(2)}, u32[]{:S(2)}) collective-permute-start(f32[96,768]{1,0:T(8,128)} %tie.25.refs_0_), channel_id=1, source_target_pairs={{0,16},{4,20},{8,24},{12,28},{16,0},{20,4},{24,8},{28,12},{1,17},{... | collective-permute-start | bytes 884744 | tf_op jit(solution)/shard_map/cond/branch_1_fun/ppermute | solution.py:451
  239.8 13.6 %collective-permute-start.38 = (f32[96,768]{1,0:T(8,128)}, f32[96,768]{1,0:T(8,128)S(1)}, u32[]{:S(2)}, u32[]{:S(2)}) collective-permute-start(f32[96,768]{1,0:T(8,128)} %tie.25.refs_0_), channel_id=1, source_target_pairs={{0,24},{4,28},{8,16},{12,20},{16,8},{20,12},{24,0},{28,4},{1,25},{... | collective-permute-start | bytes 884744 | tf_op jit(solution)/shard_map/cond/branch_1_fun/ppermute | solution.py:451
  (55 other events, 408.1 us)
Sparse Core Ops, SparseCore 0:
  12.3 91.8 all-gather.1
Sparse Core Ops, SparseCore 1:
  112.2 68.4 all-reduce.5
  185.5 67.8 all-reduce.7

commit v5 on v4

--- a/solution.py
+++ b/solution.py
@@ -76,15 +76,13 @@
 
 def start_kernel(
     part0, part1, part2, part3, mod_bias, latents, weight, bias,
-    mixed_ref, entry_ref, mod_ref, bias_ref,
+    mixed_ref, entry_ref, mod_ref,
 ):
     images, _, width = mod_ref.shape
     columns = weight.shape[1]
     positions = latents.shape[0] // images
     shared = (part0[...] + part1[...]) + (part2[...] + part3[...])
-    for j in range(3):
-        bias_ref[j : j + 1, :] = shared[images : images + 1, j * width : (j + 1) * width]
-    modulation = shared[:images] + mod_bias[...].astype(FULL)
+    modulation = shared + mod_bias[...].astype(FULL)
     for p in range(6):
         for g in range(images):
             mod_ref[g, p : p + 1, :] = modulation[g : g + 1, p * width : (p + 1) * width]
@@ -600,17 +598,13 @@
     cond_float = condition.astype(FULL)
     context_low = jax.nn.silu(cond_float).astype(LOW)
 
+    bias_own = jnp.stack(
+        [attn_input_bias[0], jnp.zeros_like(attn_input_bias[0]), attn_input_bias[1]]
+    )
+
     def forward(context_low):
         def start(context_low):
-            partial = mm(context_low, modulator)
-            bias_own = jnp.stack(
-                [attn_input_bias[0], jnp.zeros_like(attn_input_bias[0]), attn_input_bias[1]]
-            )
-            bias_row = jnp.zeros((3, n_tensor * columns), FULL)
-            bias_row = lax.dynamic_update_slice_in_dim(bias_row, bias_own.astype(FULL), z * columns, 1)
-            bias_row = bias_row.reshape(1, -1)
-            bias_row = jnp.pad(bias_row, ((0, 0), (0, partial.shape[1] - bias_row.shape[1])))
-            shared = jnp.concatenate([partial, bias_row])
+            shared = mm(context_low, modulator)
             shared = [shared] + [flip(shared, "tensor", n_tensor, k) for k in range(1, n_tensor)]
             results = call(
                 start_kernel,
@@ -619,14 +613,13 @@
                     shape((columns, tokens)),
                     shape((tokens, features), LOW),
                     shape((image_count, 6, features)),
-                    shape((3, n_tensor * columns)),
                 ),
                 (*shared, modulator_bias[None], inputs, weight_t, bias_own),
             )
             return results, shared
 
         output_parts = gather_z(attn_output, n_tensor)
-        (mixed_t, entry_one, modulation, bias_full), shared = start(context_low)
+        (mixed_t, entry_one, modulation), shared = start(context_low)
         output_parts = [tie(x, shared[-1]) for x in output_parts]
         near, far = (flip(mixed_t, "tensor", n_tensor, k) for k in (1, 2))
         inner = lax.ppermute(mixed_t, "tensor", [(1, 2), (2, 1)])
@@ -643,11 +636,11 @@
         branch_grad = (gate_two * cotangent.astype(FULL)).astype(LOW).reshape(tokens, features)
         hidden_grad = gelu_pull(mm(branch_grad, ffn_output, NT))[0].astype(LOW)
         part = mm(hidden_grad, ffn_input, NT)
-        first = mixed_t, entry_one, modulation, bias_full, attention, middle, output_full
+        first = mixed_t, entry_one, modulation, attention, middle, output_full
         return first, (active, branch_grad, entry_two, hidden_grad), part
 
     first, mlp, part = as_one(forward, context_low)
-    mixed_t, entry_one, modulation, bias_full, attention, middle, output_full = first
+    mixed_t, entry_one, modulation, attention, middle, output_full = first
     entry_two_grad = lax.psum(part, "tensor")
     mlp_shares = (ffn_output.shape[0] // GROUP, features // GROUP)
 
@@ -658,13 +651,16 @@
         branch_part = mm(active, ffn_output)
         weights = cotangent.astype(FULL)
         gate_part = jnp.sum(weights * branch_part.reshape(latents.shape), axis=1)
-        parts = [gate_part] + [flip(gate_part, "tensor", n_tensor, k) for k in range(1, n_tensor)]
-        gate_grad = (parts[0] + parts[1]) + (parts[2] + parts[3])
-        gate_grad = gate_grad + ffn_output_bias.astype(FULL) * jnp.sum(weights, axis=1)
+        bias_row = jnp.zeros((3, n_tensor * columns), FULL)
+        bias_row = lax.dynamic_update_slice_in_dim(bias_row, bias_own.astype(FULL), z * columns, 1)
+        part = jnp.concatenate([gate_part, bias_row])
+        parts = [part] + [flip(part, "tensor", n_tensor, k) for k in range(1, n_tensor)]
+        part = (parts[0] + parts[1]) + (parts[2] + parts[3])
+        gate_grad = part[:image_count] + ffn_output_bias.astype(FULL) * jnp.sum(weights, axis=1)
         sums = [jnp.sum(x.astype(FULL), axis=0) for x in (branch_grad, hidden_grad)]
-        return mlp_share, branch_part, gate_grad, sums
-
-    mlp_share, branch_part, gate_two_grad, mlp_sums = as_one(
+        return mlp_share, branch_part, gate_grad, part[image_count:], sums
+
+    mlp_share, branch_part, gate_two_grad, bias_full, mlp_sums = as_one(
         beside_entry_two, tie(place, part), mlp
     )
 

time: 274 us -> 264 us (0.964)
  local copies, waits for them, and re-layouts: 20.5 us -> 14.4 us
  waiting for transfers between devices: 93.3 us -> 89 us
  other arithmetic: 19.8 us -> 15.8 us
  starting transfers between devices: 39.1 us -> 42.2 us
    cond x78 -> x65, local copies, waits for them, and re-layouts: 9.9 us -> 5.43 us
    ppermute x1, waiting for transfers between devices: 22.4 us -> 18.8 us  [forward(): outer = lax.ppermute(far, 'tensor', [(1, 0), (2, 3)])]
    ppermute x38, starting transfers between devices: 36.6 us -> 39.7 us  [flip(): return lax.ppermute(value, axis, [(i, i ^ mask) for i in range(count)])]
  transfers between devices with their start and end apart: 43 -> 43, of which waited for: 17 -> 15; matrix products, arithmetic and copies ran while one was open for 14% -> 13% of each run, Pallas kernels for 25% -> 26%
where the time goes in v5:
time: 264 us; the launch traced here: 262 us
  waiting for transfers between devices  89 us (34%)
  Pallas kernels  71.3 us (27%)
  starting transfers between devices  42.2 us (16%)
  other arithmetic  15.8 us (6%)
  between operations  15.6 us (6%)
  local copies, waits for them, and re-layouts  14.4 us (5%)
  matrix products  13.4 us (5%)
    pallas_call x17, Pallas kernels, call(): pl.pallas_call(kernel, out_shape=out_shape, in_specs=in_specs, out_specs=...  71.2 us
    ppermute x38, waiting for transfers between devices, flip(): return lax.ppermute(value, axis, [(i, i ^ mask) for i in range(count)])  69.8 us
    ppermute x38, starting transfers between devices, flip(): return lax.ppermute(value, axis, [(i, i ^ mask) for i in range(count)])  39.7 us
    ppermute x1, waiting for transfers between devices, forward(): outer = lax.ppermute(far, 'tensor', [(1, 0), (2, 3)])  18.8 us
    dot_general x6, matrix products, mm(): return lax.dot_general(left, right, dims, preferred_element_type=FULL)  13.4 us
    cond x65, local copies, waits for them, and re-layouts  5.43 us
  transfers between devices with their start and end apart: 43, of which 15 were waited for; matrix products, arithmetic and copies ran while one was open for 13% of the time, Pallas kernels for 26%

profile of v5, /device:TPU:0, one launch (start us, length us, event | category | flops | bytes accessed | tf_op | source)
XLA Modules:
  0.0 262.3 jit_solution(13168811915169435077)
XLA Ops:
  11.4 91.6 %conditional.7 = (f32[192,512]{1,0:T(8,128)S(1)}, bf16[512,768]{1,0:T(8,128)(2,1)S(1)}, f32[2,6,768]{2,1,0:T(8,128)}, f32[512,768]{1,0:T(8,128)}, f32[512,768]{1...) conditional(s32[]{:T(128)} %convert_element_type.65, () %tuple.83, ...), branch_computations={%region_0.1_spmd, %region_1.2_spmd} | conditional | flops 1825942272 | bytes 55603812 | solution.py:566
  13.3 5.0 %collective-permute-start.5 = (f32[2,4608]{1,0:T(2,128)S(1)}, f32[2,4608]{1,0:T(2,128)S(1)}, u32[]{:S(2)}, u32[]{:S(2)}) collective-permute-start(f32[2,4608]{1,0:T(2,128)S(1)} %fusion.15.part0), channel_id=1, source_target_pairs={{0,3},{1,2},{2,1},{3,0},{4,7},{5,6},{6,5},{7,4},{8,11},{9,10},{10,... | collective-permute-start | bytes 110600 | tf_op jit(solution)/shard_map/cond/branch_1_fun/ppermute | solution.py:449
  19.8 3.8 %collective-permute-start.12 = (f32[24,768]{1,0:T(8,128)S(1)}, f32[24,768]{1,0:T(8,128)S(1)}, u32[]{:S(2)}, u32[]{:S(2)}) collective-permute-start(f32[24,768]{1,0:T(8,128)S(1)} %dynamic-slice_convert_fusion.refs_0_), channel_id=1, source_target_pairs={{0,3},{1,2},{2,1},{3,0},{4,7},{5,6},{6,5},{7,4},{8,11},{9,10},{10,... | collective-permute-start | bytes 221192 | tf_op jit(solution)/shard_map/cond/branch_1_fun/ppermute | solution.py:449
  24.2 4.3 %collective-permute-done.3.part1 = f32[2,4608]{1,0:T(2,128)S(1)} collective-permute-done((f32[2,4608]{1,0:T(2,128)S(1)}, f32[2,4608]{1,0:T(2,128)S(1)}, u32[]{:S(2)}, u32[]{:S(2)}) %collective-permute-start.3) | collective-permute-done | bytes 36896 | tf_op jit(solution)/shard_map/cond/branch_1_fun/ppermute | solution.py:449
  28.5 4.8 %collective-permute-done.4.part2 = f32[2,4608]{1,0:T(2,128)S(1)} collective-permute-done((f32[2,4608]{1,0:T(2,128)S(1)}, f32[2,4608]{1,0:T(2,128)S(1)}, u32[]{:S(2)}, u32[]{:S(2)}) %collective-permute-start.4) | collective-permute-done | bytes 36896 | tf_op jit(solution)/shard_map/cond/branch_1_fun/ppermute | solution.py:449
  33.3 4.9 %start.1 = (f32[192,512]{1,0:T(8,128)S(1)}, bf16[512,768]{1,0:T(8,128)(2,1)S(1)}, f32[2,6,768]{2,1,0:T(8,128)}) custom-call(f32[2,4608]{1,0:T(2,128)S(1)} %fusion.15.part0, f32[2,4608]{1,0:T(2,128)S(1)} %collective-permute-done.3.part1, f32[2,4608]{1,0:T(2,128)S(1)} %collective-permute-done.4.part2, f32[2,4608]{1,0:T(2,128)S(1)} %collective-permute-done.5.part3.refs_1_, ...), custom_call_target="tpu_custom_call" | custom-call | tf_op jit(solution)/shard_map/cond/branch_1_fun/start/pallas_call | solution.py:55
  47.3 9.6 %collective-permute-done.13.refs_1_ = f32[4,24,768]{2,1,0:T(8,128)S(1)} collective-permute-done((f32[4,24,768]{2,1,0:T(8,128)S(1)}, f32[4,24,768]{2,1,0:T(8,128)S(1)}, u32[]{:S(2)}, u32[]{:S(2)}) %collective-permute-start.13) | collective-permute-done | bytes 294944 | tf_op jit(solution)/shard_map/cond/branch_1_fun/ppermute | solution.py:449
  58.4 5.9 %collective-permute-done.7.mixed2 = f32[192,512]{1,0:T(8,128)S(1)} collective-permute-done((f32[192,512]{1,0:T(8,128)S(1)}, f32[192,512]{1,0:T(8,128)S(1)}, u32[]{:S(2)}, u32[]{:S(2)}) %collective-permute-start.7) | collective-permute-done | bytes 393248 | tf_op jit(solution)/shard_map/cond/branch_1_fun/ppermute | solution.py:449
  66.4 5.8 %collective-permute-done.6.mixed1 = f32[192,512]{1,0:T(8,128)S(1)} collective-permute-done((f32[192,512]{1,0:T(8,128)S(1)}, f32[192,512]{1,0:T(8,128)S(1)}, u32[]{:S(2)}, u32[]{:S(2)}) %collective-permute-start.6) | collective-permute-done | bytes 393248 | tf_op jit(solution)/shard_map/cond/branch_1_fun/ppermute | solution.py:449
  74.2 18.8 %collective-permute-done.9.outer = f32[192,512]{1,0:T(8,128)S(1)} collective-permute-done((f32[192,512]{1,0:T(8,128)S(1)}, f32[192,512]{1,0:T(8,128)S(1)}, u32[]{:S(2)}, u32[]{:S(2)}) %collective-permute-start.9) | collective-permute-done | bytes 393248 | tf_op jit(solution)/shard_map/cond/branch_1_fun/ppermute | solution.py:626
  92.9 4.3 %join_heads.1 = (f32[512,768]{1,0:T(8,128)}, f32[512,768]{1,0:T(8,128)}, bf16[512,768]{1,0:T(8,128)(2,1)}, bf16[768,768]{1,0:T(8,128)(2,1)}) custom-call(s32[3]{0:T(128)S(1)} %get-tuple-element.180.place, f32[192,512]{1,0:T(8,128)S(1)} %get-tuple-element.462.mixed0, f32[192,512]{1,0:T(8,128)S(1)} %collective-permute-done.6.mixed1, ...), custom_call_target="tpu_custom_call" | custom-call | tf_op jit(solution)/shard_map/cond/branch_1_fun/join_heads/pallas_call | solution.py:55
  97.2 3.8 %fusion.6 = (bf16[512,768]{1,0:T(8,128)(2,1)}, bf16[512,768]{1,0:T(8,128)(2,1)S(1)}) fusion(f32[512,768]{1,0:T(8,128)S(1)} %fusion.16, f32[768]{0:T(1024)S(1)} %convert_element_type.27, bf16[512,768]{1,0:T(8,128)(2,1)} %get-tuple-element.470, bf16[768,768]{1,0:T(8,128)(2,1)S(1)} %copy-done.37), kind=kOutput, calls=%fused_computation.8 | convolution fusion | flops 613023744 | bytes 5114880 | tf_op jit(solution)/shard_map/cond/branch_1_fun/dot_general | solution.py:23
  104.2 43.3 %conditional.8 = (f32[192,768]{1,0:T(8,128)S(1)}, f32[512,768]{1,0:T(8,128)}, bf16[2,768]{1,0:T(2,128)(2,1)}, f32[3,768]{1,0:T(4,128)}, f32[768]{0:T(1024)}, /*index=5*/f32[768]{0:T(1024)}) conditional(s32[]{:T(128)} %convert_element_type.65, () %tuple.82, (s32[3]{0:T(128)S(1)}, bf16[512,768]{1,0:T(8,128)(2,1)S(1)}, bf16[512,768]{1,0:T(8,128)(2,1)}, ...), branch_computations={%region_2.3_spmd, %region_3.0_spmd} | conditional | flops 607588416 | bytes 32029672 | solution.py:566
  105.1 4.1 %mlp_grads.1 = (f32[768,768]{1,0:T(8,128)}, f32[768,768]{1,0:T(8,128)S(1)}) custom-call(s32[3]{0:T(128)S(1)} %get-tuple-element.191.place, bf16[512,768]{1,0:T(8,128)(2,1)} %copy-done.16, bf16[512,768]{1,0:T(8,128)(2,1)} %get-tuple-element.193.branch_grad, bf16[512,768]{1,0:T(8,128)(2,1)} %get-tuple-element.194.entry, ...), custom_call_target="tpu_custom_call" | custom-call | tf_op jit(solution)/shard_map/cond/branch_1_fun/mlp_grads/pallas_call | solution.py:55
  109.5 3.7 %convert_reduce_fusion = (f32[2,768]{1,0:T(2,128)S(1)}, f32[2,768]{1,0:T(2,128)S(1)}, f32[512,768]{1,0:T(8,128)}) fusion(bf16[2,256,768]{2,1,0:T(8,128)(2,1)} %get-tuple-element.203, bf16[512,768]{1,0:T(8,128)(2,1)} %copy-done.16, bf16[768,768]{1,0:T(8,128)(2,1)} %get-tuple-element.202), kind=kOutput, calls=%fused_computation.15 | convolution fusion | flops 605549568 | bytes 4337664 | tf_op jit(solution)/shard_map/cond/branch_1_fun/dot_general | solution.py:23
  120.1 3.2 %collective-permute-start.23 = (f32[192,768]{1,0:T(8,128)S(1)}, f32[192,768]{1,0:T(8,128)S(1)}, u32[]{:S(2)}, u32[]{:S(2)}) collective-permute-start(f32[192,768]{1,0:T(8,128)S(1)} %get-tuple-element.201), channel_id=1, source_target_pairs={{0,24},{4,28},{8,16},{12,20},{16,8},{20,12},{24,0},{28,4},{1,25},{... | collective-permute-start | bytes 1769480 | tf_op jit(solution)/shard_map/cond/branch_1_fun/ppermute | solution.py:449
  126.5 9.5 %collective-permute-done.21 = f32[192,768]{1,0:T(8,128)S(1)} collective-permute-done((f32[192,768]{1,0:T(8,128)S(1)}, f32[192,768]{1,0:T(8,128)S(1)}, u32[]{:S(2)}, u32[]{:S(2)}) %collective-permute-start.21) | collective-permute-done | bytes 589856 | tf_op jit(solution)/shard_map/cond/branch_1_fun/ppermute | solution.py:449
  136.0 11.3 %collective-permute-done.22 = f32[192,768]{1,0:T(8,128)S(1)} collective-permute-done((f32[192,768]{1,0:T(8,128)S(1)}, f32[192,768]{1,0:T(8,128)S(1)}, u32[]{:S(2)}, u32[]{:S(2)}) %collective-permute-start.22) | collective-permute-done | bytes 589856 | tf_op jit(solution)/shard_map/cond/branch_1_fun/ppermute | solution.py:449
  147.5 27.9 %conditional.9 = (f32[192,768]{1,0:T(8,128)}, f32[192,768]{1,0:T(8,128)}, f32[192,768]{1,0:T(8,128)}, f32[192,768]{1,0:T(8,128)}, f32[2,12,256,256]{3,2,1,0:T(8,...) conditional(s32[]{:T(128)} %convert_element_type.65, () %tuple.86, (f32[192,768]{1,0:T(8,128)S(1)}, ...), branch_computations={%region_9.10_spmd, %region_10.11_spmd} | conditional | bytes 14549072 | solution.py:566
  151.9 8.5 %project_all.1 = (bf16[3,768,512]{2,1,0:T(8,128)(2,1)}, bf16[3,768,768]{2,1,0:T(8,128)(2,1)}) custom-call(f32[4,3,192,768]{3,2,1,0:T(8,128)} %get-tuple-element.208.weight_ref, f32[3,768]{1,0:T(4,128)} %get-tuple-element.209.bias, bf16[512,768]{1,0:T(8,128)(2,1)S(1)} %get-tuple-element.210.entry), custom_call_target="tpu_custom_call" | custom-call | tf_op jit(solution)/shard_map/cond/branch_1_fun/project_all/pallas_call | solution.py:55
  160.4 7.1 %all_probs.1 = f32[2,12,256,256]{3,2,1,0:T(8,128)} custom-call(bf16[3,768,512]{2,1,0:T(8,128)(2,1)} %get-tuple-element.497.proj_ref), custom_call_target="tpu_custom_call" | custom-call | tf_op jit(solution)/shard_map/cond/branch_1_fun/all_probs/pallas_call | solution.py:55
  167.5 7.9 %collective-permute-done.1 = f32[192,768]{1,0:T(8,128)} collective-permute-done((f32[192,768]{1,0:T(8,128)S(1)}, f32[192,768]{1,0:T(8,128)}, u32[]{:S(2)}, u32[]{:S(2)}) %collective-permute-start.1) | collective-permute-done | bytes 589856 | tf_op jit(solution)/shard_map/cond/branch_1_fun/ppermute | solution.py:449
  178.1 71.8 %conditional.10 = (f32[768,768]{1,0:T(8,128)}, f32[768,768]{1,0:T(8,128)}, f32[576,768]{1,0:T(8,128)}, f32[192,768]{1,0:T(8,128)}, f32[2,192]{1,0:T(2,128)}, /*i...) conditional(s32[]{:T(128)} %convert_element_type.65, () %tuple.88, ...), branch_computations={%region_12.13_spmd, %region_13.22_spmd} | conditional | flops 4658717 | bytes 63369280 | solution.py:566
  178.1 18.6 %conditional = (f32[512,768]{1,0:T(8,128)}, bf16[3,768,512]{2,1,0:T(8,128)(2,1)}, f32[384,768]{1,0:T(8,128)S(1)}, f32[384,768]{1,0:T(8,128)S(1)}, f32[768]{0:T(1...) conditional(s32[]{:T(128)} %convert_element_type.58, () %tuple.67, (bf16[2,256,768]{2,1,0:T(8,128)(2,1)}, ...), branch_computations={%region_14.14_spmd, %region_15.16_spmd} | conditional | flops 768 | bytes 6306128 | solution.py:566
  178.1 5.3 %middle_backward.2 = (f32[512,768]{1,0:T(8,128)}, bf16[512,768]{1,0:T(8,128)(2,1)S(1)}, bf16[768,512]{1,0:T(8,128)(2,1)S(1)}, f32[2,4,768]{2,1,0:T(4,128)S(1)}) custom-call(f32[512,768]{1,0:T(8,128)S(1)} %get-tuple-element.213.grad_ref, f32[512,768]{1,0:T(8,128)} %get-tuple-element.214.middle_ref, f32[512,768]{1,0:T(8,128)} %get-tuple-element.215.attention_ref, ...), custom_call_target="tpu_custom_call" | custom-call | tf_op jit(solution)/shard_map/cond/branch_1_fun/cond/branch_1_fun/middle_backward/pallas_call | solution.py:55
  183.4 10.6 %attention_backward.1.proj = bf16[3,768,512]{2,1,0:T(8,128)(2,1)} custom-call(f32[2,12,256,256]{3,2,1,0:T(8,128)} %get-tuple-element.220.probs_ref, bf16[3,768,512]{2,1,0:T(8,128)(2,1)} %get-tuple-element.221.proj_ref, bf16[768,512]{1,0:T(8,128)(2,1)S(1)} %get-tuple-element.222.grad_ref), custom_call_target="tpu_custom_call" | custom-call | tf_op jit(solution)/shard_map/cond/branch_1_fun/cond/branch_1_fun/attention_backward/pallas_call | solution.py:55
  204.7 7.3 %conditional.1 = (f32[2,2,768]{2,1,0:T(2,128)}, f32[2,256,768]{2,1,0:T(8,128)}, bf16[2,2,768]{2,1,0:T(2,128)(2,1)S(1)}) conditional(s32[]{:T(128)} %convert_element_type.58, () %tuple.66, (bf16[3,768,512]{2,1,0:T(8,128)(2,1)}, bf16[3,768,768]{2,1,0:T(8,128)(2,1)}, bf16[512,768]{1,0:T(8,128)(2,1)S(1)}, f32[512,768]{1,0:T(8,128)}, ...), branch_computations={%region_17.17_spmd, %region_18.18_spmd} | conditional | flops 3072 | bytes 1591330 | solution.py:566
  204.7 6.6 %entry_backward.1 = (f32[512,768]{1,0:T(8,128)}, f32[2,2,768]{2,1,0:T(2,128)}) custom-call(bf16[2304,512]{1,0:T(8,128)(2,1)} %bitcast.7.proj_ref, bf16[2304,768]{1,0:T(8,128)(2,1)} %bitcast.8.weight_ref, bf16[512,768]{1,0:T(8,128)(2,1)S(1)} %get-tuple-element.233.inputs_ref, f32[512,768]{1,0:T(8,128)} %get-tuple-element.234.middle_grad_ref, ...), custom_call_target="tpu_custom_call" | custom-call | tf_op jit(solution)/shard_map/cond/branch_1_fun/cond/branch_1_fun/entry_backward/pallas_call | solution.py:55
  212.8 4.5 %collective-permute-done.29.refs_2_ = f32[96,768]{1,0:T(8,128)} collective-permute-done((f32[96,768]{1,0:T(8,128)S(1)}, f32[96,768]{1,0:T(8,128)}, u32[]{:S(2)}, u32[]{:S(2)}) %collective-permute-start.29) | collective-permute-done | bytes 294944 | tf_op jit(solution)/shard_map/cond/branch_1_fun/ppermute | solution.py:449
  232.6 10.8 %conditional.2 = (f32[192,4608]{1,0:T(8,128)}, f32[768]{0:T(1024)}, f32[768]{0:T(1024)}, f32[768]{0:T(1024)}, f32[576]{0:T(1024)}, /*index=5*/f32[2,192]{1,0:T(2...) conditional(s32[]{:T(128)} %convert_element_type.58, () %tuple.65, (f32[16,7744]{1,0:T(8,128)S(1)}, ...), branch_computations={%region_19.19_spmd, %region_20.21_spmd} | conditional | flops 3585600 | bytes 9124712 | solution.py:566
  233.3 3.7 %modulator_backward.1 = (f32[192,4608]{1,0:T(8,128)}, f32[1,4608]{1,0:T(1,128)S(1)}) custom-call(f32[16,7744]{1,0:T(8,128)S(1)} %get-tuple-element.238.every_ref.context_ref, f32[16,7744]{1,0:T(8,128)S(1)} %get-tuple-element.238.every_ref.context_ref), custom_call_target="tpu_custom_call" | custom-call | tf_op jit(solution)/shard_map/cond/branch_1_fun/cond/branch_1_fun/modulator_backward/pallas_call | solution.py:55
  238.2 4.0 %whole.2 = (f32[768,768]{1,0:T(8,128)}, f32[768,768]{1,0:T(8,128)}) custom-call(s32[3]{0:T(128)S(1)} %get-tuple-element.243.place, f32[768,768]{1,0:T(8,128)S(1)} %get-tuple-element.244.mine, f32[768,768]{1,0:T(8,128)} %get-tuple-element.245.other), custom_call_target="tpu_custom_call" | custom-call | tf_op jit(solution)/shard_map/cond/branch_1_fun/cond/branch_1_fun/whole/pallas_call | solution.py:55
  (233 shorter events, 85.1 us)
Async XLA Ops:
  8.0 139.5 %all-gather.2.cloned.1.call-start = ((), (), s32[]{:S(2)}) async-start(), calls=%async_computation.1 | async-start | bytes 7299072 | tf_op jit(solution)/shard_map/all_gather | solution.py:531
  13.3 10.3 %collective-permute-start.5 = (f32[2,4608]{1,0:T(2,128)S(1)}, f32[2,4608]{1,0:T(2,128)S(1)}, u32[]{:S(2)}, u32[]{:S(2)}) collective-permute-start(f32[2,4608]{1,0:T(2,128)S(1)} %fusion.15.part0), channel_id=1, source_target_pairs={{0,3},{1,2},{2,1},{3,0},{4,7},{5,6},{6,5},{7,4},{8,11},{9,10},{10,... | collective-permute-start | bytes 110600 | tf_op jit(solution)/shard_map/cond/branch_1_fun/ppermute | solution.py:449
  19.2 19.1 %collective-permute-start.10 = (f32[24,768]{1,0:T(8,128)S(1)}, f32[24,768]{1,0:T(8,128)S(1)}, u32[]{:S(2)}, u32[]{:S(2)}) collective-permute-start(f32[24,768]{1,0:T(8,128)S(1)} %dynamic-slice_convert_fusion.refs_0_), channel_id=1, source_target_pairs={{0,1},{1,0},{2,3},{3,2},{4,5},{5,4},{6,7},{7,6},{8,9},{9,8},{10,11... | collective-permute-start | bytes 221192 | tf_op jit(solution)/shard_map/cond/branch_1_fun/ppermute | solution.py:449
  19.2 19.7 %collective-permute-start.11 = (f32[24,768]{1,0:T(8,128)S(1)}, f32[24,768]{1,0:T(8,128)S(1)}, u32[]{:S(2)}, u32[]{:S(2)}) collective-permute-start(f32[24,768]{1,0:T(8,128)S(1)} %dynamic-slice_convert_fusion.refs_0_), channel_id=1, source_target_pairs={{0,2},{1,3},{2,0},{3,1},{4,6},{5,7},{6,4},{7,5},{8,10},{9,11},{10,... | collective-permute-start | bytes 221192 | tf_op jit(solution)/shard_map/cond/branch_1_fun/ppermute | solution.py:449
  19.8 19.8 %collective-permute-start.12 = (f32[24,768]{1,0:T(8,128)S(1)}, f32[24,768]{1,0:T(8,128)S(1)}, u32[]{:S(2)}, u32[]{:S(2)}) collective-permute-start(f32[24,768]{1,0:T(8,128)S(1)} %dynamic-slice_convert_fusion.refs_0_), channel_id=1, source_target_pairs={{0,3},{1,2},{2,1},{3,0},{4,7},{5,6},{6,5},{7,4},{8,11},{9,10},{10,... | collective-permute-start | bytes 221192 | tf_op jit(solution)/shard_map/cond/branch_1_fun/ppermute | solution.py:449
  23.6 9.7 %collective-permute-start.4 = (f32[2,4608]{1,0:T(2,128)S(1)}, f32[2,4608]{1,0:T(2,128)S(1)}, u32[]{:S(2)}, u32[]{:S(2)}) collective-permute-start(f32[2,4608]{1,0:T(2,128)S(1)} %fusion.15.part0), channel_id=1, source_target_pairs={{0,2},{1,3},{2,0},{3,1},{4,6},{5,7},{6,4},{7,5},{8,10},{9,11},{10,... | collective-permute-start | bytes 110600 | tf_op jit(solution)/shard_map/cond/branch_1_fun/ppermute | solution.py:449
  38.2 26.1 %collective-permute-start.7 = (f32[192,512]{1,0:T(8,128)S(1)}, f32[192,512]{1,0:T(8,128)S(1)}, u32[]{:S(2)}, u32[]{:S(2)}) collective-permute-start(f32[192,512]{1,0:T(8,128)S(1)} %get-tuple-element.462.mixed0), channel_id=1, source_target_pairs={{0,2},{1,3},{2,0},{3,1},{4,6},{5,7},{6,4},{7,5},{8,10},{9,11},{10,... | collective-permute-start | bytes 1179656 | tf_op jit(solution)/shard_map/cond/branch_1_fun/ppermute | solution.py:449
  41.3 15.5 %collective-permute-start.13 = (f32[4,24,768]{2,1,0:T(8,128)S(1)}, f32[4,24,768]{2,1,0:T(8,128)S(1)}, u32[]{:S(2)}, u32[]{:S(2)}) collective-permute-start(f32[4,24,768]{2,1,0:T(8,128)S(1)} %pad_maximum_fusion.refs_0_), channel_id=1, source_target_pairs={{0,8},{4,12},{8,0},{12,4},{16,24},{20,28},{24,16},{28,20},{1,9},{5... | collective-permute-start | bytes 884744 | tf_op jit(solution)/shard_map/cond/branch_1_fun/ppermute | solution.py:449
  42.7 15.0 %collective-permute-start.14 = (f32[4,24,768]{2,1,0:T(8,128)S(1)}, f32[4,24,768]{2,1,0:T(8,128)S(1)}, u32[]{:S(2)}, u32[]{:S(2)}) collective-permute-start(f32[4,24,768]{2,1,0:T(8,128)S(1)} %pad_maximum_fusion.refs_0_), channel_id=1, source_target_pairs={{0,16},{4,20},{8,24},{12,28},{16,0},{20,4},{24,8},{28,12},{1,17},{... | collective-permute-start | bytes 884744 | tf_op jit(solution)/shard_map/cond/branch_1_fun/ppermute | solution.py:449
  44.3 27.9 %collective-permute-start.6 = (f32[192,512]{1,0:T(8,128)S(1)}, f32[192,512]{1,0:T(8,128)S(1)}, u32[]{:S(2)}, u32[]{:S(2)}) collective-permute-start(f32[192,512]{1,0:T(8,128)S(1)} %get-tuple-element.462.mixed0), channel_id=1, source_target_pairs={{0,1},{1,0},{2,3},{3,2},{4,5},{5,4},{6,7},{7,6},{8,9},{9,8},{10,11... | collective-permute-start | bytes 1179656 | tf_op jit(solution)/shard_map/cond/branch_1_fun/ppermute | solution.py:449
  46.7 19.0 %collective-permute-start.15 = (f32[4,24,768]{2,1,0:T(8,128)S(1)}, f32[4,24,768]{2,1,0:T(8,128)S(1)}, u32[]{:S(2)}, u32[]{:S(2)}) collective-permute-start(f32[4,24,768]{2,1,0:T(8,128)S(1)} %pad_maximum_fusion.refs_0_), channel_id=1, source_target_pairs={{0,24},{4,28},{8,16},{12,20},{16,8},{20,12},{24,0},{28,4},{1,25},{... | collective-permute-start | bytes 884744 | tf_op jit(solution)/shard_map/cond/branch_1_fun/ppermute | solution.py:449
  56.8 9.0 %collective-permute-start.16 = (f32[4,24,768]{2,1,0:T(8,128)S(1)}, f32[4,24,768]{2,1,0:T(8,128)S(1)}, u32[]{:S(2)}, u32[]{:S(2)}) collective-permute-start(f32[4,24,768]{2,1,0:T(8,128)S(1)} %pad_maximum_fusion.refs_0_), channel_id=1, source_target_pairs={{0,4},{4,0},{8,12},{12,8},{16,20},{20,16},{24,28},{28,24},{1,5},{5... | collective-permute-start | bytes 884744 | tf_op jit(solution)/shard_map/cond/branch_1_fun/ppermute | solution.py:449
  57.7 15.3 %collective-permute-start.8 = (f32[192,512]{1,0:T(8,128)S(1)}, f32[192,512]{1,0:T(8,128)S(1)}, u32[]{:S(2)}, u32[]{:S(2)}) collective-permute-start(f32[192,512]{1,0:T(8,128)S(1)} %get-tuple-element.462.mixed0), channel_id=1, source_target_pairs={{1,2},{2,1},{5,6},{6,5},{9,10},{10,9},{13,14},{14,13},{17,18},{18,... | collective-permute-start | bytes 1179656 | tf_op jit(solution)/shard_map/cond/branch_1_fun/ppermute | solution.py:625
  64.3 28.6 %collective-permute-start.9 = (f32[192,512]{1,0:T(8,128)S(1)}, f32[192,512]{1,0:T(8,128)S(1)}, u32[]{:S(2)}, u32[]{:S(2)}) collective-permute-start(f32[192,512]{1,0:T(8,128)S(1)} %collective-permute-done.7.mixed2), channel_id=1, source_target_pairs={{1,0},{2,3},{5,4},{6,7},{9,8},{10,11},{13,12},{14,15},{17,16},{18,... | collective-permute-start | bytes 1179656 | tf_op jit(solution)/shard_map/cond/branch_1_fun/ppermute | solution.py:626
  103.1 72.3 %all-reduce.5.cloned.1.call-start = ((), (), s32[]{:S(2)}) async-start(), calls=%async_computation | async-start | bytes 3145728 | tf_op jit(solution)/shard_map/psum | solution.py:644
  109.2 8.5 %collective-permute-start.20 = (f32[768,768]{1,0:T(8,128)}, f32[768,768]{1,0:T(8,128)}, u32[]{:S(2)}, u32[]{:S(2)}) collective-permute-start(f32[768,768]{1,0:T(8,128)} %get-tuple-element.197), channel_id=1, source_target_pairs={{0,4},{4,0},{8,12},{12,8},{16,20},{20,16},{24,28},{28,24},{1,5},{5... | collective-permute-start | bytes 7077896 | tf_op jit(solution)/shard_map/cond/branch_1_fun/ppermute | solution.py:449
  113.3 11.9 %collective-permute-start.25 = (f32[5,768]{1,0:T(8,128)S(1)}, f32[5,768]{1,0:T(8,128)S(1)}, u32[]{:S(2)}, u32[]{:S(2)}) collective-permute-start(f32[5,768]{1,0:T(8,128)S(1)} %pad_maximum_fusion.1), channel_id=1, source_target_pairs={{0,2},{1,3},{2,0},{3,1},{4,6},{5,7},{6,4},{7,5},{8,10},{9,11},{10,... | collective-permute-start | bytes 46088 | tf_op jit(solution)/shard_map/cond/branch_1_fun/ppermute | solution.py:449
  114.9 10.3 %collective-permute-start.26 = (f32[5,768]{1,0:T(8,128)S(1)}, f32[5,768]{1,0:T(8,128)S(1)}, u32[]{:S(2)}, u32[]{:S(2)}) collective-permute-start(f32[5,768]{1,0:T(8,128)S(1)} %pad_maximum_fusion.1), channel_id=1, source_target_pairs={{0,3},{1,2},{2,1},{3,0},{4,7},{5,6},{6,5},{7,4},{8,11},{9,10},{10,... | collective-permute-start | bytes 46088 | tf_op jit(solution)/shard_map/cond/branch_1_fun/ppermute | solution.py:449
  119.7 16.3 %collective-permute-start.21 = (f32[192,768]{1,0:T(8,128)S(1)}, f32[192,768]{1,0:T(8,128)S(1)}, u32[]{:S(2)}, u32[]{:S(2)}) collective-permute-start(f32[192,768]{1,0:T(8,128)S(1)} %get-tuple-element.199), channel_id=1, source_target_pairs={{0,8},{4,12},{8,0},{12,4},{16,24},{20,28},{24,16},{28,20},{1,9},{5... | collective-permute-start | bytes 1769480 | tf_op jit(solution)/shard_map/cond/branch_1_fun/ppermute | solution.py:449
  119.8 27.6 %collective-permute-start.22 = (f32[192,768]{1,0:T(8,128)S(1)}, f32[192,768]{1,0:T(8,128)S(1)}, u32[]{:S(2)}, u32[]{:S(2)}) collective-permute-start(f32[192,768]{1,0:T(8,128)S(1)} %get-tuple-element.200), channel_id=1, source_target_pairs={{0,16},{4,20},{8,24},{12,28},{16,0},{20,4},{24,8},{28,12},{1,17},{... | collective-permute-start | bytes 1769480 | tf_op jit(solution)/shard_map/cond/branch_1_fun/ppermute | solution.py:449
  120.1 27.3 %collective-permute-start.23 = (f32[192,768]{1,0:T(8,128)S(1)}, f32[192,768]{1,0:T(8,128)S(1)}, u32[]{:S(2)}, u32[]{:S(2)}) collective-permute-start(f32[192,768]{1,0:T(8,128)S(1)} %get-tuple-element.201), channel_id=1, source_target_pairs={{0,24},{4,28},{8,16},{12,20},{16,8},{20,12},{24,0},{28,4},{1,25},{... | collective-permute-start | bytes 1769480 | tf_op jit(solution)/shard_map/cond/branch_1_fun/ppermute | solution.py:449
  147.5 19.9 %collective-permute-start = (f32[192,768]{1,0:T(8,128)S(1)}, f32[192,768]{1,0:T(8,128)}, u32[]{:S(2)}, u32[]{:S(2)}) collective-permute-start(f32[192,768]{1,0:T(8,128)S(1)} %get-tuple-element.492), channel_id=1, source_target_pairs={{0,8},{4,12},{8,0},{12,4},{16,24},{20,28},{24,16},{28,20},{1,9},{5... | collective-permute-start | bytes 1769480 | tf_op jit(solution)/shard_map/cond/branch_1_fun/ppermute | solution.py:449
  149.3 26.1 %collective-permute-start.1 = (f32[192,768]{1,0:T(8,128)S(1)}, f32[192,768]{1,0:T(8,128)}, u32[]{:S(2)}, u32[]{:S(2)}) collective-permute-start(f32[192,768]{1,0:T(8,128)S(1)} %get-tuple-element.492), channel_id=1, source_target_pairs={{0,16},{4,20},{8,24},{12,28},{16,0},{20,4},{24,8},{28,12},{1,17},{... | collective-permute-start | bytes 1769480 | tf_op jit(solution)/shard_map/cond/branch_1_fun/ppermute | solution.py:449
  149.6 25.8 %collective-permute-start.2 = (f32[192,768]{1,0:T(8,128)S(1)}, f32[192,768]{1,0:T(8,128)}, u32[]{:S(2)}, u32[]{:S(2)}) collective-permute-start(f32[192,768]{1,0:T(8,128)S(1)} %get-tuple-element.492), channel_id=1, source_target_pairs={{0,24},{4,28},{8,16},{12,20},{16,8},{20,12},{24,0},{28,4},{1,25},{... | collective-permute-start | bytes 1769480 | tf_op jit(solution)/shard_map/cond/branch_1_fun/ppermute | solution.py:449
  176.8 74.4 %all-reduce.7.cloned.1.call-start = ((), (), s32[]{:S(2)}) async-start(), calls=%async_computation.2 | async-start | bytes 3145728 | tf_op jit(solution)/shard_map/psum | solution.py:678
  201.2 11.6 %collective-permute-start.28 = (f32[96,768]{1,0:T(8,128)S(1)}, f32[96,768]{1,0:T(8,128)S(1)}, u32[]{:S(2)}, u32[]{:S(2)}) collective-permute-start(f32[96,768]{1,0:T(8,128)S(1)} %get-tuple-element.275), channel_id=1, source_target_pairs={{0,8},{4,12},{8,0},{12,4},{16,24},{20,28},{24,16},{28,20},{1,9},{5... | collective-permute-start | bytes 884744 | tf_op jit(solution)/shard_map/cond/branch_1_fun/ppermute | solution.py:449
  202.1 15.2 %collective-permute-start.29 = (f32[96,768]{1,0:T(8,128)S(1)}, f32[96,768]{1,0:T(8,128)}, u32[]{:S(2)}, u32[]{:S(2)}) collective-permute-start(f32[96,768]{1,0:T(8,128)S(1)} %get-tuple-element.276), channel_id=1, source_target_pairs={{0,16},{4,20},{8,24},{12,28},{16,0},{20,4},{24,8},{28,12},{1,17},{... | collective-permute-start | bytes 884744 | tf_op jit(solution)/shard_map/cond/branch_1_fun/ppermute | solution.py:449
  203.5 13.8 %collective-permute-start.30 = (f32[96,768]{1,0:T(8,128)S(1)}, f32[96,768]{1,0:T(8,128)}, u32[]{:S(2)}, u32[]{:S(2)}) collective-permute-start(f32[96,768]{1,0:T(8,128)S(1)} %get-tuple-element.277), channel_id=1, source_target_pairs={{0,24},{4,28},{8,16},{12,20},{16,8},{20,12},{24,0},{28,4},{1,25},{... | collective-permute-start | bytes 884744 | tf_op jit(solution)/shard_map/cond/branch_1_fun/ppermute | solution.py:449
  219.3 13.3 %collective-permute-start.35 = (f32[768,768]{1,0:T(8,128)S(1)}, f32[768,768]{1,0:T(8,128)}, u32[]{:S(2)}, u32[]{:S(2)}) collective-permute-start(f32[768,768]{1,0:T(8,128)S(1)} %place.2), channel_id=1, source_target_pairs={{0,4},{4,0},{8,12},{12,8},{16,20},{20,16},{24,28},{28,24},{1,5},{5... | collective-permute-start | bytes 7077896 | tf_op jit(solution)/shard_map/cond/branch_1_fun/ppermute | solution.py:449
  226.0 17.4 %collective-permute-start.36 = (f32[96,768]{1,0:T(8,128)}, f32[96,768]{1,0:T(8,128)S(1)}, u32[]{:S(2)}, u32[]{:S(2)}) collective-permute-start(f32[96,768]{1,0:T(8,128)} %tie.25.refs_0_), channel_id=1, source_target_pairs={{0,8},{4,12},{8,0},{12,4},{16,24},{20,28},{24,16},{28,20},{1,9},{5... | collective-permute-start | bytes 884744 | tf_op jit(solution)/shard_map/cond/branch_1_fun/ppermute | solution.py:449
  228.0 15.4 %collective-permute-start.37 = (f32[96,768]{1,0:T(8,128)}, f32[96,768]{1,0:T(8,128)S(1)}, u32[]{:S(2)}, u32[]{:S(2)}) collective-permute-start(f32[96,768]{1,0:T(8,128)} %tie.25.refs_0_), channel_id=1, source_target_pairs={{0,16},{4,20},{8,24},{12,28},{16,0},{20,4},{24,8},{28,12},{1,17},{... | collective-permute-start | bytes 884744 | tf_op jit(solution)/shard_map/cond/branch_1_fun/ppermute | solution.py:449
  229.9 13.5 %collective-permute-start.38 = (f32[96,768]{1,0:T(8,128)}, f32[96,768]{1,0:T(8,128)S(1)}, u32[]{:S(2)}, u32[]{:S(2)}) collective-permute-start(f32[96,768]{1,0:T(8,128)} %tie.25.refs_0_), channel_id=1, source_target_pairs={{0,24},{4,28},{8,16},{12,20},{16,8},{20,12},{24,0},{28,4},{1,25},{... | collective-permute-start | bytes 884744 | tf_op jit(solution)/shard_map/cond/branch_1_fun/ppermute | solution.py:449
  (50 other events, 429.2 us)
Sparse Core Ops, SparseCore 0:
  11.7 88.5 all-gather.1
Sparse Core Ops, SparseCore 1:
  106.5 67.6 all-reduce.4
  179.7 66.7 all-reduce.6

commit v6 on v5

--- a/solution.py
+++ b/solution.py
@@ -635,11 +635,11 @@
         gate_two = modulation[:, None, 5]
         branch_grad = (gate_two * cotangent.astype(FULL)).astype(LOW).reshape(tokens, features)
         hidden_grad = gelu_pull(mm(branch_grad, ffn_output, NT))[0].astype(LOW)
-        part = mm(hidden_grad, ffn_input, NT)
         first = mixed_t, entry_one, modulation, attention, middle, output_full
-        return first, (active, branch_grad, entry_two, hidden_grad), part
-
-    first, mlp, part = as_one(forward, context_low)
+        return first, (active, branch_grad, entry_two, hidden_grad)
+
+    first, mlp = as_one(forward, context_low)
+    part = mm(mlp[3], ffn_input, NT)
     mixed_t, entry_one, modulation, attention, middle, output_full = first
     entry_two_grad = lax.psum(part, "tensor")
     mlp_shares = (ffn_output.shape[0] // GROUP, features // GROUP)

time: 264 us -> 262 us (level)
  other arithmetic: 15.8 us -> 12.8 us
    cond x65 -> x57, local copies, waits for them, and re-layouts: 5.43 us -> 7.9 us
  transfers between devices with their start and end apart: 43 -> 43, of which waited for: 15 -> 14; matrix products, arithmetic and copies ran while one was open for 13% -> 12% of each run, Pallas kernels for 26% -> 27%
where the time goes in v6:
time: 262 us; the launch traced here: 261 us
  waiting for transfers between devices  88.6 us (34%)
  Pallas kernels  70.3 us (27%)
  starting transfers between devices  42.4 us (16%)
  between operations  15.6 us (6%)
  matrix products  15.5 us (6%)
  local copies, waits for them, and re-layouts  14.8 us (6%)
  other arithmetic  12.8 us (5%)
    pallas_call x17, Pallas kernels, call(): pl.pallas_call(kernel, out_shape=out_shape, in_specs=in_specs, out_specs=...  70.3 us
    ppermute x38, waiting for transfers between devices, flip(): return lax.ppermute(value, axis, [(i, i ^ mask) for i in range(count)])  69.8 us
    ppermute x38, starting transfers between devices, flip(): return lax.ppermute(value, axis, [(i, i ^ mask) for i in range(count)])  40 us
    ppermute x1, waiting for transfers between devices, forward(): outer = lax.ppermute(far, 'tensor', [(1, 0), (2, 3)])  18.1 us
    dot_general x6, matrix products, mm(): return lax.dot_general(left, right, dims, preferred_element_type=FULL)  15.5 us
    cond x57, local copies, waits for them, and re-layouts  7.9 us
  transfers between devices with their start and end apart: 43, of which 14 were waited for; matrix products, arithmetic and copies ran while one was open for 12% of the time, Pallas kernels for 27%

profile of v6, /device:TPU:0, one launch (start us, length us, event | category | flops | bytes accessed | tf_op | source)
XLA Modules:
  0.0 260.6 jit_solution(13351581111961873387)
XLA Ops:
  11.4 87.6 %conditional.7 = (f32[192,512]{1,0:T(8,128)S(1)}, bf16[512,768]{1,0:T(8,128)(2,1)S(1)}, f32[2,6,768]{2,1,0:T(8,128)}, f32[512,768]{1,0:T(8,128)}, f32[512,768]{1...) conditional(s32[]{:T(128)} %convert_element_type.65, () %tuple.83, ...), branch_computations={%region_0.1_spmd, %region_1.2_spmd} | conditional | flops 1221962496 | bytes 49066588 | solution.py:566
  13.3 5.0 %collective-permute-start.5 = (f32[2,4608]{1,0:T(2,128)S(1)}, f32[2,4608]{1,0:T(2,128)S(1)}, u32[]{:S(2)}, u32[]{:S(2)}) collective-permute-start(f32[2,4608]{1,0:T(2,128)S(1)} %fusion.15.part0), channel_id=1, source_target_pairs={{0,3},{1,2},{2,1},{3,0},{4,7},{5,6},{6,5},{7,4},{8,11},{9,10},{10,... | collective-permute-start | bytes 110600 | tf_op jit(solution)/shard_map/cond/branch_1_fun/ppermute | solution.py:449
  19.8 3.8 %collective-permute-start.12 = (f32[24,768]{1,0:T(8,128)S(1)}, f32[24,768]{1,0:T(8,128)S(1)}, u32[]{:S(2)}, u32[]{:S(2)}) collective-permute-start(f32[24,768]{1,0:T(8,128)S(1)} %dynamic-slice_convert_fusion.refs_0_), channel_id=1, source_target_pairs={{0,3},{1,2},{2,1},{3,0},{4,7},{5,6},{6,5},{7,4},{8,11},{9,10},{10,... | collective-permute-start | bytes 221192 | tf_op jit(solution)/shard_map/cond/branch_1_fun/ppermute | solution.py:449
  24.2 4.3 %collective-permute-done.3.part1 = f32[2,4608]{1,0:T(2,128)S(1)} collective-permute-done((f32[2,4608]{1,0:T(2,128)S(1)}, f32[2,4608]{1,0:T(2,128)S(1)}, u32[]{:S(2)}, u32[]{:S(2)}) %collective-permute-start.3) | collective-permute-done | bytes 36896 | tf_op jit(solution)/shard_map/cond/branch_1_fun/ppermute | solution.py:449
  28.5 4.7 %collective-permute-done.4.part2 = f32[2,4608]{1,0:T(2,128)S(1)} collective-permute-done((f32[2,4608]{1,0:T(2,128)S(1)}, f32[2,4608]{1,0:T(2,128)S(1)}, u32[]{:S(2)}, u32[]{:S(2)}) %collective-permute-start.4) | collective-permute-done | bytes 36896 | tf_op jit(solution)/shard_map/cond/branch_1_fun/ppermute | solution.py:449
  33.2 4.4 %start.1 = (f32[192,512]{1,0:T(8,128)S(1)}, bf16[512,768]{1,0:T(8,128)(2,1)S(1)}, f32[2,6,768]{2,1,0:T(8,128)S(1)}) custom-call(f32[2,4608]{1,0:T(2,128)S(1)} %fusion.15.part0, f32[2,4608]{1,0:T(2,128)S(1)} %collective-permute-done.3.part1, f32[2,4608]{1,0:T(2,128)S(1)} %collective-permute-done.4.part2, f32[2,4608]{1,0:T(2,128)S(1)} %collective-permute-done.5.part3.refs_1_, ...), custom_call_target="tpu_custom_call" | custom-call | tf_op jit(solution)/shard_map/cond/branch_1_fun/start/pallas_call | solution.py:55
  46.8 9.1 %collective-permute-done.13.refs_1_ = f32[4,24,768]{2,1,0:T(8,128)S(1)} collective-permute-done((f32[4,24,768]{2,1,0:T(8,128)S(1)}, f32[4,24,768]{2,1,0:T(8,128)S(1)}, u32[]{:S(2)}, u32[]{:S(2)}) %collective-permute-start.13) | collective-permute-done | bytes 294944 | tf_op jit(solution)/shard_map/cond/branch_1_fun/ppermute | solution.py:449
  56.7 7.0 %collective-permute-done.7.mixed2 = f32[192,512]{1,0:T(8,128)S(1)} collective-permute-done((f32[192,512]{1,0:T(8,128)S(1)}, f32[192,512]{1,0:T(8,128)S(1)}, u32[]{:S(2)}, u32[]{:S(2)}) %collective-permute-start.7) | collective-permute-done | bytes 393248 | tf_op jit(solution)/shard_map/cond/branch_1_fun/ppermute | solution.py:449
  66.6 5.1 %collective-permute-done.6.mixed1 = f32[192,512]{1,0:T(8,128)S(1)} collective-permute-done((f32[192,512]{1,0:T(8,128)S(1)}, f32[192,512]{1,0:T(8,128)S(1)}, u32[]{:S(2)}, u32[]{:S(2)}) %collective-permute-start.6) | collective-permute-done | bytes 393248 | tf_op jit(solution)/shard_map/cond/branch_1_fun/ppermute | solution.py:449
  73.9 18.1 %collective-permute-done.9.outer = f32[192,512]{1,0:T(8,128)S(1)} collective-permute-done((f32[192,512]{1,0:T(8,128)S(1)}, f32[192,512]{1,0:T(8,128)S(1)}, u32[]{:S(2)}, u32[]{:S(2)}) %collective-permute-start.9) | collective-permute-done | bytes 393248 | tf_op jit(solution)/shard_map/cond/branch_1_fun/ppermute | solution.py:626
  92.0 4.0 %join_heads.1 = (f32[512,768]{1,0:T(8,128)}, f32[512,768]{1,0:T(8,128)}, bf16[512,768]{1,0:T(8,128)(2,1)}, bf16[768,768]{1,0:T(8,128)(2,1)}) custom-call(s32[3]{0:T(128)S(1)} %get-tuple-element.180.place, f32[192,512]{1,0:T(8,128)S(1)} %get-tuple-element.457.mixed0, f32[192,512]{1,0:T(8,128)S(1)} %collective-permute-done.6.mixed1, ...), custom_call_target="tpu_custom_call" | custom-call | tf_op jit(solution)/shard_map/cond/branch_1_fun/join_heads/pallas_call | solution.py:55
  99.1 3.7 %fusion.17.refs_1_ = f32[512,768]{1,0:T(8,128)} fusion(bf16[512,768]{1,0:T(8,128)(2,1)S(1)} %get-tuple-element.344, bf16[768,768]{1,0:T(8,128)(2,1)} %param.35), kind=kOutput, calls=%fused_computation.61 | convolution fusion | flops 603979776 | bytes 3538944 | tf_op jit(solution)/shard_map/dot_general | solution.py:23
  103.4 44.3 %conditional.8 = (f32[192,768]{1,0:T(8,128)}, f32[512,768]{1,0:T(8,128)}, bf16[2,768]{1,0:T(2,128)(2,1)S(1)}, f32[3,768]{1,0:T(4,128)S(1)}, f32[768]{0:T(1024)S(1)}, /*index=5*/f32[768]{0:T(1024)S(1)}) conditional(s32[]{:T(128)} %convert_element_type.65, () %tuple.82, (s32[3]{0:T(128)S(1)}, bf16[512,768]{1,0:T(8,128)(2,1)S(1)}, ...), branch_computations={%region_2.3_spmd, %region_3.0_spmd} | conditional | flops 607588416 | bytes 35169104 | solution.py:566
  104.6 4.1 %mlp_grads.1 = (f32[768,768]{1,0:T(8,128)}, f32[768,768]{1,0:T(8,128)S(1)}) custom-call(s32[3]{0:T(128)S(1)} %get-tuple-element.191.place, bf16[512,768]{1,0:T(8,128)(2,1)} %copy-done.19, bf16[512,768]{1,0:T(8,128)(2,1)} %get-tuple-element.193.branch_grad, bf16[512,768]{1,0:T(8,128)(2,1)} %get-tuple-element.194.entry, bf16[512,768]{1,0:T(8,128)(2,1)} %copy-done.9), custom_call_target="tpu_custom_call" | custom-call | tf_op jit(solution)/shard_map/cond/branch_1_fun/mlp_grads/pallas_call | solution.py:55
  108.9 3.7 %convert_reduce_fusion = (f32[2,768]{1,0:T(2,128)S(1)}, f32[2,768]{1,0:T(2,128)S(1)}, f32[512,768]{1,0:T(8,128)}) fusion(bf16[2,256,768]{2,1,0:T(8,128)(2,1)} %get-tuple-element.203, bf16[512,768]{1,0:T(8,128)(2,1)} %copy-done.19, bf16[768,768]{1,0:T(8,128)(2,1)} %get-tuple-element.202), kind=kOutput, calls=%fused_computation.15 | convolution fusion | flops 605549568 | bytes 4337664 | tf_op jit(solution)/shard_map/cond/branch_1_fun/dot_general | solution.py:23
  119.3 3.4 %collective-permute-start.23 = (f32[192,768]{1,0:T(8,128)S(1)}, f32[192,768]{1,0:T(8,128)S(1)}, u32[]{:S(2)}, u32[]{:S(2)}) collective-permute-start(f32[192,768]{1,0:T(8,128)S(1)} %get-tuple-element.201), channel_id=1, source_target_pairs={{0,24},{4,28},{8,16},{12,20},{16,8},{20,12},{24,0},{28,4},{1,25},{... | collective-permute-start | bytes 1769480 | tf_op jit(solution)/shard_map/cond/branch_1_fun/ppermute | solution.py:449
  124.1 11.3 %collective-permute-done.21 = f32[192,768]{1,0:T(8,128)S(1)} collective-permute-done((f32[192,768]{1,0:T(8,128)S(1)}, f32[192,768]{1,0:T(8,128)S(1)}, u32[]{:S(2)}, u32[]{:S(2)}) %collective-permute-start.21) | collective-permute-done | bytes 589856 | tf_op jit(solution)/shard_map/cond/branch_1_fun/ppermute | solution.py:449
  135.4 11.3 %collective-permute-done.22 = f32[192,768]{1,0:T(8,128)S(1)} collective-permute-done((f32[192,768]{1,0:T(8,128)S(1)}, f32[192,768]{1,0:T(8,128)S(1)}, u32[]{:S(2)}, u32[]{:S(2)}) %collective-permute-start.22) | collective-permute-done | bytes 589856 | tf_op jit(solution)/shard_map/cond/branch_1_fun/ppermute | solution.py:449
  147.7 28.0 %conditional.9 = (f32[192,768]{1,0:T(8,128)}, f32[192,768]{1,0:T(8,128)}, f32[192,768]{1,0:T(8,128)}, f32[192,768]{1,0:T(8,128)}, f32[2,12,256,256]{3,2,1,0:T(8,...) conditional(s32[]{:T(128)} %convert_element_type.65, () %tuple.86, (f32[192,768]{1,0:T(8,128)}, ...), branch_computations={%region_9.10_spmd, %region_10.11_spmd} | conditional | bytes 14549072 | solution.py:566
  153.2 8.5 %project_all.1 = (bf16[3,768,512]{2,1,0:T(8,128)(2,1)}, bf16[3,768,768]{2,1,0:T(8,128)(2,1)}) custom-call(f32[4,3,192,768]{3,2,1,0:T(8,128)} %get-tuple-element.208.weight_ref, f32[3,768]{1,0:T(4,128)S(1)} %get-tuple-element.209.bias, bf16[512,768]{1,0:T(8,128)(2,1)S(1)} %get-tuple-element.210.entry), custom_call_target="tpu_custom_call" | custom-call | tf_op jit(solution)/shard_map/cond/branch_1_fun/project_all/pallas_call | solution.py:55
  161.7 7.1 %all_probs.1 = f32[2,12,256,256]{3,2,1,0:T(8,128)} custom-call(bf16[3,768,512]{2,1,0:T(8,128)(2,1)} %get-tuple-element.491.proj_ref), custom_call_target="tpu_custom_call" | custom-call | tf_op jit(solution)/shard_map/cond/branch_1_fun/all_probs/pallas_call | solution.py:55
  168.7 7.0 %collective-permute-done.1 = f32[192,768]{1,0:T(8,128)} collective-permute-done((f32[192,768]{1,0:T(8,128)}, f32[192,768]{1,0:T(8,128)}, u32[]{:S(2)}, u32[]{:S(2)}) %collective-permute-start.1) | collective-permute-done | bytes 589856 | tf_op jit(solution)/shard_map/cond/branch_1_fun/ppermute | solution.py:449
  178.6 70.8 %conditional.10 = (f32[768,768]{1,0:T(8,128)}, f32[768,768]{1,0:T(8,128)}, f32[576,768]{1,0:T(8,128)}, f32[192,768]{1,0:T(8,128)}, f32[2,192]{1,0:T(2,128)}, /*i...) conditional(s32[]{:T(128)} %convert_element_type.65, () %tuple.88, ...), branch_computations={%region_12.13_spmd, %region_13.22_spmd} | conditional | flops 4658717 | bytes 59926464 | solution.py:566
  178.6 18.0 %conditional = (f32[512,768]{1,0:T(8,128)}, bf16[3,768,512]{2,1,0:T(8,128)(2,1)}, f32[384,768]{1,0:T(8,128)S(1)}, f32[384,768]{1,0:T(8,128)S(1)}, f32[768]{0:T(1...) conditional(s32[]{:T(128)} %convert_element_type.58, () %tuple.67, (bf16[2,256,768]{2,1,0:T(8,128)(2,1)}, ...), branch_computations={%region_14.14_spmd, %region_15.16_spmd} | conditional | flops 768 | bytes 6306128 | solution.py:566
  178.6 4.5 %middle_backward.2 = (f32[512,768]{1,0:T(8,128)}, bf16[512,768]{1,0:T(8,128)(2,1)S(1)}, bf16[768,512]{1,0:T(8,128)(2,1)S(1)}, f32[2,4,768]{2,1,0:T(4,128)S(1)}) custom-call(f32[512,768]{1,0:T(8,128)S(1)} %get-tuple-element.213.grad_ref, f32[512,768]{1,0:T(8,128)S(1)} %get-tuple-element.214.middle_ref, f32[512,768]{1,0:T(8,128)} %get-tuple-element.215.attention_ref, ...), custom_call_target="tpu_custom_call" | custom-call | tf_op jit(solution)/shard_map/cond/branch_1_fun/cond/branch_1_fun/middle_backward/pallas_call | solution.py:55
  183.1 10.7 %attention_backward.1.proj = bf16[3,768,512]{2,1,0:T(8,128)(2,1)} custom-call(f32[2,12,256,256]{3,2,1,0:T(8,128)} %get-tuple-element.220.probs_ref, bf16[3,768,512]{2,1,0:T(8,128)(2,1)} %get-tuple-element.221.proj_ref, bf16[768,512]{1,0:T(8,128)(2,1)S(1)} %get-tuple-element.222.grad_ref), custom_call_target="tpu_custom_call" | custom-call | tf_op jit(solution)/shard_map/cond/branch_1_fun/cond/branch_1_fun/attention_backward/pallas_call | solution.py:55
  205.6 7.1 %conditional.1 = (f32[2,2,768]{2,1,0:T(2,128)}, f32[2,256,768]{2,1,0:T(8,128)}, bf16[2,2,768]{2,1,0:T(2,128)(2,1)S(1)}) conditional(s32[]{:T(128)} %convert_element_type.58, () %tuple.66, (bf16[3,768,512]{2,1,0:T(8,128)(2,1)}, bf16[3,768,768]{2,1,0:T(8,128)(2,1)}, bf16[512,768]{1,0:T(8,128)(2,1)S(1)}, f32[512,768]{1,0:T(8,128)}, ...), branch_computations={%region_17.17_spmd, %region_18.18_spmd} | conditional | flops 3072 | bytes 1591330 | solution.py:566
  205.6 6.4 %entry_backward.1 = (f32[512,768]{1,0:T(8,128)}, f32[2,2,768]{2,1,0:T(2,128)}) custom-call(bf16[2304,512]{1,0:T(8,128)(2,1)} %bitcast.7.proj_ref, bf16[2304,768]{1,0:T(8,128)(2,1)} %bitcast.8.weight_ref, bf16[512,768]{1,0:T(8,128)(2,1)S(1)} %get-tuple-element.233.inputs_ref, f32[512,768]{1,0:T(8,128)} %get-tuple-element.234.middle_grad_ref, ...), custom_call_target="tpu_custom_call" | custom-call | tf_op jit(solution)/shard_map/cond/branch_1_fun/cond/branch_1_fun/entry_backward/pallas_call | solution.py:55
  213.4 3.4 %collective-permute-done.29.refs_2_ = f32[96,768]{1,0:T(8,128)} collective-permute-done((f32[96,768]{1,0:T(8,128)S(1)}, f32[96,768]{1,0:T(8,128)}, u32[]{:S(2)}, u32[]{:S(2)}) %collective-permute-start.29) | collective-permute-done | bytes 294944 | tf_op jit(solution)/shard_map/cond/branch_1_fun/ppermute | solution.py:449
  231.4 11.5 %conditional.2 = (f32[192,4608]{1,0:T(8,128)}, f32[768]{0:T(1024)}, f32[768]{0:T(1024)}, f32[768]{0:T(1024)}, f32[576]{0:T(1024)}, /*index=5*/f32[2,192]{1,0:T(2...) conditional(s32[]{:T(128)} %convert_element_type.58, () %tuple.65, (f32[16,7744]{1,0:T(8,128)S(1)}, ...), branch_computations={%region_19.19_spmd, %region_20.21_spmd} | conditional | flops 3585600 | bytes 9124712 | solution.py:566
  232.1 3.7 %modulator_backward.1 = (f32[192,4608]{1,0:T(8,128)}, f32[1,4608]{1,0:T(1,128)S(1)}) custom-call(f32[16,7744]{1,0:T(8,128)S(1)} %get-tuple-element.238.every_ref.context_ref, f32[16,7744]{1,0:T(8,128)S(1)} %get-tuple-element.238.every_ref.context_ref), custom_call_target="tpu_custom_call" | custom-call | tf_op jit(solution)/shard_map/cond/branch_1_fun/cond/branch_1_fun/modulator_backward/pallas_call | solution.py:55
  237.0 4.8 %whole.2 = (f32[768,768]{1,0:T(8,128)}, f32[768,768]{1,0:T(8,128)}) custom-call(s32[3]{0:T(128)S(1)} %get-tuple-element.243.place, f32[768,768]{1,0:T(8,128)} %get-tuple-element.244.mine, f32[768,768]{1,0:T(8,128)} %get-tuple-element.245.other), custom_call_target="tpu_custom_call" | custom-call | tf_op jit(solution)/shard_map/cond/branch_1_fun/cond/branch_1_fun/whole/pallas_call | solution.py:55
  (225 shorter events, 85.3 us)
Async XLA Ops:
  8.0 139.7 %all-gather.2.cloned.1.call-start = ((), (), s32[]{:S(2)}) async-start(), calls=%async_computation.1 | async-start | bytes 7299072 | tf_op jit(solution)/shard_map/all_gather | solution.py:531
  13.3 10.3 %collective-permute-start.5 = (f32[2,4608]{1,0:T(2,128)S(1)}, f32[2,4608]{1,0:T(2,128)S(1)}, u32[]{:S(2)}, u32[]{:S(2)}) collective-permute-start(f32[2,4608]{1,0:T(2,128)S(1)} %fusion.15.part0), channel_id=1, source_target_pairs={{0,3},{1,2},{2,1},{3,0},{4,7},{5,6},{6,5},{7,4},{8,11},{9,10},{10,... | collective-permute-start | bytes 110600 | tf_op jit(solution)/shard_map/cond/branch_1_fun/ppermute | solution.py:449
  19.1 18.6 %collective-permute-start.10 = (f32[24,768]{1,0:T(8,128)S(1)}, f32[24,768]{1,0:T(8,128)S(1)}, u32[]{:S(2)}, u32[]{:S(2)}) collective-permute-start(f32[24,768]{1,0:T(8,128)S(1)} %dynamic-slice_convert_fusion.refs_0_), channel_id=1, source_target_pairs={{0,1},{1,0},{2,3},{3,2},{4,5},{5,4},{6,7},{7,6},{8,9},{9,8},{10,11... | collective-permute-start | bytes 221192 | tf_op jit(solution)/shard_map/cond/branch_1_fun/ppermute | solution.py:449
  19.2 19.2 %collective-permute-start.11 = (f32[24,768]{1,0:T(8,128)S(1)}, f32[24,768]{1,0:T(8,128)S(1)}, u32[]{:S(2)}, u32[]{:S(2)}) collective-permute-start(f32[24,768]{1,0:T(8,128)S(1)} %dynamic-slice_convert_fusion.refs_0_), channel_id=1, source_target_pairs={{0,2},{1,3},{2,0},{3,1},{4,6},{5,7},{6,4},{7,5},{8,10},{9,11},{10,... | collective-permute-start | bytes 221192 | tf_op jit(solution)/shard_map/cond/branch_1_fun/ppermute | solution.py:449
  19.8 19.2 %collective-permute-start.12 = (f32[24,768]{1,0:T(8,128)S(1)}, f32[24,768]{1,0:T(8,128)S(1)}, u32[]{:S(2)}, u32[]{:S(2)}) collective-permute-start(f32[24,768]{1,0:T(8,128)S(1)} %dynamic-slice_convert_fusion.refs_0_), channel_id=1, source_target_pairs={{0,3},{1,2},{2,1},{3,0},{4,7},{5,6},{6,5},{7,4},{8,11},{9,10},{10,... | collective-permute-start | bytes 221192 | tf_op jit(solution)/shard_map/cond/branch_1_fun/ppermute | solution.py:449
  23.6 9.6 %collective-permute-start.4 = (f32[2,4608]{1,0:T(2,128)S(1)}, f32[2,4608]{1,0:T(2,128)S(1)}, u32[]{:S(2)}, u32[]{:S(2)}) collective-permute-start(f32[2,4608]{1,0:T(2,128)S(1)} %fusion.15.part0), channel_id=1, source_target_pairs={{0,2},{1,3},{2,0},{3,1},{4,6},{5,7},{6,4},{7,5},{8,10},{9,11},{10,... | collective-permute-start | bytes 110600 | tf_op jit(solution)/shard_map/cond/branch_1_fun/ppermute | solution.py:449
  37.6 26.1 %collective-permute-start.7 = (f32[192,512]{1,0:T(8,128)S(1)}, f32[192,512]{1,0:T(8,128)S(1)}, u32[]{:S(2)}, u32[]{:S(2)}) collective-permute-start(f32[192,512]{1,0:T(8,128)S(1)} %get-tuple-element.457.mixed0), channel_id=1, source_target_pairs={{0,2},{1,3},{2,0},{3,1},{4,6},{5,7},{6,4},{7,5},{8,10},{9,11},{10,... | collective-permute-start | bytes 1179656 | tf_op jit(solution)/shard_map/cond/branch_1_fun/ppermute | solution.py:449
  40.8 15.2 %collective-permute-start.13 = (f32[4,24,768]{2,1,0:T(8,128)S(1)}, f32[4,24,768]{2,1,0:T(8,128)S(1)}, u32[]{:S(2)}, u32[]{:S(2)}) collective-permute-start(f32[4,24,768]{2,1,0:T(8,128)S(1)} %pad_maximum_fusion.refs_0_), channel_id=1, source_target_pairs={{0,8},{4,12},{8,0},{12,4},{16,24},{20,28},{24,16},{28,20},{1,9},{5... | collective-permute-start | bytes 884744 | tf_op jit(solution)/shard_map/cond/branch_1_fun/ppermute | solution.py:449
  42.2 13.8 %collective-permute-start.14 = (f32[4,24,768]{2,1,0:T(8,128)S(1)}, f32[4,24,768]{2,1,0:T(8,128)S(1)}, u32[]{:S(2)}, u32[]{:S(2)}) collective-permute-start(f32[4,24,768]{2,1,0:T(8,128)S(1)} %pad_maximum_fusion.refs_0_), channel_id=1, source_target_pairs={{0,16},{4,20},{8,24},{12,28},{16,0},{20,4},{24,8},{28,12},{1,17},{... | collective-permute-start | bytes 884744 | tf_op jit(solution)/shard_map/cond/branch_1_fun/ppermute | solution.py:449
  43.9 27.8 %collective-permute-start.6 = (f32[192,512]{1,0:T(8,128)S(1)}, f32[192,512]{1,0:T(8,128)S(1)}, u32[]{:S(2)}, u32[]{:S(2)}) collective-permute-start(f32[192,512]{1,0:T(8,128)S(1)} %get-tuple-element.457.mixed0), channel_id=1, source_target_pairs={{0,1},{1,0},{2,3},{3,2},{4,5},{5,4},{6,7},{7,6},{8,9},{9,8},{10,11... | collective-permute-start | bytes 1179656 | tf_op jit(solution)/shard_map/cond/branch_1_fun/ppermute | solution.py:449
  46.3 19.8 %collective-permute-start.15 = (f32[4,24,768]{2,1,0:T(8,128)S(1)}, f32[4,24,768]{2,1,0:T(8,128)S(1)}, u32[]{:S(2)}, u32[]{:S(2)}) collective-permute-start(f32[4,24,768]{2,1,0:T(8,128)S(1)} %pad_maximum_fusion.refs_0_), channel_id=1, source_target_pairs={{0,24},{4,28},{8,16},{12,20},{16,8},{20,12},{24,0},{28,4},{1,25},{... | collective-permute-start | bytes 884744 | tf_op jit(solution)/shard_map/cond/branch_1_fun/ppermute | solution.py:449
  55.9 10.1 %collective-permute-start.16 = (f32[4,24,768]{2,1,0:T(8,128)S(1)}, f32[4,24,768]{2,1,0:T(8,128)S(1)}, u32[]{:S(2)}, u32[]{:S(2)}) collective-permute-start(f32[4,24,768]{2,1,0:T(8,128)S(1)} %pad_maximum_fusion.refs_0_), channel_id=1, source_target_pairs={{0,4},{4,0},{8,12},{12,8},{16,20},{20,16},{24,28},{28,24},{1,5},{5... | collective-permute-start | bytes 884744 | tf_op jit(solution)/shard_map/cond/branch_1_fun/ppermute | solution.py:449
  56.0 17.9 %collective-permute-start.8 = (f32[192,512]{1,0:T(8,128)S(1)}, f32[192,512]{1,0:T(8,128)S(1)}, u32[]{:S(2)}, u32[]{:S(2)}) collective-permute-start(f32[192,512]{1,0:T(8,128)S(1)} %get-tuple-element.457.mixed0), channel_id=1, source_target_pairs={{1,2},{2,1},{5,6},{6,5},{9,10},{10,9},{13,14},{14,13},{17,18},{18,... | collective-permute-start | bytes 1179656 | tf_op jit(solution)/shard_map/cond/branch_1_fun/ppermute | solution.py:625
  63.7 28.3 %collective-permute-start.9 = (f32[192,512]{1,0:T(8,128)S(1)}, f32[192,512]{1,0:T(8,128)S(1)}, u32[]{:S(2)}, u32[]{:S(2)}) collective-permute-start(f32[192,512]{1,0:T(8,128)S(1)} %collective-permute-done.7.mixed2), channel_id=1, source_target_pairs={{1,0},{2,3},{5,4},{6,7},{9,8},{10,11},{13,12},{14,15},{17,16},{18,... | collective-permute-start | bytes 1179656 | tf_op jit(solution)/shard_map/cond/branch_1_fun/ppermute | solution.py:626
  102.7 73.0 %all-reduce.5.cloned.1.call-start = ((), (), s32[]{:S(2)}) async-start(), calls=%async_computation | async-start | bytes 3145728 | tf_op jit(solution)/shard_map/psum | solution.py:644
  108.6 8.5 %collective-permute-start.20 = (f32[768,768]{1,0:T(8,128)}, f32[768,768]{1,0:T(8,128)}, u32[]{:S(2)}, u32[]{:S(2)}) collective-permute-start(f32[768,768]{1,0:T(8,128)} %get-tuple-element.197), channel_id=1, source_target_pairs={{0,4},{4,0},{8,12},{12,8},{16,20},{20,16},{24,28},{28,24},{1,5},{5... | collective-permute-start | bytes 7077896 | tf_op jit(solution)/shard_map/cond/branch_1_fun/ppermute | solution.py:449
  112.7 11.3 %collective-permute-start.25 = (f32[5,768]{1,0:T(8,128)S(1)}, f32[5,768]{1,0:T(8,128)S(1)}, u32[]{:S(2)}, u32[]{:S(2)}) collective-permute-start(f32[5,768]{1,0:T(8,128)S(1)} %pad_maximum_fusion.1), channel_id=1, source_target_pairs={{0,2},{1,3},{2,0},{3,1},{4,6},{5,7},{6,4},{7,5},{8,10},{9,11},{10,... | collective-permute-start | bytes 46088 | tf_op jit(solution)/shard_map/cond/branch_1_fun/ppermute | solution.py:449
  114.7 9.4 %collective-permute-start.26 = (f32[5,768]{1,0:T(8,128)S(1)}, f32[5,768]{1,0:T(8,128)S(1)}, u32[]{:S(2)}, u32[]{:S(2)}) collective-permute-start(f32[5,768]{1,0:T(8,128)S(1)} %pad_maximum_fusion.1), channel_id=1, source_target_pairs={{0,3},{1,2},{2,1},{3,0},{4,7},{5,6},{6,5},{7,4},{8,11},{9,10},{10,... | collective-permute-start | bytes 46088 | tf_op jit(solution)/shard_map/cond/branch_1_fun/ppermute | solution.py:449
  119.1 16.3 %collective-permute-start.21 = (f32[192,768]{1,0:T(8,128)S(1)}, f32[192,768]{1,0:T(8,128)S(1)}, u32[]{:S(2)}, u32[]{:S(2)}) collective-permute-start(f32[192,768]{1,0:T(8,128)S(1)} %get-tuple-element.199), channel_id=1, source_target_pairs={{0,8},{4,12},{8,0},{12,4},{16,24},{20,28},{24,16},{28,20},{1,9},{5... | collective-permute-start | bytes 1769480 | tf_op jit(solution)/shard_map/cond/branch_1_fun/ppermute | solution.py:449
  119.2 27.6 %collective-permute-start.22 = (f32[192,768]{1,0:T(8,128)S(1)}, f32[192,768]{1,0:T(8,128)S(1)}, u32[]{:S(2)}, u32[]{:S(2)}) collective-permute-start(f32[192,768]{1,0:T(8,128)S(1)} %get-tuple-element.200), channel_id=1, source_target_pairs={{0,16},{4,20},{8,24},{12,28},{16,0},{20,4},{24,8},{28,12},{1,17},{... | collective-permute-start | bytes 1769480 | tf_op jit(solution)/shard_map/cond/branch_1_fun/ppermute | solution.py:449
  119.3 27.5 %collective-permute-start.23 = (f32[192,768]{1,0:T(8,128)S(1)}, f32[192,768]{1,0:T(8,128)S(1)}, u32[]{:S(2)}, u32[]{:S(2)}) collective-permute-start(f32[192,768]{1,0:T(8,128)S(1)} %get-tuple-element.201), channel_id=1, source_target_pairs={{0,24},{4,28},{8,16},{12,20},{16,8},{20,12},{24,0},{28,4},{1,25},{... | collective-permute-start | bytes 1769480 | tf_op jit(solution)/shard_map/cond/branch_1_fun/ppermute | solution.py:449
  147.7 21.0 %collective-permute-start = (f32[192,768]{1,0:T(8,128)}, f32[192,768]{1,0:T(8,128)}, u32[]{:S(2)}, u32[]{:S(2)}) collective-permute-start(f32[192,768]{1,0:T(8,128)} %get-tuple-element.486), channel_id=1, source_target_pairs={{0,8},{4,12},{8,0},{12,4},{16,24},{20,28},{24,16},{28,20},{1,9},{5... | collective-permute-start | bytes 1769480 | tf_op jit(solution)/shard_map/cond/branch_1_fun/ppermute | solution.py:449
  149.4 26.3 %collective-permute-start.1 = (f32[192,768]{1,0:T(8,128)}, f32[192,768]{1,0:T(8,128)}, u32[]{:S(2)}, u32[]{:S(2)}) collective-permute-start(f32[192,768]{1,0:T(8,128)} %get-tuple-element.486), channel_id=1, source_target_pairs={{0,16},{4,20},{8,24},{12,28},{16,0},{20,4},{24,8},{28,12},{1,17},{... | collective-permute-start | bytes 1769480 | tf_op jit(solution)/shard_map/cond/branch_1_fun/ppermute | solution.py:449
  149.7 26.1 %collective-permute-start.2 = (f32[192,768]{1,0:T(8,128)}, f32[192,768]{1,0:T(8,128)}, u32[]{:S(2)}, u32[]{:S(2)}) collective-permute-start(f32[192,768]{1,0:T(8,128)} %get-tuple-element.486), channel_id=1, source_target_pairs={{0,24},{4,28},{8,16},{12,20},{16,8},{20,12},{24,0},{28,4},{1,25},{... | collective-permute-start | bytes 1769480 | tf_op jit(solution)/shard_map/cond/branch_1_fun/ppermute | solution.py:449
  177.2 73.6 %all-reduce.7.cloned.1.call-start = ((), (), s32[]{:S(2)}) async-start(), calls=%async_computation.2 | async-start | bytes 3145728 | tf_op jit(solution)/shard_map/psum | solution.py:678
  200.9 12.4 %collective-permute-start.28 = (f32[96,768]{1,0:T(8,128)S(1)}, f32[96,768]{1,0:T(8,128)}, u32[]{:S(2)}, u32[]{:S(2)}) collective-permute-start(f32[96,768]{1,0:T(8,128)S(1)} %get-tuple-element.275), channel_id=1, source_target_pairs={{0,8},{4,12},{8,0},{12,4},{16,24},{20,28},{24,16},{28,20},{1,9},{5... | collective-permute-start | bytes 884744 | tf_op jit(solution)/shard_map/cond/branch_1_fun/ppermute | solution.py:449
  201.6 15.2 %collective-permute-start.29 = (f32[96,768]{1,0:T(8,128)S(1)}, f32[96,768]{1,0:T(8,128)}, u32[]{:S(2)}, u32[]{:S(2)}) collective-permute-start(f32[96,768]{1,0:T(8,128)S(1)} %get-tuple-element.276), channel_id=1, source_target_pairs={{0,16},{4,20},{8,24},{12,28},{16,0},{20,4},{24,8},{28,12},{1,17},{... | collective-permute-start | bytes 884744 | tf_op jit(solution)/shard_map/cond/branch_1_fun/ppermute | solution.py:449
  203.0 13.8 %collective-permute-start.30 = (f32[96,768]{1,0:T(8,128)S(1)}, f32[96,768]{1,0:T(8,128)}, u32[]{:S(2)}, u32[]{:S(2)}) collective-permute-start(f32[96,768]{1,0:T(8,128)S(1)} %get-tuple-element.277), channel_id=1, source_target_pairs={{0,24},{4,28},{8,16},{12,20},{16,8},{20,12},{24,0},{28,4},{1,25},{... | collective-permute-start | bytes 884744 | tf_op jit(solution)/shard_map/cond/branch_1_fun/ppermute | solution.py:449
  220.1 11.3 %collective-permute-start.35 = (f32[768,768]{1,0:T(8,128)}, f32[768,768]{1,0:T(8,128)}, u32[]{:S(2)}, u32[]{:S(2)}) collective-permute-start(f32[768,768]{1,0:T(8,128)} %place.2), channel_id=1, source_target_pairs={{0,4},{4,0},{8,12},{12,8},{16,20},{20,16},{24,28},{28,24},{1,5},{5... | collective-permute-start | bytes 7077896 | tf_op jit(solution)/shard_map/cond/branch_1_fun/ppermute | solution.py:449
  226.3 16.7 %collective-permute-start.36 = (f32[96,768]{1,0:T(8,128)}, f32[96,768]{1,0:T(8,128)S(1)}, u32[]{:S(2)}, u32[]{:S(2)}) collective-permute-start(f32[96,768]{1,0:T(8,128)} %tie.25.refs_0_), channel_id=1, source_target_pairs={{0,8},{4,12},{8,0},{12,4},{16,24},{20,28},{24,16},{28,20},{1,9},{5... | collective-permute-start | bytes 884744 | tf_op jit(solution)/shard_map/cond/branch_1_fun/ppermute | solution.py:449
  227.9 15.0 %collective-permute-start.37 = (f32[96,768]{1,0:T(8,128)}, f32[96,768]{1,0:T(8,128)S(1)}, u32[]{:S(2)}, u32[]{:S(2)}) collective-permute-start(f32[96,768]{1,0:T(8,128)} %tie.25.refs_0_), channel_id=1, source_target_pairs={{0,16},{4,20},{8,24},{12,28},{16,0},{20,4},{24,8},{28,12},{1,17},{... | collective-permute-start | bytes 884744 | tf_op jit(solution)/shard_map/cond/branch_1_fun/ppermute | solution.py:449
  229.7 13.2 %collective-permute-start.38 = (f32[96,768]{1,0:T(8,128)}, f32[96,768]{1,0:T(8,128)S(1)}, u32[]{:S(2)}, u32[]{:S(2)}) collective-permute-start(f32[96,768]{1,0:T(8,128)} %tie.25.refs_0_), channel_id=1, source_target_pairs={{0,24},{4,28},{8,16},{12,20},{16,8},{20,12},{24,0},{28,4},{1,25},{... | collective-permute-start | bytes 884744 | tf_op jit(solution)/shard_map/cond/branch_1_fun/ppermute | solution.py:449
  (46 other events, 470.3 us)
Sparse Core Ops, SparseCore 0:
  11.7 87.9 all-gather.1
Sparse Core Ops, SparseCore 1:
  106.1 67.9 all-reduce.4
  180.0 66.9 all-reduce.6
